TPU v7x, 32 devices: a whole 2x2x4 slice. The times are simulated.
32 devices in a mesh: silo: 8 (over y, x, core), fsdp: 4 (over z).
Axes of the slice: x: 2, y: 2, z: 4, core: 2. Of those that a mesh axis runs over, the one named last changes fastest.
Arguments:
- activations: bfloat16 [8, 1024, 2304], P('silo', 'fsdp'), may hold values from -6 to 6
- key_cot: bfloat16 [8, 1024, 512], P('silo', 'fsdp'), may hold values from -0.29882812 to 0.29882812
- key_weight: bfloat16 [8, 2304, 512], P('silo', 'fsdp'), may hold values from -0.125 to 0.125
- weight_first: float32 [8, 2304, 512], P('silo', 'fsdp'), may hold values from -2 to 2
- weight_second: float32 [8, 2304, 512], P('silo', 'fsdp'), may hold values from 1 to 16
- norm_gain: float32 [8, 2304], P('silo', 'fsdp'), may hold values from 0.5 to 1.5
- gain_first: float32 [8, 2304], P('silo', 'fsdp'), may hold values from -2 to 2
- gain_second: float32 [8, 2304], P('silo', 'fsdp'), may hold values from 0.5 to 4
- pseudo_grad: bfloat16 [8, 1572864], P('silo', 'fsdp'), may hold values from -6 to 6
- outer_params: float32 [1572864], P('fsdp'), may hold values from -6 to 6
- outer_mom: float32 [1572864], P('fsdp'), may hold values from -3 to 3
Outputs:
- keys: bfloat16 [8, 1024, 512], P('silo', 'fsdp')
- new_weight: bfloat16 [8, 2304, 512], P('silo', 'fsdp')
- new_weight_first: float32 [8, 2304, 512], P('silo', 'fsdp')
- new_weight_second: float32 [8, 2304, 512], P('silo', 'fsdp')
- new_gain: float32 [8, 2304], P('silo', 'fsdp')
- new_gain_first: float32 [8, 2304], P('silo', 'fsdp')
- new_gain_second: float32 [8, 2304], P('silo', 'fsdp')
- new_outer_params: float32 [1572864], P('fsdp')
- new_outer_mom: float32 [1572864], P('fsdp')
All inputs are finite; a program needn't handle non-finite values.
Results may differ from a plain program's by a relative error of at most 0.0095.
Values may be sent and summed in bfloat16 or wider, within the bound.
No kernel may reach another device: no remote copies, remote signals or barrier semaphores. Data moves between devices by JAX's collectives and lax.ppermute only.
A program may use at most 64 MiB of HBM per device.

v0:
```python
import math

import jax
import jax.numpy as jnp
from jax import lax
from jax.sharding import PartitionSpec as P

norm_eps = 1e-05
beta_one = 0.9
beta_two = 0.95
corr_one = 1.0 - math.exp(200.0 * math.log(0.9))
corr_two = 1.0 - math.exp(200.0 * math.log(0.95))
learn_rate = 0.001
adam_eps = 1e-08
weight_decay = 0.1
outer_beta = 0.9
outer_rate = 0.7


def adam_step(params, gradient, first_moment, second_moment):
    first_new = beta_one * first_moment + (1.0 - beta_one) * gradient
    second_new = beta_two * second_moment + (1.0 - beta_two) * gradient * gradient
    update = (
        first_new / corr_one / (jnp.sqrt(second_new / corr_two) + adam_eps) + weight_decay * params
    )
    return (params - learn_rate * update, first_new, second_new)


def nesterov(delta_part, params_part, mom_part):
    new_mom = outer_beta * mom_part + delta_part
    new_params = params_part - outer_rate * (delta_part + outer_beta * new_mom)
    return (new_params, new_mom)


def outer_update(pseudo_grad, outer_params, outer_mom):
    grad_wide = pseudo_grad[0].astype(jnp.float32)
    silo_count = lax.axis_size("silo")
    silo_total = lax.psum(grad_wide, "silo")
    return nesterov(silo_total / silo_count, outer_params, outer_mom)


def per_device(
    activations,
    key_cot,
    key_weight,
    weight_first,
    weight_second,
    norm_gain,
    gain_first,
    gain_second,
    pseudo_grad,
    outer_params,
    outer_mom,
):
    wide_inputs = activations[0].astype(jnp.float32)
    cotangent = key_cot[0]
    inv_rms = lax.rsqrt(jnp.mean(wide_inputs * wide_inputs, axis=1, keepdims=True) + norm_eps)
    gain_wire = norm_gain.astype(jnp.bfloat16)
    weight_piece = lax.all_gather(key_weight, "fsdp", axis=1, tiled=True)[0]
    gain_piece = lax.all_gather(gain_wire, "fsdp", axis=1, tiled=True)[0].astype(jnp.float32)
    normed_piece = (wide_inputs * inv_rms * gain_piece[None, :]).astype(jnp.bfloat16)
    key_sum = jnp.dot(normed_piece, weight_piece, preferred_element_type=jnp.float32)
    back_grad = lax.dot_general(
        cotangent, weight_piece, (((1,), (1,)), ((), ())), preferred_element_type=jnp.float32
    )
    gain_piece_grad = jnp.sum(back_grad * wide_inputs * inv_rms, axis=0)
    gain_grad = gain_piece_grad
    key_sum, normed, gain_grad = (key_sum, normed_piece, gain_grad)
    weight_grad = lax.psum_scatter(
        lax.dot_general(
            normed, cotangent, (((0,), (0,)), ((), ())), preferred_element_type=jnp.float32
        ).astype(jnp.bfloat16),
        "fsdp",
        scatter_dimension=0,
        tiled=True,
    ).astype(jnp.float32)
    gain_share = lax.psum_scatter(gain_grad, "fsdp", scatter_dimension=0, tiled=True)
    new_weight, new_first, new_second = adam_step(
        key_weight[0].astype(jnp.float32), weight_grad, weight_first[0], weight_second[0]
    )
    new_gain, new_gain_first, new_gain_second = adam_step(
        norm_gain[0], gain_share, gain_first[0], gain_second[0]
    )
    new_params, new_mom = outer_update(pseudo_grad, outer_params, outer_mom)
    return (
        key_sum.astype(jnp.bfloat16)[None],
        new_weight.astype(jnp.bfloat16)[None],
        new_first[None],
        new_second[None],
        new_gain[None],
        new_gain_first[None],
        new_gain_second[None],
        new_params,
        new_mom,
    )


def solution(mesh):
    return jax.shard_map(
        per_device,
        mesh=mesh,
        in_specs=(
            P("silo", "fsdp", None),
            P("silo", "fsdp", None),
            P("silo", "fsdp", None),
            P("silo", "fsdp", None),
            P("silo", "fsdp", None),
            P("silo", "fsdp"),
            P("silo", "fsdp"),
            P("silo", "fsdp"),
            P("silo", "fsdp"),
            P("fsdp"),
            P("fsdp"),
        ),
        out_specs=(
            P("silo", "fsdp", None),
            P("silo", "fsdp", None),
            P("silo", "fsdp", None),
            P("silo", "fsdp", None),
            P("silo", "fsdp"),
            P("silo", "fsdp"),
            P("silo", "fsdp"),
            P("fsdp"),
            P("fsdp"),
        ),
        check_vma=False,
    )
```

profile of v0, /device:TPU:0, one launch (start us, length us, event | category | flops | bytes accessed | tf_op | source)
XLA Modules:
  0.0 127.2 jit_solution(2205501710150560514)
XLA Ops:
  8.0 0.0 copy-start
  8.0 0.0 all-reduce.4.cloned.1.call-start
  8.1 4.2 %convert_element_type.62 = f32[1,393216]{1,0:T(1,128)} convert(bf16[1,393216]{1,0:T(2,128)(2,1)} %param.19) | non-fusion elementwise | flops 393216 | bytes 2359296 | tf_op jit(solution)/shard_map/convert_element_type | solution.py:36
  12.3 0.0 copy-start.10
  12.3 0.0 copy-start.7
  12.3 0.0 copy-start.6
  12.3 0.0 all-reduce.4.cloned.1.call-update
  12.3 0.0 all-gather.2.cloned.1.call-start
  12.3 0.5 all-gather.2.cloned.1.call-update
  12.9 0.0 reduce-scatter.2.cloned.1.call-start
  12.9 0.0 copy-done.10
  12.9 0.6 fusion.32
  14.2 0.0 copy-done.7
  14.2 0.2 dynamic-update-slice
  14.5 13.8 %all-reduce = bf16[2304]{0:T(1024)(128)(2,1)S(1)} all-reduce(bf16[2304]{0:T(1024)(128)(2,1)S(1)} %dynamic-update-slice), channel_id=1, replica_groups=mesh['silo'=8,'fsdp'=4] {'fsdp'}, use_global_device_ids=true, to_apply=%add | all-reduce | flops 2304 | bytes 9216
  28.3 0.0 copy-done.6
  28.3 0.3 fusion.2
  28.6 0.0 copy-done
  28.6 0.0 copy-start.3
  28.6 2.3 %convolution_convert_fusion = bf16[2304,512]{1,0:T(8,128)(2,1)} fusion(bf16[1,256,2304]{2,1,0:T(8,128)(2,1)S(1)} %copy-done.6, f32[2304]{0:T(1024)S(1)} %mul.169, f32[256]{0:T(256)S(1)} %add_rsqrt_fusion, bf16[1,256,512]{2,1,0:T(8,128)(2,1)S(1)} %copy-done), kind=kOutput, calls=%fused_computation | convolution fusion | flops 607518720 | bytes 3811328 | tf_op jit(solution)/shard_map/dot_general | solution.py:70
  30.9 0.0 copy-start.8
  30.9 0.0 copy-start.9
  30.9 0.0 copy-start.2
  30.9 0.0 reduce-scatter.2.cloned.1.call-update
  31.7 0.0 copy-done.8
  31.8 0.0 copy-done.9
  31.8 42.6 %all-reduce.4.cloned.1.call-done = f32[393216]{0:T(1024)} async-done(((f32[393216]{0:T(1024)}), f32[393216]{0:T(1024)}) %all-reduce.4.cloned.1.call-update) | async-done | bytes 1572880 | tf_op jit(solution)/shard_map/psum | solution.py:38
  74.4 0.0 copy-done.3
  74.4 0.0 copy-done.2
  74.4 3.5 %multiply_subtract_fusion = (f32[393216]{0:T(1024)}, f32[393216]{0:T(1024)}) fusion(f32[393216]{0:T(1024)S(1)} %copy-done.2, f32[393216]{0:T(1024)} %all-reduce.4.cloned.1.call-done, f32[393216]{0:T(1024)S(1)} %copy-done.3), kind=kLoop, calls=%fused_computation.13 | loop fusion | flops 2752512 | bytes 7864320 | tf_op jit(solution)/shard_map/sub | solution.py:31
  77.9 0.0 all-gather.2.cloned.1.call-done
  77.9 2.8 %fusion.8 = f32[2304]{0:T(1024)S(1)} fusion(bf16[1,256,2304]{2,1,0:T(8,128)(2,1)} %param.11, bf16[1,2304,512]{2,1,0:T(8,128)(2,1)} %all-gather.2.cloned.1.call-done, f32[256]{0:T(256)S(1)} %add_rsqrt_fusion, bf16[1,256,512]{2,1,0:T(8,128)(2,1)S(1)} %copy-done), kind=kOutput, calls=%fused_computation.18 | convolution fusion | flops 606336768 | bytes 3811328 | tf_op jit(solution)/shard_map/dot_general | solution.py:63
  80.7 20.0 %all-reduce.1 = f32[2304]{0:T(1024)S(1)} all-reduce(f32[2304]{0:T(1024)S(1)} %fusion.8), channel_id=3, replica_groups=mesh['silo'=8,'fsdp'=4] {'fsdp'}, use_global_device_ids=true, to_apply=%region_3.0.clone | all-reduce | flops 2304 | bytes 18432
  100.7 0.1 multiply_subtract_fusion.1
  100.8 0.6 broadcast_in_dim.27
  101.4 0.6 broadcast_in_dim.29
  102.0 0.6 broadcast_in_dim.28
  102.5 0.0 copy-start.1
  102.5 0.0 copy-start.4
  102.5 0.0 copy-start.5
  102.5 3.7 %fusion.20 = bf16[1,256,512]{2,1,0:T(8,128)(2,1)} fusion(bf16[1,2304,512]{2,1,0:T(8,128)(2,1)} %all-gather.2.cloned.1.call-done, bf16[1,256,2304]{2,1,0:T(8,128)(2,1)} %param.11, f32[2304]{0:T(1024)S(1)} %mul.169, f32[256]{0:T(256)S(1)} %add_rsqrt_fusion), kind=kOutput, calls=%fused_computation.26 | convolution fusion | flops 606470144 | bytes 3811328 | tf_op jit(solution)/shard_map/dot_general | solution.py:62
  106.3 9.8 %reduce-scatter.2.cloned.1.call-done = bf16[576,512]{1,0:T(8,128)(2,1)} async-done(((bf16[2304,512]{1,0:T(8,128)(2,1)}), bf16[576,512]{1,0:T(8,128)(2,1)}) %reduce-scatter.2.cloned.1.call-update) | async-done | bytes 589840 | tf_op jit(solution)/shard_map/reduce_scatter | solution.py:69
  116.1 0.0 copy-done.1
  116.1 0.0 copy-done.4
  116.1 0.0 copy-done.5
  116.1 3.7 %fusion.24 = (f32[1,576,512]{2,1,0:T(8,128)}, bf16[1,576,512]{2,1,0:T(8,128)(2,1)}, f32[1,576,512]{2,1,0:T(8,128)}) fusion(bf16[576,512]{1,0:T(8,128)(2,1)} %reduce-scatter.2.cloned.1.call-done, f32[1,576,512]{2,1,0:T(8,128)S(1)} %copy-done.4, f32[1,576,512]{2,1,0:T(8,128)S(1)} %copy-done.5, bf16[1,576,512]{2,1,0:T(8,128)(2,1)S(1)} %copy-done.1), kind=kLoop, calls=%fused_computation.28 | loop fusion | flops 5013504 | bytes 6488064 | tf_op jit(solution)/shard_map/broadcast_in_dim | solution.py:89
  (6 shorter events, 0.1 us)
Async XLA Ops:
  8.0 20.6 %copy-start = (bf16[1,256,512]{2,1,0:T(8,128)(2,1)S(1)}, bf16[1,256,512]{2,1,0:T(8,128)(2,1)}, u32[]{:S(2)}) copy-start(bf16[1,256,512]{2,1,0:T(8,128)(2,1)} %param.12) | copy-start | bytes 786436
  8.0 66.3 %all-reduce.4.cloned.1.call-start = ((), (), s32[]{:S(2)}) async-start(), calls=%async_computation.3 | async-start | bytes 3145728 | tf_op jit(solution)/shard_map/psum | solution.py:38
  12.3 0.7 copy-start.10
  12.3 1.9 %copy-start.7 = (f32[1,576]{1,0:T(1,128)S(1)}, f32[1,576]{1,0:T(1,128)}, u32[]{:S(2)}) copy-start(f32[1,576]{1,0:T(1,128)} %param.16) | copy-start | bytes 6916
  12.3 16.0 %copy-start.6 = (bf16[1,256,2304]{2,1,0:T(8,128)(2,1)S(1)}, bf16[1,256,2304]{2,1,0:T(8,128)(2,1)}, u32[]{:S(2)}) copy-start(bf16[1,256,2304]{2,1,0:T(8,128)(2,1)} %param.11) | copy-start | bytes 3538948
  12.3 65.6 %all-gather.2.cloned.1.call-start = ((), (), s32[]{:S(2)}) async-start(), calls=%async_computation.1 | async-start | bytes 2949120 | tf_op jit(solution)/shard_map/all_gather | solution.py:59
  12.9 103.2 %reduce-scatter.2.cloned.1.call-start = ((), (), s32[]{:S(2)}) async-start(), calls=%async_computation.2 | async-start | bytes 2949120 | tf_op jit(solution)/shard_map/reduce_scatter | solution.py:69
  28.6 45.8 %copy-start.3 = (f32[393216]{0:T(1024)S(1)}, f32[393216]{0:T(1024)}, u32[]{:S(2)}) copy-start(f32[393216]{0:T(1024)} %param.21) | copy-start | bytes 4718596
  30.9 0.8 copy-start.8
  30.9 0.8 copy-start.9
  30.9 43.4 %copy-start.2 = (f32[393216]{0:T(1024)S(1)}, f32[393216]{0:T(1024)}, u32[]{:S(2)}) copy-start(f32[393216]{0:T(1024)} %param.20) | copy-start | bytes 4718596
  102.5 13.6 %copy-start.1 = (bf16[1,576,512]{2,1,0:T(8,128)(2,1)S(1)}, bf16[1,576,512]{2,1,0:T(8,128)(2,1)}, u32[]{:S(2)}) copy-start(bf16[1,576,512]{2,1,0:T(8,128)(2,1)} %param.13) | copy-start | bytes 1769476
  102.5 13.6 %copy-start.4 = (f32[1,576,512]{2,1,0:T(8,128)S(1)}, f32[1,576,512]{2,1,0:T(8,128)}, u32[]{:S(2)}) copy-start(f32[1,576,512]{2,1,0:T(8,128)} %param.15) | copy-start | bytes 3538948
  102.5 13.6 %copy-start.5 = (f32[1,576,512]{2,1,0:T(8,128)S(1)}, f32[1,576,512]{2,1,0:T(8,128)}, u32[]{:S(2)}) copy-start(f32[1,576,512]{2,1,0:T(8,128)} %param.14) | copy-start | bytes 3538948
Sparse Core Ops, SparseCore 0:
  12.7 61.6 all-reduce.3
Sparse Core Ops, SparseCore 1:
  14.3 52.7 all-gather.1
  69.2 46.8 reduce-scatter.1
where the time goes:
time: 128 us; the launch traced here: 127 us
  waiting for transfers between devices  53 us (41%)
  blocking collectives  33.8 us (26%)
  between operations  17 us (13%)
  other arithmetic  11.8 us (9%)
  matrix products  8.81 us (7%)
  local copies, waits for them, and re-layouts  2.64 us (2%)
    psum x1, waiting for transfers between devices, outer_update(): silo_total = lax.psum(grad_wide, 'silo')  42.6 us
    unnamed x2, blocking collectives  33.8 us
    reduce_scatter x1, waiting for transfers between devices, per_device(): lax.psum_scatter(lax.dot_general(normed, cotangent, (((0,), (0,)), ((), (...  9.85 us
    convert_element_type x1, other arithmetic, outer_update(): grad_wide = pseudo_grad[0].astype(jnp.float32)  4.19 us
    dot_general x1, matrix products, per_device(): jnp.dot(normed_piece, weight_piece, preferred_element_type=jnp.float32)  3.71 us
    broadcast_in_dim x1, other arithmetic, per_device(): new_second[None]  3.68 us
    sub x1, other arithmetic, nesterov(): new_params = params_part - outer_rate * (delta_part + outer_beta * new_mom)  3.48 us
    dot_general x1, matrix products, per_device(): lax.dot_general(cotangent, weight_piece, (((1,), (1,)), ((), ())), prefer...  2.8 us
  transfers between devices with their start and end apart: 3, of which 2 were waited for; matrix products, arithmetic and copies ran while one was open for 12% of the time, Pallas kernels for 0%

commit v1 on v0

v1 whole, which is shorter than its diff:
```python
import math

import jax
import jax.numpy as jnp
from jax import lax
from jax.sharding import PartitionSpec as P

norm_eps = 1e-05
beta_one = 0.9
beta_two = 0.95
corr_one = 1.0 - math.exp(200.0 * math.log(0.9))
corr_two = 1.0 - math.exp(200.0 * math.log(0.95))
learn_rate = 0.001
adam_eps = 1e-08
weight_decay = 0.1
outer_beta = 0.9
outer_rate = 0.7
chunk_count = 2

wide = jnp.float32
narrow = jnp.bfloat16


def adam_step(params, gradient, first_moment, second_moment):
    first_new = beta_one * first_moment + (1.0 - beta_one) * gradient
    second_new = beta_two * second_moment + (1.0 - beta_two) * gradient * gradient
    update = (
        first_new / corr_one / (jnp.sqrt(second_new / corr_two) + adam_eps) + weight_decay * params
    )
    return (params - learn_rate * update, first_new, second_new)


def nesterov(delta_part, params_part, mom_part):
    new_mom = outer_beta * mom_part + delta_part
    new_params = params_part - outer_rate * (delta_part + outer_beta * new_mom)
    return (new_params, new_mom)


def add_narrow(left, right):
    return (left.astype(wide) + right.astype(wide)).astype(narrow)


def silo_sum(halves, silos):
    core = lax.axis_index("silo") & 1

    def swap(part, bit):
        return lax.ppermute(part, "silo", [(i, i ^ bit) for i in range(silos)])

    keep = lax.dynamic_index_in_dim(halves, core, 0, keepdims=False)
    give = lax.dynamic_index_in_dim(halves, 1 - core, 0, keepdims=False)
    total = add_narrow(keep, swap(give, 1))
    bit = 2
    while bit < silos:
        total = add_narrow(total, swap(total, bit))
        bit *= 2
    total = lax.optimization_barrier(total)
    other = swap(total, 1)
    first = jnp.where(core == 0, total, other)
    second = jnp.where(core == 0, other, total)
    return jnp.stack([first, second])


def outer_update(pseudo_grad, outer_params, outer_mom, silos):
    size = pseudo_grad.shape[1]
    spread = lax.optimization_barrier(pseudo_grad[0].astype(wide))
    if silos > 1 and silos & (silos - 1) == 0 and size % 4096 == 0:
        halves = spread.reshape(2, size // 256, 128).astype(narrow)
        total = silo_sum(halves, silos).astype(wide).reshape(size)
    else:
        total = lax.psum(spread, "silo")
    return nesterov(total / silos, outer_params, outer_mom)


def make(silos, n):
    def per_device(
        activations,
        key_cot,
        key_weight,
        weight_first,
        weight_second,
        norm_gain,
        gain_first,
        gain_second,
        pseudo_grad,
        outer_params,
        outer_mom,
    ):
        me = lax.axis_index("fsdp")
        inputs = activations[0]
        tokens, feats = inputs.shape
        rows, cols = key_weight.shape[1:]
        chunks = chunk_count if rows % (16 * chunk_count) == 0 else 1
        depth = rows // chunks

        wide_inputs = inputs.astype(wide)
        inv_rms = lax.rsqrt(
            jnp.mean(wide_inputs * wide_inputs, axis=1, keepdims=True) + norm_eps
        )
        cot_scaled = (key_cot[0].astype(wide) * inv_rms).astype(narrow)
        gain_used = norm_gain[0].astype(narrow).astype(wide)[:, None]
        weight = key_weight[0].astype(wide)
        weight_sent = (weight * gain_used).astype(narrow)

        partial = lax.dot_general(
            inputs, cot_scaled, (((0,), (0,)), ((), ())), preferred_element_type=wide
        ).astype(narrow)
        partial = partial.reshape(n, chunks, depth, cols)
        blocks = inputs.reshape(tokens, n, chunks, depth).transpose(1, 2, 0, 3)

        def shard_of(k, c):
            return lax.dynamic_index_in_dim(partial[:, c], k, 0, keepdims=False)

        def inputs_of(k, c):
            return lax.dynamic_index_in_dim(blocks[:, c], k, 0, keepdims=False)

        even = (me & 1) == 0
        links = [
            [pair for i in range(start, n - 1, 2) for pair in ((i, i + 1), (i + 1, i))]
            for start in (0, 1)
        ]
        to_right = [even, jnp.logical_not(even)]
        places = [jnp.where(right, me, n - 1 - me) for right in to_right]

        def device_at(k, right):
            k = jnp.clip(k, 0, n - 1)
            return jnp.where(right, k, n - 1 - k)

        own = weight_sent.reshape(chunks, depth, cols)
        acc = jnp.zeros((tokens, cols), wide)
        for c in range(chunks):
            acc = acc + jnp.dot(inputs_of(me, c), own[c], preferred_element_type=wide)
        got = [[None for _ in range(chunks)] for _ in links]
        for s in range(n):
            for c in range(chunks):
                sent = [own[c], own[c]]
                if s > 0:
                    for w in range(2):
                        before = got[1 - w][c]
                        owner = device_at(n - s + places[w], to_right[w])
                        sent[w] = jnp.where(
                            s > places[w], add_narrow(before, shard_of(owner, c)), before
                        )
                for w in range(2):
                    got[w][c] = lax.ppermute(sent[w], "fsdp", links[w])
            if s < n - 1:
                for c in range(chunks):
                    for w in range(2):
                        right, place = to_right[1 - w], places[1 - w]
                        block = inputs_of(device_at(place - 1 - s, right), c)
                        term = jnp.dot(block, got[w][c], preferred_element_type=wide)
                        acc = acc + jnp.where(s < place, term, 0.0)
        keys = (acc * inv_rms).astype(narrow)

        new_weight, new_first, new_second, gain_share = [], [], [], []
        for c in range(chunks):
            span = slice(c * depth, (c + 1) * depth)
            raw = shard_of(me, c).astype(wide)
            for w in range(2):
                raw = raw + got[w][c].astype(wide)
            gain_share.append(jnp.sum(raw * weight[span], axis=1))
            out = adam_step(
                weight[span], raw * gain_used[span], weight_first[0, span], weight_second[0, span]
            )
            new_weight.append(out[0].astype(narrow))
            new_first.append(out[1])
            new_second.append(out[2])
        new_gain, new_gain_first, new_gain_second = adam_step(
            norm_gain[0], jnp.concatenate(gain_share), gain_first[0], gain_second[0]
        )
        new_params, new_mom = outer_update(pseudo_grad, outer_params, outer_mom, silos)
        return (
            keys[None],
            jnp.concatenate(new_weight)[None],
            jnp.concatenate(new_first)[None],
            jnp.concatenate(new_second)[None],
            new_gain[None],
            new_gain_first[None],
            new_gain_second[None],
            new_params,
            new_mom,
        )

    return per_device


def solution(mesh):
    return jax.shard_map(
        make(mesh.shape["silo"], mesh.shape["fsdp"]),
        mesh=mesh,
        in_specs=(
            P("silo", "fsdp", None),
            P("silo", "fsdp", None),
            P("silo", "fsdp", None),
            P("silo", "fsdp", None),
            P("silo", "fsdp", None),
            P("silo", "fsdp"),
            P("silo", "fsdp"),
            P("silo", "fsdp"),
            P("silo", "fsdp"),
            P("fsdp"),
            P("fsdp"),
        ),
        out_specs=(
            P("silo", "fsdp", None),
            P("silo", "fsdp", None),
            P("silo", "fsdp", None),
            P("silo", "fsdp", None),
            P("silo", "fsdp"),
            P("silo", "fsdp"),
            P("silo", "fsdp"),
            P("fsdp"),
            P("fsdp"),
        ),
        check_vma=False,
    )
```

time: 128 us -> 88.3 us (0.69)
  waiting for transfers between devices: 53 us -> 9.28 us
  starting transfers between devices: 0.12 us -> 34 us
  blocking collectives: 33.8 us -> 0 us
  between operations: 17 us -> 1.25 us
  local copies, waits for them, and re-layouts: 2.64 us -> 12.7 us
  other arithmetic: 11.8 us -> 17.1 us
  matrix products: 8.81 us -> 13.1 us
    psum x1 -> x0, waiting for transfers between devices: 42.6 us -> none  [outer_update(): silo_total = lax.psum(grad_wide, 'silo')]
    ppermute x0 -> x20, starting transfers between devices: none -> 34 us  [the longest x16 30.8 us: per_device(): got[w][c] = lax.ppermute(sent[w], 'fsdp', links[w])]
    unnamed x2 -> x0, blocking collectives: 33.8 us -> none
    reduce_scatter x1 -> x0, waiting for transfers between devices: 9.85 us -> none  [per_device(): lax.psum_scatter(lax.dot_general(normed, cotangent, (((0,), (0,)), ((), (...]
    ppermute x0 -> x20, waiting for transfers between devices: none -> 9.28 us  [the longest x16 9.09 us: per_device(): got[w][c] = lax.ppermute(sent[w], 'fsdp', links[w])]
    slice x0 -> x4, local copies, waits for them, and re-layouts: none -> 5.06 us  [the longest x1 2.2 us: inputs_of(): return lax.dynamic_index_in_dim(blocks[:, c], k, 0, keepdims=False)]
    dot_general x3 -> x15, matrix products: 8.81 us -> 13.1 us  [the longest x12 8.89 us: per_device(): term = jnp.dot(block, got[w][c], preferred_element_type=wide)]
    select_n x0 -> x6, other arithmetic: none -> 3.74 us  [per_device(): jnp.where(s > places[w], add_narrow(before, shard_of(owner, c)), before)]
  transfers between devices with their start and end apart: 3 -> 20, of which waited for: 2 -> 3; matrix products, arithmetic and copies ran while one was open for 12% -> 40% of each run, Pallas kernels for 0% -> 0%
where the time goes in v1:
time: 88.3 us; the launch traced here: 87.4 us
  starting transfers between devices  34 us (39%)
  other arithmetic  17.1 us (19%)
  matrix products  13.1 us (15%)
  local copies, waits for them, and re-layouts  12.7 us (14%)
  waiting for transfers between devices  9.28 us (11%)
  between operations  1.25 us (1%)
    ppermute x16, starting transfers between devices, per_device(): got[w][c] = lax.ppermute(sent[w], 'fsdp', links[w])  30.8 us
    ppermute x16, waiting for transfers between devices, per_device(): got[w][c] = lax.ppermute(sent[w], 'fsdp', links[w])  9.09 us
    dot_general x12, matrix products, per_device(): term = jnp.dot(block, got[w][c], preferred_element_type=wide)  8.89 us
    unnamed x35, local copies, waits for them, and re-layouts  4.37 us
    select_n x6, other arithmetic, per_device(): jnp.where(s > places[w], add_narrow(before, shard_of(owner, c)), before)  3.74 us
    ppermute x4, starting transfers between devices, swap(): return lax.ppermute(part, 'silo', [(i, i ^ bit) for i in range(silos)])  3.21 us
    convert_element_type x1, local copies, waits for them, and re-layouts, per_device(): partial = lax.dot_general(inputs, cot_scaled, (((0,), (0,)), ((), ())), p...  2.48 us
    dot_general x2, matrix products, per_device(): acc = acc + jnp.dot(inputs_of(me, c), own[c], preferred_element_type=wide)  2.35 us
  transfers between devices with their start and end apart: 20, of which 3 were waited for; matrix products, arithmetic and copies ran while one was open for 40% of the time, Pallas kernels for 0%

profile of v1, /device:TPU:0, one launch (start us, length us, event | category | flops | bytes accessed | tf_op | source)
XLA Modules:
  0.0 87.4 jit_solution(15521027817738577269)
XLA Ops:
  0.6 0.7 convert_convert_fusion
  1.4 1.4 %fusion.16 = bf16[576,512]{1,0:T(8,128)(2,1)S(1)} fusion(f32[576]{0:T(1024)S(1)} %get-tuple-element.50, bf16[1,576,512]{2,1,0:T(8,128)(2,1)} %param.13), kind=kLoop, calls=%fused_computation.37 | loop fusion | flops 884736 | bytes 1181952 | tf_op jit(solution)/shard_map/convert_element_type | solution.py:102
  2.7 0.9 %fusion.102 = (bf16[288,512]{1,0:T(8,128)(2,1)}, bf16[288,512]{1,0:T(8,128)(2,1)}) fusion(bf16[576,512]{1,0:T(8,128)(2,1)S(1)} %fusion.16), kind=kLoop, calls=%fused_computation.159 | loop fusion | bytes 1179648 | tf_op jit(solution)/shard_map/slice | solution.py:131
  3.6 3.0 %collective-permute-start.2 = (bf16[288,512]{1,0:T(8,128)(2,1)}, bf16[288,512]{1,0:T(8,128)(2,1)}, u32[]{:S(2)}, u32[]{:S(2)}) collective-permute-start(bf16[288,512]{1,0:T(8,128)(2,1)} %get-tuple-element.48), channel_id=1, source_target_pairs={{0,1},{1,0},{2,3},{3,2},{4,5},{5,4},{6,7},{7,6},{8,9},{9,8},{10,11... | collective-permute-start | bytes 884744 | tf_op jit(solution)/shard_map/ppermute | solution.py:144
  6.7 1.4 %collective-permute-start.3 = (bf16[288,512]{1,0:T(8,128)(2,1)}, bf16[288,512]{1,0:T(8,128)(2,1)}, u32[]{:S(2)}, u32[]{:S(2)}) collective-permute-start(bf16[288,512]{1,0:T(8,128)(2,1)} %get-tuple-element.48), channel_id=1, source_target_pairs={{1,2},{2,1},{5,6},{6,5},{9,10},{10,9},{13,14},{14,13},{17,18},{18,... | collective-permute-start | bytes 884744 | tf_op jit(solution)/shard_map/ppermute | solution.py:144
  8.0 3.7 %collective-permute-start = (bf16[288,512]{1,0:T(8,128)(2,1)}, bf16[288,512]{1,0:T(8,128)(2,1)}, u32[]{:S(2)}, u32[]{:S(2)}) collective-permute-start(bf16[288,512]{1,0:T(8,128)(2,1)} %get-tuple-element.47), channel_id=1, source_target_pairs={{0,1},{1,0},{2,3},{3,2},{4,5},{5,4},{6,7},{7,6},{8,9},{9,8},{10,11... | collective-permute-start | bytes 884744 | tf_op jit(solution)/shard_map/ppermute | solution.py:144
  11.8 1.4 %collective-permute-start.1 = (bf16[288,512]{1,0:T(8,128)(2,1)}, bf16[288,512]{1,0:T(8,128)(2,1)}, u32[]{:S(2)}, u32[]{:S(2)}) collective-permute-start(bf16[288,512]{1,0:T(8,128)(2,1)} %get-tuple-element.47), channel_id=1, source_target_pairs={{1,2},{2,1},{5,6},{6,5},{9,10},{10,9},{13,14},{14,13},{17,18},{18,... | collective-permute-start | bytes 884744 | tf_op jit(solution)/shard_map/ppermute | solution.py:144
  13.2 1.7 %convert_element_type.370 = f32[1,393216]{1,0:T(1,128)S(1)} convert(bf16[1,393216]{1,0:T(2,128)(2,1)S(1)} %copy-done.9) | non-fusion elementwise | flops 393216 | bytes 2359296 | tf_op jit(solution)/shard_map/convert_element_type | solution.py:65
  15.0 0.8 dynamic-slice_bitcast_fusion
  15.7 0.8 copy-done
  16.9 1.4 %copy.22 = bf16[1,256,2304]{1,2,0:T(8,128)(2,1)} copy(bf16[1,256,2304]{2,1,0:T(8,128)(2,1)S(1)} %copy-done) | data formatting | bytes 2359296 | tf_op args[0]
  18.3 1.9 %fusion = bf16[2304,512]{0,1:T(8,128)(2,1)S(1)} fusion(bf16[1,256,2304]{2,1,0:T(8,128)(2,1)S(1)} %copy-done, bf16[1,256,512]{2,1,0:T(8,128)(2,1)} %param.12, f32[256]{0:T(256)S(1)} %add_rsqrt_fusion), kind=kOutput, calls=%fused_computation.1 | convolution fusion | flops 605552640 | bytes 3802112 | tf_op jit(solution)/shard_map/dot_general | solution.py:104
  20.1 2.5 %copy.23 = bf16[2304,512]{1,0:T(8,128)(2,1)} copy(bf16[2304,512]{0,1:T(8,128)(2,1)S(1)} %fusion) | data formatting | bytes 4718592 | tf_op jit(solution)/shard_map/convert_element_type | solution.py:106
  22.6 1.9 %fusion.100 = (bf16[4,1,288,512]{3,2,1,0:T(8,128)(2,1)S(1)}, bf16[4,1,288,512]{3,2,1,0:T(8,128)(2,1)S(1)}) fusion(bf16[4,2,288,512]{3,2,1,0:T(8,128)(2,1)} %bitcast.173), kind=kLoop, calls=%fused_computation.157 | loop fusion | bytes 4718592 | tf_op jit(solution)/shard_map/slice | solution.py:111
  24.5 2.2 %fusion.101 = (bf16[4,1,256,288]{2,3,1,0:T(8,128)(2,1)S(1)}, bf16[4,1,256,288]{2,3,1,0:T(8,128)(2,1)}) fusion(bf16[4,2,256,288]{2,3,1,0:T(8,128)(2,1)} %bitcast.176), kind=kLoop, calls=%fused_computation.158 | loop fusion | bytes 2359296 | tf_op jit(solution)/shard_map/slice | solution.py:114
  27.1 2.0 %convolution_add_fusion = f32[256,512]{1,0:T(8,128)} fusion(f32[256,512]{1,0:T(8,128)S(1)} %fusion.63, bf16[4,1,256,288]{2,3,1,0:T(8,128)(2,1)} %get-tuple-element.40, s32[]{:T(128)S(6)} %select_n.254, bf16[576,512]{1,0:T(8,128)(2,1)S(1)} %copy-done.2), kind=kOutput, calls=%fused_computation.21 | convolution fusion | flops 75628544 | bytes 1490948 | tf_op jit(solution)/shard_map/dot_general | solution.py:131
  29.3 1.2 %convert_element_type.270 = f32[1,576,512]{2,1,0:T(8,128)S(1)} convert(bf16[1,576,512]{2,1,0:T(8,128)(2,1)} %param.13) | non-fusion elementwise | flops 294912 | bytes 1769472 | tf_op jit(solution)/shard_map/convert_element_type | solution.py:101
  30.6 1.5 %fusion.38 = (bf16[288,512]{1,0:T(8,128)(2,1)S(1)}, bf16[288,512]{1,0:T(8,128)(2,1)S(1)}) fusion(bf16[288,512]{1,0:T(8,128)(2,1)} %collective-permute-done.2, bf16[4,1,288,512]{3,2,1,0:T(8,128)(2,1)S(1)} %get-tuple-element.30, s32[]{:T(128)S(6)} %select_n.280, pred[]{:T(512)S(6)} %lt.94, bf16[288,512]{1,0:T(8,128)(2,1)} %collective-permute-done.3, ...), kind=kLoop, calls=%fused_computation.88 | loop fusion | flops 1474560 | bytes 1769482 | tf_op jit(solution)/shard_map/jit(_where)/select_n | solution.py:140
  32.1 0.8 collective-permute-start.7
  32.9 3.9 %collective-permute-start.6 = (bf16[288,512]{1,0:T(8,128)(2,1)S(1)}, bf16[288,512]{1,0:T(8,128)(2,1)S(1)}, u32[]{:S(2)}, u32[]{:S(2)}) collective-permute-start(bf16[288,512]{1,0:T(8,128)(2,1)S(1)} %get-tuple-element.44), channel_id=1, source_target_pairs={{0,1},{1,0},{2,3},{3,2},{4,5},{5,4},{6,7},{7,6},{8,9},{9,8},{10,11... | collective-permute-start | bytes 884744 | tf_op jit(solution)/shard_map/ppermute | solution.py:144
  36.8 1.5 %fusion.36 = (bf16[288,512]{1,0:T(8,128)(2,1)S(1)}, bf16[288,512]{1,0:T(8,128)(2,1)S(1)}) fusion(bf16[288,512]{1,0:T(8,128)(2,1)} %collective-permute-done, bf16[4,1,288,512]{3,2,1,0:T(8,128)(2,1)S(1)} %get-tuple-element.29, s32[]{:T(128)S(6)} %select_n.280, pred[]{:T(512)S(6)} %lt.94, bf16[288,512]{1,0:T(8,128)(2,1)} %collective-permute-done.1, ...), kind=kLoop, calls=%fused_computation.86 | loop fusion | flops 1474560 | bytes 1769482 | tf_op jit(solution)/shard_map/jit(_where)/select_n | solution.py:140
  38.3 0.7 collective-permute-start.5
  39.0 1.3 %collective-permute-start.4 = (bf16[288,512]{1,0:T(8,128)(2,1)S(1)}, bf16[288,512]{1,0:T(8,128)(2,1)S(1)}, u32[]{:S(2)}, u32[]{:S(2)}) collective-permute-start(bf16[288,512]{1,0:T(8,128)(2,1)S(1)} %get-tuple-element.38), channel_id=1, source_target_pairs={{0,1},{1,0},{2,3},{3,2},{4,5},{5,4},{6,7},{7,6},{8,9},{9,8},{10,11... | collective-permute-start | bytes 884744 | tf_op jit(solution)/shard_map/ppermute | solution.py:144
  40.4 1.3 %convolution_select_fusion.8 = f32[256,512]{1,0:T(8,128)S(1)} fusion(bf16[288,512]{1,0:T(8,128)(2,1)} %collective-permute-done.3, pred[]{:T(512)S(6)} %gt.25, bf16[4,1,256,288]{2,3,1,0:T(8,128)(2,1)S(1)} %copy-done.5, s32[]{:T(128)S(6)} %select_n.263), kind=kOutput, calls=%fused_computation.14 | convolution fusion | flops 75628544 | bytes 966661 | tf_op jit(solution)/shard_map/dot_general | solution.py:150
  41.7 1.4 %convolution_select_fusion.10 = f32[256,512]{1,0:T(8,128)S(1)} fusion(bf16[288,512]{1,0:T(8,128)(2,1)} %collective-permute-done.1, pred[]{:T(512)S(6)} %gt.25, bf16[4,1,256,288]{2,3,1,0:T(8,128)(2,1)S(1)} %copy-done.4, s32[]{:T(128)S(6)} %select_n.263), kind=kOutput, calls=%fused_computation.16 | convolution fusion | flops 75628544 | bytes 966661 | tf_op jit(solution)/shard_map/dot_general | solution.py:150
  43.0 1.3 %convolution_select_fusion.9 = f32[256,512]{1,0:T(8,128)S(1)} fusion(bf16[288,512]{1,0:T(8,128)(2,1)} %collective-permute-done.2, pred[]{:T(512)S(6)} %gt.24, bf16[4,1,256,288]{2,3,1,0:T(8,128)(2,1)S(1)} %copy-done.5, s32[]{:T(128)S(6)} %select_n.258), kind=kOutput, calls=%fused_computation.15 | convolution fusion | flops 75628544 | bytes 966661 | tf_op jit(solution)/shard_map/dot_general | solution.py:150
  44.3 1.1 %fusion.18 = bf16[1536,128]{1,0:T(8,128)(2,1)S(1)} fusion(bf16[1536,128]{1,0:T(8,128)(2,1)} %collective-permute-done.16, bf16[2,1536,128]{2,1,0:T(8,128)(2,1)S(1)} %bitcast.178, s32[]{:T(128)S(6)} %select_n.318), kind=kLoop, calls=%fused_computation.42 | loop fusion | flops 786432 | bytes 1179652 | tf_op jit(solution)/shard_map/convert_element_type | solution.py:40
  45.5 1.6 %collective-permute-start.17 = (bf16[1536,128]{1,0:T(8,128)(2,1)S(1)}, bf16[1536,128]{1,0:T(8,128)(2,1)S(1)}, u32[]{:S(2)}, u32[]{:S(2)}) collective-permute-start(bf16[1536,128]{1,0:T(8,128)(2,1)S(1)} %fusion.18), channel_id=1, source_target_pairs={{0,8},{4,12},{8,0},{12,4},{16,24},{20,28},{24,16},{28,20},{1,9},{5... | collective-permute-start | bytes 1179656 | tf_op jit(solution)/shard_map/ppermute | solution.py:47
  47.2 0.7 collective-permute-start.11
  47.9 3.3 %collective-permute-start.10 = (bf16[288,512]{1,0:T(8,128)(2,1)S(1)}, bf16[288,512]{1,0:T(8,128)(2,1)S(1)}, u32[]{:S(2)}, u32[]{:S(2)}) collective-permute-start(bf16[288,512]{1,0:T(8,128)(2,1)S(1)} %get-tuple-element.41), channel_id=1, source_target_pairs={{0,1},{1,0},{2,3},{3,2},{4,5},{5,4},{6,7},{7,6},{8,9},{9,8},{10,11... | collective-permute-start | bytes 884744 | tf_op jit(solution)/shard_map/ppermute | solution.py:144
  51.4 0.7 collective-permute-start.9
  52.1 2.1 %collective-permute-start.8 = (bf16[288,512]{1,0:T(8,128)(2,1)S(1)}, bf16[288,512]{1,0:T(8,128)(2,1)S(1)}, u32[]{:S(2)}, u32[]{:S(2)}) collective-permute-start(bf16[288,512]{1,0:T(8,128)(2,1)S(1)} %get-tuple-element.35), channel_id=1, source_target_pairs={{0,1},{1,0},{2,3},{3,2},{4,5},{5,4},{6,7},{7,6},{8,9},{9,8},{10,11... | collective-permute-start | bytes 884744 | tf_op jit(solution)/shard_map/ppermute | solution.py:144
  55.8 1.6 %collective-permute-start.18 = (bf16[1536,128]{1,0:T(8,128)(2,1)S(1)}, bf16[1536,128]{1,0:T(8,128)(2,1)S(1)}, u32[]{:S(2)}, u32[]{:S(2)}) collective-permute-start(bf16[1536,128]{1,0:T(8,128)(2,1)S(1)} %add_convert_fusion.1), channel_id=1, source_target_pairs={{0,16},{4,20},{8,24},{12,28},{16,0},{20,4},{24,8},{28,12},{1,17},{... | collective-permute-start | bytes 1179656 | tf_op jit(solution)/shard_map/ppermute | solution.py:47
  57.4 5.9 %collective-permute-done.8 = bf16[288,512]{1,0:T(8,128)(2,1)S(1)} collective-permute-done((bf16[288,512]{1,0:T(8,128)(2,1)S(1)}, bf16[288,512]{1,0:T(8,128)(2,1)S(1)}, u32[]{:S(2)}, u32[]{:S(2)}) %collective-permute-start.8) | collective-permute-done | bytes 294944 | tf_op jit(solution)/shard_map/ppermute | solution.py:144
  63.5 0.7 collective-permute-start.13
  64.2 3.5 %collective-permute-start.12 = (bf16[288,512]{1,0:T(8,128)(2,1)S(1)}, bf16[288,512]{1,0:T(8,128)(2,1)S(1)}, u32[]{:S(2)}, u32[]{:S(2)}) collective-permute-start(bf16[288,512]{1,0:T(8,128)(2,1)S(1)} %get-tuple-element.31), channel_id=1, source_target_pairs={{0,1},{1,0},{2,3},{3,2},{4,5},{5,4},{6,7},{7,6},{8,9},{9,8},{10,11... | collective-permute-start | bytes 884744 | tf_op jit(solution)/shard_map/ppermute | solution.py:144
  67.9 0.7 collective-permute-start.15
  68.6 2.9 %collective-permute-start.14 = (bf16[288,512]{1,0:T(8,128)(2,1)S(1)}, bf16[288,512]{1,0:T(8,128)(2,1)S(1)}, u32[]{:S(2)}, u32[]{:S(2)}) collective-permute-start(bf16[288,512]{1,0:T(8,128)(2,1)S(1)} %get-tuple-element.33), channel_id=1, source_target_pairs={{0,1},{1,0},{2,3},{3,2},{4,5},{5,4},{6,7},{7,6},{8,9},{9,8},{10,11... | collective-permute-start | bytes 884744 | tf_op jit(solution)/shard_map/ppermute | solution.py:144
  72.8 0.4 copy-done.8
  73.2 2.4 %fusion.17 = bf16[1,256,512]{2,1,0:T(8,128)(2,1)} fusion(f32[256,512]{1,0:T(8,128)S(1)} %convolution_select_fusion, f32[256,512]{1,0:T(8,128)S(1)} %convolution_select_fusion.1, f32[256,512]{1,0:T(8,128)S(1)} %convolution_select_fusion.2, f32[256,512]{1,0:T(8,128)S(1)} %convolution_select_fusion.3, f32[256,512]{1,0:T(8,128)S(1)} %convolution_select_fusion.4, ...), kind=kOutput, calls=%fused_computation.38 | convolution fusion | flops 77463552 | bytes 6996997 | tf_op jit(solution)/shard_map/dot_general | solution.py:150
  75.6 3.1 %collective-permute-done.14 = bf16[288,512]{1,0:T(8,128)(2,1)S(1)} collective-permute-done((bf16[288,512]{1,0:T(8,128)(2,1)S(1)}, bf16[288,512]{1,0:T(8,128)(2,1)S(1)}, u32[]{:S(2)}, u32[]{:S(2)}) %collective-permute-start.14) | collective-permute-done | bytes 294944 | tf_op jit(solution)/shard_map/ppermute | solution.py:144
  78.7 1.4 %subtract_convert_fusion.1 = (bf16[288,512]{1,0:T(8,128)(2,1)S(1)}, f32[288,512]{1,0:T(8,128)S(1)}, f32[288,512]{1,0:T(8,128)S(1)}, bf16[288,512]{1,0:T(8,128)(2...) fusion(f32[1,576,512]{2,1,0:T(8,128)S(1)} %convert_element_type.270, ...), kind=kLoop, calls=%fused_computation.83 | loop fusion | flops 6782400 | bytes 8262148 | tf_op jit(solution)/shard_map/convert_element_type | solution.py:164
  80.3 0.9 maximum_bitcast_fusion.2
  81.2 1.6 %maximum_bitcast_fusion = (f32[1,576,512]{2,1,0:T(8,128)}, f32[1,576,512]{2,1,0:T(8,128)}) fusion(f32[288,512]{1,0:T(8,128)S(1)} %get-tuple-element.26, f32[288,512]{1,0:T(8,128)S(1)} %get-tuple-element.20, f32[288,512]{1,0:T(8,128)S(1)} %get-tuple-element.25, f32[288,512]{1,0:T(8,128)S(1)} %get-tuple-element.19), kind=kLoop, calls=%fused_computation.33 | loop fusion | flops 589824 | bytes 4718592 | tf_op jit(solution)/shard_map/broadcast_in_dim | solution.py:174
  82.8 0.7 multiply_subtract_fusion.1
  83.7 1.2 %copy-done.11 = f32[393216]{0:T(1024)S(1)} copy-done((f32[393216]{0:T(1024)S(1)}, f32[393216]{0:T(1024)}, u32[]{:S(2)}) %copy-start.11) | copy-done | bytes 1572888
  84.9 0.5 copy-done.10
  85.4 2.0 %multiply_subtract_fusion = (f32[393216]{0:T(1024)}, f32[393216]{0:T(1024)}) fusion(f32[393216]{0:T(1024)S(1)} %copy-done.10, f32[393216]{0:T(1024)S(1)} %bitcast.175, f32[393216]{0:T(1024)S(1)} %copy-done.11), kind=kLoop, calls=%fused_computation.3 | loop fusion | flops 2359296 | bytes 7864320 | tf_op jit(solution)/shard_map/sub | solution.py:35
  (73 shorter events, 4.9 us)
Async XLA Ops:
  1.3 11.8 %copy-start.9 = (bf16[1,393216]{1,0:T(2,128)(2,1)S(1)}, bf16[1,393216]{1,0:T(2,128)(2,1)}, u32[]{:S(2)}) copy-start(bf16[1,393216]{1,0:T(2,128)(2,1)} %param.19) | copy-start | bytes 2359300
  2.7 10.5 %copy-start.1 = (bf16[576,512]{1,0:T(8,128)(2,1)}, bf16[576,512]{1,0:T(8,128)(2,1)S(1)}, u32[]{:S(2)}) copy-start(bf16[576,512]{1,0:T(8,128)(2,1)S(1)} %fusion.16) | copy-start | bytes 1769476
  3.6 26.9 %collective-permute-start.2 = (bf16[288,512]{1,0:T(8,128)(2,1)}, bf16[288,512]{1,0:T(8,128)(2,1)}, u32[]{:S(2)}, u32[]{:S(2)}) collective-permute-start(bf16[288,512]{1,0:T(8,128)(2,1)} %get-tuple-element.48), channel_id=1, source_target_pairs={{0,1},{1,0},{2,3},{3,2},{4,5},{5,4},{6,7},{7,6},{8,9},{9,8},{10,11... | collective-permute-start | bytes 884744 | tf_op jit(solution)/shard_map/ppermute | solution.py:144
  6.7 23.9 %collective-permute-start.3 = (bf16[288,512]{1,0:T(8,128)(2,1)}, bf16[288,512]{1,0:T(8,128)(2,1)}, u32[]{:S(2)}, u32[]{:S(2)}) collective-permute-start(bf16[288,512]{1,0:T(8,128)(2,1)} %get-tuple-element.48), channel_id=1, source_target_pairs={{1,2},{2,1},{5,6},{6,5},{9,10},{10,9},{13,14},{14,13},{17,18},{18,... | collective-permute-start | bytes 884744 | tf_op jit(solution)/shard_map/ppermute | solution.py:144
  8.0 28.7 %collective-permute-start = (bf16[288,512]{1,0:T(8,128)(2,1)}, bf16[288,512]{1,0:T(8,128)(2,1)}, u32[]{:S(2)}, u32[]{:S(2)}) collective-permute-start(bf16[288,512]{1,0:T(8,128)(2,1)} %get-tuple-element.47), channel_id=1, source_target_pairs={{0,1},{1,0},{2,3},{3,2},{4,5},{5,4},{6,7},{7,6},{8,9},{9,8},{10,11... | collective-permute-start | bytes 884744 | tf_op jit(solution)/shard_map/ppermute | solution.py:144
  11.8 25.0 %collective-permute-start.1 = (bf16[288,512]{1,0:T(8,128)(2,1)}, bf16[288,512]{1,0:T(8,128)(2,1)}, u32[]{:S(2)}, u32[]{:S(2)}) collective-permute-start(bf16[288,512]{1,0:T(8,128)(2,1)} %get-tuple-element.47), channel_id=1, source_target_pairs={{1,2},{2,1},{5,6},{6,5},{9,10},{10,9},{13,14},{14,13},{17,18},{18,... | collective-permute-start | bytes 884744 | tf_op jit(solution)/shard_map/ppermute | solution.py:144
  14.8 1.7 %copy-start = (bf16[1,256,2304]{2,1,0:T(8,128)(2,1)S(1)}, bf16[1,256,2304]{2,1,0:T(8,128)(2,1)}, u32[]{:S(2)}) copy-start(bf16[1,256,2304]{2,1,0:T(8,128)(2,1)} %param.11) | copy-start | bytes 3538948
  14.9 3.3 %copy-start.6 = (bf16[393216]{0:T(1024)(128)(2,1)}, bf16[393216]{0:T(1024)(128)(2,1)S(1)}, u32[]{:S(2)}) copy-start(bf16[393216]{0:T(1024)(128)(2,1)S(1)} %convert_element_type.343) | copy-start | bytes 2359300
  15.7 28.6 %collective-permute-start.16 = (bf16[1536,128]{1,0:T(8,128)(2,1)}, bf16[1536,128]{1,0:T(8,128)(2,1)}, u32[]{:S(2)}, u32[]{:S(2)}) collective-permute-start(bf16[1536,128]{1,0:T(8,128)(2,1)} %dynamic-slice_bitcast_fusion), channel_id=1, source_target_pairs={{0,4},{4,0},{8,12},{12,8},{16,20},{20,16},{24,28},{28,24},{1,5},{5... | collective-permute-start | bytes 1179656 | tf_op jit(solution)/shard_map/ppermute | solution.py:47
  24.5 2.2 %copy-start.2 = (bf16[576,512]{1,0:T(8,128)(2,1)S(1)}, bf16[576,512]{1,0:T(8,128)(2,1)}, u32[]{:S(2)}) copy-start(bf16[576,512]{1,0:T(8,128)(2,1)} %copy-done.1) | copy-start | bytes 1769476
  26.7 2.4 %copy-start.3 = (bf16[4,1,256,288]{2,3,1,0:T(8,128)(2,1)}, bf16[4,1,256,288]{2,3,1,0:T(8,128)(2,1)S(1)}, u32[]{:S(2)}) copy-start(bf16[4,1,256,288]{2,3,1,0:T(8,128)(2,1)S(1)} %get-tuple-element.39) | copy-start | bytes 1769476
  32.1 8.3 %copy-start.5 = (bf16[4,1,256,288]{2,3,1,0:T(8,128)(2,1)S(1)}, bf16[4,1,256,288]{2,3,1,0:T(8,128)(2,1)}, u32[]{:S(2)}) copy-start(bf16[4,1,256,288]{2,3,1,0:T(8,128)(2,1)} %get-tuple-element.40) | copy-start | bytes 1769476
  32.1 15.0 %collective-permute-start.7 = (bf16[288,512]{1,0:T(8,128)(2,1)S(1)}, bf16[288,512]{1,0:T(8,128)(2,1)S(1)}, u32[]{:S(2)}, u32[]{:S(2)}) collective-permute-start(bf16[288,512]{1,0:T(8,128)(2,1)S(1)} %get-tuple-element.43), channel_id=1, source_target_pairs={{1,2},{2,1},{5,6},{6,5},{9,10},{10,9},{13,14},{14,13},{17,18},{18,... | collective-permute-start | bytes 884744 | tf_op jit(solution)/shard_map/ppermute | solution.py:144
  32.9 14.1 %collective-permute-start.6 = (bf16[288,512]{1,0:T(8,128)(2,1)S(1)}, bf16[288,512]{1,0:T(8,128)(2,1)S(1)}, u32[]{:S(2)}, u32[]{:S(2)}) collective-permute-start(bf16[288,512]{1,0:T(8,128)(2,1)S(1)} %get-tuple-element.44), channel_id=1, source_target_pairs={{0,1},{1,0},{2,3},{3,2},{4,5},{5,4},{6,7},{7,6},{8,9},{9,8},{10,11... | collective-permute-start | bytes 884744 | tf_op jit(solution)/shard_map/ppermute | solution.py:144
  36.8 4.9 %copy-start.4 = (bf16[4,1,256,288]{2,3,1,0:T(8,128)(2,1)S(1)}, bf16[4,1,256,288]{2,3,1,0:T(8,128)(2,1)}, u32[]{:S(2)}) copy-start(bf16[4,1,256,288]{2,3,1,0:T(8,128)(2,1)} %copy-done.3) | copy-start | bytes 1769476
  38.3 12.9 %collective-permute-start.5 = (bf16[288,512]{1,0:T(8,128)(2,1)S(1)}, bf16[288,512]{1,0:T(8,128)(2,1)S(1)}, u32[]{:S(2)}, u32[]{:S(2)}) collective-permute-start(bf16[288,512]{1,0:T(8,128)(2,1)S(1)} %get-tuple-element.37), channel_id=1, source_target_pairs={{1,2},{2,1},{5,6},{6,5},{9,10},{10,9},{13,14},{14,13},{17,18},{18,... | collective-permute-start | bytes 884744 | tf_op jit(solution)/shard_map/ppermute | solution.py:144
  39.0 12.2 %collective-permute-start.4 = (bf16[288,512]{1,0:T(8,128)(2,1)S(1)}, bf16[288,512]{1,0:T(8,128)(2,1)S(1)}, u32[]{:S(2)}, u32[]{:S(2)}) collective-permute-start(bf16[288,512]{1,0:T(8,128)(2,1)S(1)} %get-tuple-element.38), channel_id=1, source_target_pairs={{0,1},{1,0},{2,3},{3,2},{4,5},{5,4},{6,7},{7,6},{8,9},{9,8},{10,11... | collective-permute-start | bytes 884744 | tf_op jit(solution)/shard_map/ppermute | solution.py:144
  41.7 2.7 %copy-start.7 = (bf16[393216]{0:T(1024)(128)(2,1)S(1)}, bf16[393216]{0:T(1024)(128)(2,1)}, u32[]{:S(2)}) copy-start(bf16[393216]{0:T(1024)(128)(2,1)} %copy-done.6) | copy-start | bytes 2359300
  45.5 10.2 %collective-permute-start.17 = (bf16[1536,128]{1,0:T(8,128)(2,1)S(1)}, bf16[1536,128]{1,0:T(8,128)(2,1)S(1)}, u32[]{:S(2)}, u32[]{:S(2)}) collective-permute-start(bf16[1536,128]{1,0:T(8,128)(2,1)S(1)} %fusion.18), channel_id=1, source_target_pairs={{0,8},{4,12},{8,0},{12,4},{16,24},{20,28},{24,16},{28,20},{1,9},{5... | collective-permute-start | bytes 1179656 | tf_op jit(solution)/shard_map/ppermute | solution.py:47
  47.2 20.5 %collective-permute-start.11 = (bf16[288,512]{1,0:T(8,128)(2,1)S(1)}, bf16[288,512]{1,0:T(8,128)(2,1)S(1)}, u32[]{:S(2)}, u32[]{:S(2)}) collective-permute-start(bf16[288,512]{1,0:T(8,128)(2,1)S(1)} %get-tuple-element.42), channel_id=1, source_target_pairs={{1,2},{2,1},{5,6},{6,5},{9,10},{10,9},{13,14},{14,13},{17,18},{18,... | collective-permute-start | bytes 884744 | tf_op jit(solution)/shard_map/ppermute | solution.py:144
  47.9 19.8 %collective-permute-start.10 = (bf16[288,512]{1,0:T(8,128)(2,1)S(1)}, bf16[288,512]{1,0:T(8,128)(2,1)S(1)}, u32[]{:S(2)}, u32[]{:S(2)}) collective-permute-start(bf16[288,512]{1,0:T(8,128)(2,1)S(1)} %get-tuple-element.41), channel_id=1, source_target_pairs={{0,1},{1,0},{2,3},{3,2},{4,5},{5,4},{6,7},{7,6},{8,9},{9,8},{10,11... | collective-permute-start | bytes 884744 | tf_op jit(solution)/shard_map/ppermute | solution.py:144
  51.4 6.0 %collective-permute-start.9 = (bf16[288,512]{1,0:T(8,128)(2,1)S(1)}, bf16[288,512]{1,0:T(8,128)(2,1)S(1)}, u32[]{:S(2)}, u32[]{:S(2)}) collective-permute-start(bf16[288,512]{1,0:T(8,128)(2,1)S(1)} %get-tuple-element.36), channel_id=1, source_target_pairs={{1,2},{2,1},{5,6},{6,5},{9,10},{10,9},{13,14},{14,13},{17,18},{18,... | collective-permute-start | bytes 884744 | tf_op jit(solution)/shard_map/ppermute | solution.py:144
  52.1 11.2 %collective-permute-start.8 = (bf16[288,512]{1,0:T(8,128)(2,1)S(1)}, bf16[288,512]{1,0:T(8,128)(2,1)S(1)}, u32[]{:S(2)}, u32[]{:S(2)}) collective-permute-start(bf16[288,512]{1,0:T(8,128)(2,1)S(1)} %get-tuple-element.35), channel_id=1, source_target_pairs={{0,1},{1,0},{2,3},{3,2},{4,5},{5,4},{6,7},{7,6},{8,9},{9,8},{10,11... | collective-permute-start | bytes 884744 | tf_op jit(solution)/shard_map/ppermute | solution.py:144
  55.8 24.3 %collective-permute-start.18 = (bf16[1536,128]{1,0:T(8,128)(2,1)S(1)}, bf16[1536,128]{1,0:T(8,128)(2,1)S(1)}, u32[]{:S(2)}, u32[]{:S(2)}) collective-permute-start(bf16[1536,128]{1,0:T(8,128)(2,1)S(1)} %add_convert_fusion.1), channel_id=1, source_target_pairs={{0,16},{4,20},{8,24},{12,28},{16,0},{20,4},{24,8},{28,12},{1,17},{... | collective-permute-start | bytes 1179656 | tf_op jit(solution)/shard_map/ppermute | solution.py:47
  63.5 12.1 %collective-permute-start.13 = (bf16[288,512]{1,0:T(8,128)(2,1)S(1)}, bf16[288,512]{1,0:T(8,128)(2,1)S(1)}, u32[]{:S(2)}, u32[]{:S(2)}) collective-permute-start(bf16[288,512]{1,0:T(8,128)(2,1)S(1)} %get-tuple-element.32), channel_id=1, source_target_pairs={{1,2},{2,1},{5,6},{6,5},{9,10},{10,9},{13,14},{14,13},{17,18},{18,... | collective-permute-start | bytes 884744 | tf_op jit(solution)/shard_map/ppermute | solution.py:144
  64.2 11.4 %collective-permute-start.12 = (bf16[288,512]{1,0:T(8,128)(2,1)S(1)}, bf16[288,512]{1,0:T(8,128)(2,1)S(1)}, u32[]{:S(2)}, u32[]{:S(2)}) collective-permute-start(bf16[288,512]{1,0:T(8,128)(2,1)S(1)} %get-tuple-element.31), channel_id=1, source_target_pairs={{0,1},{1,0},{2,3},{3,2},{4,5},{5,4},{6,7},{7,6},{8,9},{9,8},{10,11... | collective-permute-start | bytes 884744 | tf_op jit(solution)/shard_map/ppermute | solution.py:144
  67.9 7.7 %collective-permute-start.15 = (bf16[288,512]{1,0:T(8,128)(2,1)S(1)}, bf16[288,512]{1,0:T(8,128)(2,1)S(1)}, u32[]{:S(2)}, u32[]{:S(2)}) collective-permute-start(bf16[288,512]{1,0:T(8,128)(2,1)S(1)} %get-tuple-element.34), channel_id=1, source_target_pairs={{1,2},{2,1},{5,6},{6,5},{9,10},{10,9},{13,14},{14,13},{17,18},{18,... | collective-permute-start | bytes 884744 | tf_op jit(solution)/shard_map/ppermute | solution.py:144
  68.6 10.1 %collective-permute-start.14 = (bf16[288,512]{1,0:T(8,128)(2,1)S(1)}, bf16[288,512]{1,0:T(8,128)(2,1)S(1)}, u32[]{:S(2)}, u32[]{:S(2)}) collective-permute-start(bf16[288,512]{1,0:T(8,128)(2,1)S(1)} %get-tuple-element.33), channel_id=1, source_target_pairs={{0,1},{1,0},{2,3},{3,2},{4,5},{5,4},{6,7},{7,6},{8,9},{9,8},{10,11... | collective-permute-start | bytes 884744 | tf_op jit(solution)/shard_map/ppermute | solution.py:144
  72.1 1.0 %copy-start.8 = (f32[256,512]{1,0:T(8,128)S(1)}, f32[256,512]{1,0:T(8,128)}, u32[]{:S(2)}) copy-start(f32[256,512]{1,0:T(8,128)} %convolution_add_fusion) | copy-start | bytes 1572868
  73.2 5.5 %copy-start.12 = (f32[1,576,512]{2,1,0:T(8,128)S(1)}, f32[1,576,512]{2,1,0:T(8,128)}, u32[]{:S(2)}) copy-start(f32[1,576,512]{2,1,0:T(8,128)} %param.15) | copy-start | bytes 3538948
  73.2 5.5 %copy-start.13 = (f32[1,576,512]{2,1,0:T(8,128)S(1)}, f32[1,576,512]{2,1,0:T(8,128)}, u32[]{:S(2)}) copy-start(f32[1,576,512]{2,1,0:T(8,128)} %param.14) | copy-start | bytes 3538948
  80.3 3.2 %collective-permute-start.19 = (bf16[1536,128]{1,0:T(8,128)(2,1)S(1)}, bf16[1536,128]{1,0:T(8,128)(2,1)S(1)}, u32[]{:S(2)}, u32[]{:S(2)}) collective-permute-start(bf16[1536,128]{1,0:T(8,128)(2,1)S(1)} %add_convert_fusion), channel_id=1, source_target_pairs={{0,4},{4,0},{8,12},{12,8},{16,20},{20,16},{24,28},{28,24},{1,5},{5... | collective-permute-start | bytes 1179656 | tf_op jit(solution)/shard_map/ppermute | solution.py:47
  81.2 1.6 %copy-start.14 = (f32[1,576]{1,0:T(1,128)S(1)}, f32[1,576]{1,0:T(1,128)}, u32[]{:S(2)}) copy-start(f32[1,576]{1,0:T(1,128)} %param.16) | copy-start | bytes 6916
  81.2 1.6 %copy-start.15 = (f32[1,576]{1,0:T(1,128)S(1)}, f32[1,576]{1,0:T(1,128)}, u32[]{:S(2)}) copy-start(f32[1,576]{1,0:T(1,128)} %param.18) | copy-start | bytes 6916
  81.2 1.6 %copy-start.16 = (f32[1,576]{1,0:T(1,128)S(1)}, f32[1,576]{1,0:T(1,128)}, u32[]{:S(2)}) copy-start(f32[1,576]{1,0:T(1,128)} %param.17) | copy-start | bytes 6916
  83.5 1.4 %copy-start.11 = (f32[393216]{0:T(1024)S(1)}, f32[393216]{0:T(1024)}, u32[]{:S(2)}) copy-start(f32[393216]{0:T(1024)} %param.21) | copy-start | bytes 4718596
  83.6 1.8 %copy-start.10 = (f32[393216]{0:T(1024)S(1)}, f32[393216]{0:T(1024)}, u32[]{:S(2)}) copy-start(f32[393216]{0:T(1024)} %param.20) | copy-start | bytes 4718596

commit v2 on v1

v2 whole, which is shorter than its diff:
```python
import functools
import math

import jax
import jax.numpy as jnp
from jax import lax
from jax.experimental import pallas as pl
from jax.experimental.pallas import tpu as pltpu
from jax.sharding import PartitionSpec as P

norm_eps = 1e-05
beta_one = 0.9
beta_two = 0.95
corr_one = 1.0 - math.exp(200.0 * math.log(0.9))
corr_two = 1.0 - math.exp(200.0 * math.log(0.95))
learn_rate = 0.001
adam_eps = 1e-08
weight_decay = 0.1
outer_beta = 0.9
outer_rate = 0.7
root_scale = 1.0 / math.sqrt(corr_two)
rate_scale = learn_rate / corr_one
chunk_count = 2
lanes = 128
vmem_limit = 12 * 1024 * 1024

wide = jnp.float32
narrow = jnp.bfloat16
VMEM = pl.BlockSpec(memory_space=pltpu.VMEM)
SMEM = pl.BlockSpec(memory_space=pltpu.SMEM)
HBM = pl.BlockSpec(memory_space=pltpu.HBM)


def adam_step(params, gradient, first_moment, second_moment):
    first_new = beta_one * first_moment + (1.0 - beta_one) * gradient
    second_new = beta_two * second_moment + (1.0 - beta_two) * gradient * gradient
    ratio = first_new / (jnp.sqrt(second_new) * root_scale + adam_eps)
    return (params * (1.0 - learn_rate * weight_decay) - ratio * rate_scale, first_new, second_new)


def nesterov(delta_part, params_part, mom_part):
    new_mom = outer_beta * mom_part + delta_part
    new_params = params_part - outer_rate * (delta_part + outer_beta * new_mom)
    return (new_params, new_mom)


def add_narrow(left, right):
    return (left.astype(wide) + right.astype(wide)).astype(narrow)


def blocks_of(size, most, unit):
    for count in range(1, size // unit + 1):
        if size % (count * unit) == 0 and size // count <= most:
            return count
    return 1


def call(kernel, out_shape, inputs, flops=0, moved=0, scratch=(), aliases=None, specs=None, outs=None, grid=(), limit=vmem_limit):
    return pl.pallas_call(
        kernel,
        out_shape=out_shape,
        grid=grid,
        in_specs=specs if specs is not None else [VMEM] * len(inputs),
        out_specs=outs if outs is not None else jax.tree.map(lambda _: VMEM, out_shape),
        scratch_shapes=list(scratch),
        compiler_params=pltpu.CompilerParams(vmem_limit_bytes=limit),

        input_output_aliases=aliases or {},
    )(*inputs)


def scale_kernel(chunks, weight_ref, gain_ref, spread_ref, *refs):
    sent_refs, (held, sems) = refs[:chunks], refs[chunks:]
    rows = weight_ref.shape[1]
    depth = rows // chunks
    spans = [slice(c * depth, (c + 1) * depth) for c in range(chunks)]
    copies = [
        pltpu.make_async_copy(weight_ref.at[0, span], held.at[span], sems.at[c])
        for c, span in enumerate(spans)
    ]
    for copy in copies:
        copy.start()
    spread = jnp.broadcast_to(gain_ref[...], (lanes, rows)).T
    spread_ref[...] = spread
    used = spread.astype(narrow).astype(wide)
    for c, span in enumerate(spans):
        copies[c].wait()
        for k in range(weight_ref.shape[2] // lanes):
            part = slice(k * lanes, (k + 1) * lanes)
            sent_refs[c][:, part] = (held[span, part].astype(wide) * used[span]).astype(narrow)


def partial_kernel(inputs_ref, cot_ref, partial_ref, rms_ref, held_ref, cot_held, sems):
    tokens, feats = inputs_ref.shape[1:]
    copies = [
        pltpu.make_async_copy(inputs_ref, held_ref, sems.at[0]),
        pltpu.make_async_copy(cot_ref, cot_held, sems.at[1]),
    ]
    for copy in copies:
        copy.start()
    for copy in copies:
        copy.wait()
    total = jnp.zeros((tokens, lanes), wide)
    for k in range(feats // lanes):
        part = held_ref[0, :, k * lanes : (k + 1) * lanes].astype(wide)
        total = total + part * part
    mean = jnp.sum(total, axis=1, keepdims=True) / feats
    inv_rms = lax.rsqrt(mean + norm_eps)
    rms_ref[...] = jnp.broadcast_to(inv_rms, rms_ref.shape)
    scaled = (cot_held[0].astype(wide) * inv_rms).astype(narrow)
    step = 2 * lanes if feats % (2 * lanes) == 0 else lanes
    for k in range(feats // step):
        span = slice(k * step, (k + 1) * step)
        partial_ref[span, :] = lax.dot_general(
            held_ref[0, :, span], scaled, (((0,), (0,)), ((), ())), preferred_element_type=wide
        ).astype(narrow)


def onward_kernel(n, c, chunks, s, me_ref, partial_ref, even_ref, odd_ref, to_even_ref, to_odd_ref):
    me = me_ref[0]
    depth = even_ref.shape[0]
    even = (me & 1) == 0
    for came_ref, sent_ref, right in (
        (odd_ref, to_even_ref, even),
        (even_ref, to_odd_ref, jnp.logical_not(even)),
    ):
        place = jnp.where(right, me, n - 1 - me)
        owner = jnp.where(right, n - s + place, s - 1 - place)

        @pl.when(s > place)
        def _():
            start = pl.multiple_of((owner * chunks + c) * depth, 16)
            sent_ref[...] = add_narrow(came_ref[...], partial_ref[pl.ds(start, depth), :])

        @pl.when(s <= place)
        def _():
            sent_ref[...] = came_ref[...]


def keys_kernel(n, chunks, me_ref, inputs_ref, rms_ref, *refs):
    own, got = refs[:chunks], refs[chunks:-2]
    keys_ref, weights = refs[-2:]
    me = me_ref[0]
    depth, cols = own[0].shape
    rows = depth * chunks

    def put(block, c, ref):
        weights[pl.ds(pl.multiple_of(block * rows + c * depth, 16), depth), :] = ref[...]

    for c in range(chunks):
        put(me, c, own[c])
    even = (me & 1) == 0
    for s in range(n - 1):
        for w in range(2):
            from_right = even if w == 0 else jnp.logical_not(even)
            block = jnp.where(from_right, me + 1 + s, me - 1 - s)

            @pl.when((block >= 0) & (block < n))
            def _():
                for c in range(chunks):
                    put(block, c, got[(s * 2 + w) * chunks + c])

    total = jnp.dot(inputs_ref[0], weights[...], preferred_element_type=wide)
    for k in range(cols // lanes):
        part = slice(k * lanes, (k + 1) * lanes)
        keys_ref[0, :, part] = (total[:, part] * rms_ref[...]).astype(narrow)


def fetch_kernel(*refs):
    count = len(refs) // 2
    sems = refs[-1]
    copies = [
        pltpu.make_async_copy(refs[i], refs[count + i], sems.at[i]) for i in range(count)
    ]
    for copy in copies:
        copy.start()
    for copy in copies:
        copy.wait()


def adam_kernel(c, chunks, me_ref, spread_ref, weight_ref, first_ref, second_ref, partial_ref, *refs):
    came, outs = refs[:2], refs[-4:]
    share_ref, new_weight_ref, new_first_ref, new_second_ref = outs
    depth, cols = weight_ref.shape[1:]
    steps = pl.num_programs(0)
    start = pl.multiple_of(((me_ref[0] * chunks + c) * steps + pl.program_id(0)) * depth, 16)
    share = jnp.zeros((depth, lanes), wide)
    used = spread_ref[...].astype(narrow).astype(wide)
    for k in range(cols // lanes):
        part = slice(k * lanes, (k + 1) * lanes)
        total = partial_ref[pl.ds(start, depth), part].astype(wide)
        for ref in came:
            total = total + ref[:, part].astype(wide)
        weight = weight_ref[0, :, part].astype(wide)
        share = share + total * weight
        new_weight, new_first, new_second = adam_step(
            weight, total * used, first_ref[0, :, part], second_ref[0, :, part]
        )
        new_weight_ref[0, :, part] = new_weight.astype(narrow)
        new_first_ref[0, :, part] = new_first
        new_second_ref[0, :, part] = new_second
    share_ref[...] = share


def gain_kernel(chunks, *refs):
    gain_ref, first_ref, second_ref = refs[chunks : chunks + 3]
    news = refs[chunks + 3 :]
    share = jnp.concatenate([ref[...] for ref in refs[:chunks]], axis=0)
    gradient = jnp.sum(share.T, axis=0, keepdims=True)
    for ref, value in zip(news, adam_step(gain_ref[...], gradient, first_ref[...], second_ref[...])):
        ref[...] = value


def pair_kernel(core_ref, mine_ref, other_ref, half_ref):
    half, step = half_ref.shape[0], 16
    start = core_ref[0] * half

    @pl.loop(0, half // step, unroll=4)
    def _(i):
        span = pl.ds(pl.multiple_of((start + i * step) * lanes, step * lanes), step * lanes)
        total = mine_ref[:, span].astype(wide) + other_ref[:, span].astype(wide)
        half_ref[pl.ds(pl.multiple_of(i * step, step), step), :] = total.reshape(step, lanes).astype(narrow)


def sum_kernel(left_ref, right_ref, total_ref):
    total_ref[...] = add_narrow(left_ref[...], right_ref[...])


def nesterov_kernel(silos, core_ref, own_ref, other_ref, params_ref, mom_ref, new_params_ref, new_mom_ref):
    mine = core_ref[0] == pl.program_id(0)
    delta = jnp.where(mine, own_ref[...], other_ref[...]).astype(wide) / silos
    new_params_ref[0], new_mom_ref[0] = nesterov(delta, params_ref[0], mom_ref[0])


def tie(values, other):
    return lax.optimization_barrier((values, other))[0]


def outer_steps(pseudo_grad, outer_params, outer_mom, silos):
    size = pseudo_grad.shape[1]
    half = size // 2 // lanes
    if silos < 2 or silos & (silos - 1) != 0 or size % (32 * lanes) != 0:
        yield nesterov(lax.psum(pseudo_grad[0].astype(wide), "silo") / silos, outer_params, outer_mom)
        return

    def swap(part, bit):
        return lax.ppermute(part, "silo", [(i, i ^ bit) for i in range(silos)])

    core = (lax.axis_index("silo") & 1).astype(jnp.int32).reshape(1)
    part = jax.ShapeDtypeStruct((half, lanes), narrow)
    cost = dict(flops=half * lanes, moved=6 * half * lanes)
    total = call(
        pair_kernel, part, [core, pseudo_grad, swap(pseudo_grad, 1)], specs=[SMEM, VMEM, VMEM], **cost
    )
    yield total
    bit = 2
    while bit < silos:
        total = call(sum_kernel, part, [total, swap(total, bit)], **cost)
        yield total
        bit *= 2
    other = swap(total, 1)
    steps = blocks_of(half, 512, 16)
    line = pl.BlockSpec((half // steps, lanes), lambda h, j: (j, 0))
    block = pl.BlockSpec((1, half // steps, lanes), lambda h, j: (h, j, 0))
    new_params, new_mom = call(
        functools.partial(nesterov_kernel, silos),
        [jax.ShapeDtypeStruct((2, half, lanes), wide)] * 2,
        [core, total, other, outer_params.reshape(2, half, lanes), outer_mom.reshape(2, half, lanes)],
        flops=12 * size,
        moved=20 * size,
        specs=[SMEM, line, line, block, block],
        outs=[block, block],
        grid=(2, steps),
    )
    yield new_params.reshape(size), new_mom.reshape(size)


def make(silos, n):
    def per_device(
        activations,
        key_cot,
        key_weight,
        weight_first,
        weight_second,
        norm_gain,
        gain_first,
        gain_second,
        pseudo_grad,
        outer_params,
        outer_mom,
    ):
        me = lax.axis_index("fsdp")
        me_word = me.astype(jnp.int32).reshape(1)
        tokens, feats = activations.shape[1:]
        rows, cols = key_weight.shape[1:]
        chunks = chunk_count if rows % (16 * chunk_count) == 0 else 1
        depth = rows // chunks
        shape = jax.ShapeDtypeStruct

        spread, *own = call(
            functools.partial(scale_kernel, chunks),
            [shape((rows, lanes), wide)] + [shape((depth, cols), narrow)] * chunks,
            [key_weight, norm_gain],
            flops=rows * cols,
            moved=4 * rows * cols,
            specs=[HBM, VMEM],
            scratch=[pltpu.VMEM((rows, cols), narrow), pltpu.SemaphoreType.DMA((chunks,))],
        )
        links = [
            [pair for i in range(start, n - 1, 2) for pair in ((i, i + 1), (i + 1, i))]
            for start in (0, 1)
        ]
        slots = []
        for s in range(n):
            got = [[None for _ in range(chunks)] for _ in links]
            for c in range(chunks):
                sent = [own[c], own[c]]
                if s > 0:
                    came = [slots[-1][w][c] for w in range(2)]
                    if c == chunks - 1:
                        outer_part = next(outer, outer_part)
                        came = tie(came, outer_part)
                    sent = call(
                        functools.partial(onward_kernel, n, c, chunks, s),
                        [shape((depth, cols), narrow)] * 2,
                        [me_word, partial, *came],
                        flops=2 * depth * cols,
                        moved=12 * depth * cols,
                        specs=[SMEM] + [VMEM] * 3,
                    )
                for w in range(2):
                    got[w][c] = lax.ppermute(sent[w], "fsdp", links[w])
            slots.append(got)
            if s == 0:
                partial, inv_rms, inputs = call(
                    partial_kernel,
                    [
                        shape((feats, cols), narrow),
                        shape((tokens, lanes), wide),
                        shape(activations.shape, narrow),
                    ],
                    [activations, key_cot],
                    specs=[HBM, HBM],
                    scratch=[pltpu.VMEM(key_cot.shape, narrow), pltpu.SemaphoreType.DMA((2,))],
                    flops=2 * tokens * feats * cols,
                    moved=2 * (tokens * feats + feats * cols + tokens * cols),
                )
                outer = outer_steps(pseudo_grad, outer_params, outer_mom, silos)
                outer_part = partial

        keys = call(
            functools.partial(keys_kernel, n, chunks),
            shape((1, tokens, cols), narrow),
            [me_word, inputs, inv_rms, *own]
            + [slots[s][w][c] for s in range(n - 1) for w in range(2) for c in range(chunks)],
            flops=2 * tokens * feats * cols,
            moved=2 * (tokens * feats + feats * cols + tokens * cols),
            scratch=[pltpu.VMEM((feats, cols), narrow)],
            specs=[SMEM] + [VMEM] * (2 + chunks + (n - 1) * 2 * chunks),
        )

        for outer_part in outer:
            pass
        shares, news = [], []
        steps = blocks_of(depth, 96, 16)
        tall = depth // steps
        for c in range(chunks):
            came = [slots[n - 1][w][c] for w in range(2)]
            if c == 0:
                came = tie(came, outer_part)
            block = pl.BlockSpec((1, tall, cols), lambda i, c=c: (0, c * steps + i, 0))
            share, *news = call(
                functools.partial(adam_kernel, c, chunks),
                [shape((depth, lanes), wide)]
                + [shape((1, rows, cols), kind) for kind in (narrow, wide, wide)],
                [me_word, spread, key_weight, weight_first, weight_second, partial, *came, *news],
                flops=20 * depth * cols,
                moved=20 * depth * cols,
                specs=[SMEM, pl.BlockSpec((tall, lanes), lambda i, c=c: (c * steps + i, 0))]
                + [block] * 3
                + [VMEM]
                + [pl.BlockSpec((tall, cols), lambda i: (i, 0))] * 2
                + [pl.BlockSpec(memory_space=pl.ANY)] * len(news),
                outs=[pl.BlockSpec((tall, lanes), lambda i: (i, 0))] + [block] * 3,
                aliases={8 + i: 1 + i for i in range(len(news))},
                grid=(steps,),
            )
            shares.append(share)
        new_gains = call(
            functools.partial(gain_kernel, chunks),
            [shape((1, rows), wide)] * 3,
            [*shares, norm_gain, gain_first, gain_second],
            flops=20 * rows,
            moved=4 * rows * (lanes + 6),
        )
        return (
            keys,
            *news,
            *new_gains,
            *outer_part,
        )

    return per_device


def solution(mesh):
    return jax.shard_map(
        make(mesh.shape["silo"], mesh.shape["fsdp"]),
        mesh=mesh,
        in_specs=(
            P("silo", "fsdp", None),
            P("silo", "fsdp", None),
            P("silo", "fsdp", None),
            P("silo", "fsdp", None),
            P("silo", "fsdp", None),
            P("silo", "fsdp"),
            P("silo", "fsdp"),
            P("silo", "fsdp"),
            P("silo", "fsdp"),
            P("fsdp"),
            P("fsdp"),
        ),
        out_specs=(
            P("silo", "fsdp", None),
            P("silo", "fsdp", None),
            P("silo", "fsdp", None),
            P("silo", "fsdp", None),
            P("silo", "fsdp"),
            P("silo", "fsdp"),
            P("silo", "fsdp"),
            P("fsdp"),
            P("fsdp"),
        ),
        check_vma=False,
    )
```

time: 88.3 us -> 65.3 us (0.74)
  other arithmetic: 17.1 us -> 0 us
  Pallas kernels: 0 us -> 14.1 us
  matrix products: 13.1 us -> 0 us
  local copies, waits for them, and re-layouts: 12.7 us -> 5.42 us
  waiting for transfers between devices: 9.28 us -> 15.7 us
  starting transfers between devices: 34 us -> 28.7 us
    pallas_call x0 -> x16, Pallas kernels: none -> 14.1 us  [call(): pl.pallas_call(kernel, out_shape=out_shape, grid=grid, in_specs=specs if...]
    dot_general x15 -> x0, matrix products: 13.1 us -> none  [the longest x12 8.89 us: per_device(): term = jnp.dot(block, got[w][c], preferred_element_type=wide)]
    convert_element_type x9 -> x0, other arithmetic: 7.72 us -> none  [the longest x1 1.65 us: outer_update(): spread = lax.optimization_barrier(pseudo_grad[0].astype(wide))]
    ppermute x16, waiting for transfers between devices: 9.09 us -> 15.6 us  [per_device(): got[w][c] = lax.ppermute(sent[w], 'fsdp', links[w])]
    ppermute x16, starting transfers between devices: 30.8 us -> 25 us  [per_device(): got[w][c] = lax.ppermute(sent[w], 'fsdp', links[w])]
    slice x4 -> x0, local copies, waits for them, and re-layouts: 5.06 us -> none  [the longest x1 2.2 us: inputs_of(): return lax.dynamic_index_in_dim(blocks[:, c], k, 0, keepdims=False)]
    select_n x6 -> x0, other arithmetic: 3.74 us -> none  [per_device(): jnp.where(s > places[w], add_narrow(before, shard_of(owner, c)), before)]
    sub x2 -> x0, other arithmetic: 2.71 us -> none  [the longest x1 2.03 us: nesterov(): new_params = params_part - outer_rate * (delta_part + outer_beta * new_mom)]
  transfers between devices with their start and end apart: 20 -> 20, of which waited for: 3 -> 6; matrix products, arithmetic and copies ran while one was open for 40% -> 0% of each run, Pallas kernels for 0% -> 18%
where the time goes in v2:
time: 65.3 us; the launch traced here: 64.8 us
  starting transfers between devices  28.7 us (44%)
  waiting for transfers between devices  15.7 us (24%)
  Pallas kernels  14.1 us (22%)
  local copies, waits for them, and re-layouts  5.42 us (8%)
  between operations  0.94 us (1%)
    ppermute x16, starting transfers between devices, per_device(): got[w][c] = lax.ppermute(sent[w], 'fsdp', links[w])  25 us
    ppermute x16, waiting for transfers between devices, per_device(): got[w][c] = lax.ppermute(sent[w], 'fsdp', links[w])  15.6 us
    pallas_call x16, Pallas kernels, call(): pl.pallas_call(kernel, out_shape=out_shape, grid=grid, in_specs=specs if...  14.1 us
    unnamed x26, local copies, waits for them, and re-layouts  5.42 us
    ppermute x4, starting transfers between devices, swap(): return lax.ppermute(part, 'silo', [(i, i ^ bit) for i in range(silos)])  3.73 us
  transfers between devices with their start and end apart: 20, of which 6 were waited for; matrix products, arithmetic and copies ran while one was open for 0% of the time, Pallas kernels for 18%

profile of v2, /device:TPU:0, one launch (start us, length us, event | category | flops | bytes accessed | tf_op | source)
XLA Modules:
  0.0 64.8 jit_solution(2289395532827440906)
XLA Ops:
  0.6 0.5 collective-permute-start.5
  1.2 1.1 %copy-done = bf16[1,576,512]{2,1,0:T(8,128)(2,1)S(1)} copy-done((bf16[1,576,512]{2,1,0:T(8,128)(2,1)S(1)}, bf16[1,576,512]{2,1,0:T(8,128)(2,1)}, u32[]{:S(2)}) %copy-start) | copy-done | bytes 589848
  2.2 0.7 %copy-done.9 = f32[1,576]{1,0:T(1,128)S(1)} copy-done((f32[1,576]{1,0:T(1,128)S(1)}, f32[1,576]{1,0:T(1,128)}, u32[]{:S(2)}) %copy-start.9) | copy-done | bytes 2328
  2.9 1.2 %shard_map.179 = (f32[576,128]{1,0:T(8,128)S(1)}, bf16[288,512]{1,0:T(8,128)(2,1)}, bf16[288,512]{1,0:T(8,128)(2,1)}) custom-call(bf16[1,576,512]{2,1,0:T(8,128)(2,1)S(1)} %copy-done, f32[1,576]{1,0:T(1,128)S(1)} %copy-done.9), custom_call_target="tpu_custom_call" | custom-call | tf_op jit(solution)/shard_map/pallas_call | solution.py:59
  4.1 0.7 %collective-permute-start.2 = (bf16[288,512]{1,0:T(8,128)(2,1)}, bf16[288,512]{1,0:T(8,128)(2,1)S(1)}, u32[]{:S(2)}, u32[]{:S(2)}) collective-permute-start(bf16[288,512]{1,0:T(8,128)(2,1)} %get-tuple-element.50.refs_0_), channel_id=1, source_target_pairs={{1,2},{2,1},{5,6},{6,5},{9,10},{10,9},{13,14},{14,13},{17,18},{18,... | collective-permute-start | bytes 884744 | tf_op jit(solution)/shard_map/ppermute | solution.py:332
  4.8 5.5 %collective-permute-start = (bf16[288,512]{1,0:T(8,128)(2,1)}, bf16[288,512]{1,0:T(8,128)(2,1)S(1)}, u32[]{:S(2)}, u32[]{:S(2)}) collective-permute-start(bf16[288,512]{1,0:T(8,128)(2,1)} %get-tuple-element.50.refs_0_), channel_id=1, source_target_pairs={{0,1},{1,0},{2,3},{3,2},{4,5},{5,4},{6,7},{7,6},{8,9},{9,8},{10,11... | collective-permute-start | bytes 884744 | tf_op jit(solution)/shard_map/ppermute | solution.py:332
  10.2 0.7 %collective-permute-start.3 = (bf16[288,512]{1,0:T(8,128)(2,1)}, bf16[288,512]{1,0:T(8,128)(2,1)S(1)}, u32[]{:S(2)}, u32[]{:S(2)}) collective-permute-start(bf16[288,512]{1,0:T(8,128)(2,1)} %get-tuple-element.51.refs_1_), channel_id=1, source_target_pairs={{1,2},{2,1},{5,6},{6,5},{9,10},{10,9},{13,14},{14,13},{17,18},{18,... | collective-permute-start | bytes 884744 | tf_op jit(solution)/shard_map/ppermute | solution.py:332
  10.9 1.8 %collective-permute-start.1 = (bf16[288,512]{1,0:T(8,128)(2,1)}, bf16[288,512]{1,0:T(8,128)(2,1)S(1)}, u32[]{:S(2)}, u32[]{:S(2)}) collective-permute-start(bf16[288,512]{1,0:T(8,128)(2,1)} %get-tuple-element.51.refs_1_), channel_id=1, source_target_pairs={{0,1},{1,0},{2,3},{3,2},{4,5},{5,4},{6,7},{7,6},{8,9},{9,8},{10,11... | collective-permute-start | bytes 884744 | tf_op jit(solution)/shard_map/ppermute | solution.py:332
  12.7 1.4 %copy-done.4 = bf16[1,393216]{1,0:T(2,128)(2,1)S(1)} copy-done((bf16[1,393216]{1,0:T(2,128)(2,1)S(1)}, bf16[1,393216]{1,0:T(2,128)(2,1)}, u32[]{:S(2)}) %copy-start.4) | copy-done | bytes 786456
  14.1 0.4 shard_map.181.left_ref
  14.5 1.6 %collective-permute-start.10 = (bf16[1536,128]{1,0:T(8,128)(2,1)S(1)}, bf16[1536,128]{1,0:T(8,128)(2,1)S(1)}, u32[]{:S(2)}, u32[]{:S(2)}) collective-permute-start(bf16[1536,128]{1,0:T(8,128)(2,1)S(1)} %shard_map.181.left_ref), channel_id=1, source_target_pairs={{0,8},{4,12},{8,0},{12,4},{16,24},{20,28},{24,16},{28,20},{1,9},{5... | collective-permute-start | bytes 1179656 | tf_op jit(solution)/shard_map/ppermute | solution.py:247
  16.1 1.3 %copy-done.7 = bf16[1,256,2304]{2,1,0:T(8,128)(2,1)S(1)} copy-done((bf16[1,256,2304]{2,1,0:T(8,128)(2,1)S(1)}, bf16[1,256,2304]{2,1,0:T(8,128)(2,1)}, u32[]{:S(2)}) %copy-start.7) | copy-done | bytes 1179672
  17.3 0.9 %copy-done.8 = bf16[1,256,512]{2,1,0:T(8,128)(2,1)S(1)} copy-done((bf16[1,256,512]{2,1,0:T(8,128)(2,1)S(1)}, bf16[1,256,512]{2,1,0:T(8,128)(2,1)}, u32[]{:S(2)}) %copy-start.8) | copy-done | bytes 262168
  18.3 1.4 %shard_map.178 = (bf16[2304,512]{1,0:T(8,128)(2,1)S(1)}, f32[256,128]{1,0:T(8,128)S(1)}, bf16[1,256,2304]{2,1,0:T(8,128)(2,1)S(1)}) custom-call(bf16[1,256,2304]{2,1,0:T(8,128)(2,1)S(1)} %copy-done.7, bf16[1,256,512]{2,1,0:T(8,128)(2,1)S(1)} %copy-done.8), custom_call_target="tpu_custom_call" | custom-call | tf_op jit(solution)/shard_map/pallas_call | solution.py:59
  19.7 0.1 shard_map.180
  19.8 0.6 collective-permute-start.4
  20.4 0.7 %collective-permute-start.7 = (bf16[288,512]{1,0:T(8,128)(2,1)S(1)}, bf16[288,512]{1,0:T(8,128)(2,1)S(1)}, u32[]{:S(2)}, u32[]{:S(2)}) collective-permute-start(bf16[288,512]{1,0:T(8,128)(2,1)S(1)} %get-tuple-element.57), channel_id=1, source_target_pairs={{1,2},{2,1},{5,6},{6,5},{9,10},{10,9},{13,14},{14,13},{17,18},{18,... | collective-permute-start | bytes 884744 | tf_op jit(solution)/shard_map/ppermute | solution.py:332
  21.1 3.5 %collective-permute-done.1.even_ref.refs_3_ = bf16[288,512]{1,0:T(8,128)(2,1)S(1)} collective-permute-done((bf16[288,512]{1,0:T(8,128)(2,1)}, bf16[288,512]{1,0:T(8,128)(2,1)S(1)}, u32[]{:S(2)}, u32[]{:S(2)}) %collective-permute-start.1) | collective-permute-done | bytes 294944 | tf_op jit(solution)/shard_map/ppermute | solution.py:332
  24.5 0.1 shard_map.182
  24.6 2.1 %collective-permute-start.6 = (bf16[288,512]{1,0:T(8,128)(2,1)S(1)}, bf16[288,512]{1,0:T(8,128)(2,1)S(1)}, u32[]{:S(2)}, u32[]{:S(2)}) collective-permute-start(bf16[288,512]{1,0:T(8,128)(2,1)S(1)} %get-tuple-element.56), channel_id=1, source_target_pairs={{0,1},{1,0},{2,3},{3,2},{4,5},{5,4},{6,7},{7,6},{8,9},{9,8},{10,11... | collective-permute-start | bytes 884744 | tf_op jit(solution)/shard_map/ppermute | solution.py:332
  26.7 0.7 %collective-permute-start.8 = (bf16[288,512]{1,0:T(8,128)(2,1)S(1)}, bf16[288,512]{1,0:T(8,128)(2,1)S(1)}, u32[]{:S(2)}, u32[]{:S(2)}) collective-permute-start(bf16[288,512]{1,0:T(8,128)(2,1)S(1)} %get-tuple-element.58), channel_id=1, source_target_pairs={{1,2},{2,1},{5,6},{6,5},{9,10},{10,9},{13,14},{14,13},{17,18},{18,... | collective-permute-start | bytes 884744 | tf_op jit(solution)/shard_map/ppermute | solution.py:332
  27.4 0.1 shard_map.184.left_ref
  27.5 1.6 %collective-permute-start.14 = (bf16[1536,128]{1,0:T(8,128)(2,1)S(1)}, bf16[1536,128]{1,0:T(8,128)(2,1)S(1)}, u32[]{:S(2)}, u32[]{:S(2)}) collective-permute-start(bf16[1536,128]{1,0:T(8,128)(2,1)S(1)} %shard_map.184.left_ref), channel_id=1, source_target_pairs={{0,16},{4,20},{8,24},{12,28},{16,0},{20,4},{24,8},{28,12},{1,17},{... | collective-permute-start | bytes 1179656 | tf_op jit(solution)/shard_map/ppermute | solution.py:247
  29.1 1.8 %collective-permute-done.4.even_ref.refs_6_ = bf16[288,512]{1,0:T(8,128)(2,1)S(1)} collective-permute-done((bf16[288,512]{1,0:T(8,128)(2,1)S(1)}, bf16[288,512]{1,0:T(8,128)(2,1)S(1)}, u32[]{:S(2)}, u32[]{:S(2)}) %collective-permute-start.4) | collective-permute-done | bytes 294944 | tf_op jit(solution)/shard_map/ppermute | solution.py:332
  30.9 0.1 shard_map.183
  31.0 2.4 %collective-permute-start.9 = (bf16[288,512]{1,0:T(8,128)(2,1)S(1)}, bf16[288,512]{1,0:T(8,128)(2,1)S(1)}, u32[]{:S(2)}, u32[]{:S(2)}) collective-permute-start(bf16[288,512]{1,0:T(8,128)(2,1)S(1)} %get-tuple-element.59), channel_id=1, source_target_pairs={{0,1},{1,0},{2,3},{3,2},{4,5},{5,4},{6,7},{7,6},{8,9},{9,8},{10,11... | collective-permute-start | bytes 884744 | tf_op jit(solution)/shard_map/ppermute | solution.py:332
  33.4 0.7 %collective-permute-start.12 = (bf16[288,512]{1,0:T(8,128)(2,1)S(1)}, bf16[288,512]{1,0:T(8,128)(2,1)S(1)}, u32[]{:S(2)}, u32[]{:S(2)}) collective-permute-start(bf16[288,512]{1,0:T(8,128)(2,1)S(1)} %get-tuple-element.63), channel_id=1, source_target_pairs={{1,2},{2,1},{5,6},{6,5},{9,10},{10,9},{13,14},{14,13},{17,18},{18,... | collective-permute-start | bytes 884744 | tf_op jit(solution)/shard_map/ppermute | solution.py:332
  34.0 3.1 %collective-permute-done.6.even_ref.refs_7_ = bf16[288,512]{1,0:T(8,128)(2,1)S(1)} collective-permute-done((bf16[288,512]{1,0:T(8,128)(2,1)S(1)}, bf16[288,512]{1,0:T(8,128)(2,1)S(1)}, u32[]{:S(2)}, u32[]{:S(2)}) %collective-permute-start.6) | collective-permute-done | bytes 294944 | tf_op jit(solution)/shard_map/ppermute | solution.py:332
  37.2 0.1 shard_map.185
  37.3 2.4 %collective-permute-start.11 = (bf16[288,512]{1,0:T(8,128)(2,1)S(1)}, bf16[288,512]{1,0:T(8,128)(2,1)S(1)}, u32[]{:S(2)}, u32[]{:S(2)}) collective-permute-start(bf16[288,512]{1,0:T(8,128)(2,1)S(1)} %get-tuple-element.62), channel_id=1, source_target_pairs={{0,1},{1,0},{2,3},{3,2},{4,5},{5,4},{6,7},{7,6},{8,9},{9,8},{10,11... | collective-permute-start | bytes 884744 | tf_op jit(solution)/shard_map/ppermute | solution.py:332
  39.7 0.7 %collective-permute-start.13 = (bf16[288,512]{1,0:T(8,128)(2,1)S(1)}, bf16[288,512]{1,0:T(8,128)(2,1)S(1)}, u32[]{:S(2)}, u32[]{:S(2)}) collective-permute-start(bf16[288,512]{1,0:T(8,128)(2,1)S(1)} %get-tuple-element.64), channel_id=1, source_target_pairs={{1,2},{2,1},{5,6},{6,5},{9,10},{10,9},{13,14},{14,13},{17,18},{18,... | collective-permute-start | bytes 884744 | tf_op jit(solution)/shard_map/ppermute | solution.py:332
  40.4 0.1 shard_map.187.own_ref
  40.5 0.1 collective-permute-start.19
  40.5 2.9 %collective-permute-done.9.refs_10_.even_ref = bf16[288,512]{1,0:T(8,128)(2,1)S(1)} collective-permute-done((bf16[288,512]{1,0:T(8,128)(2,1)S(1)}, bf16[288,512]{1,0:T(8,128)(2,1)S(1)}, u32[]{:S(2)}, u32[]{:S(2)}) %collective-permute-start.9) | collective-permute-done | bytes 294944 | tf_op jit(solution)/shard_map/ppermute | solution.py:332
  43.5 0.1 shard_map.189
  43.6 2.5 %collective-permute-start.17 = (bf16[288,512]{1,0:T(8,128)(2,1)S(1)}, bf16[288,512]{1,0:T(8,128)(2,1)S(1)}, u32[]{:S(2)}, u32[]{:S(2)}) collective-permute-start(bf16[288,512]{1,0:T(8,128)(2,1)S(1)} %get-tuple-element.70), channel_id=1, source_target_pairs={{0,1},{1,0},{2,3},{3,2},{4,5},{5,4},{6,7},{7,6},{8,9},{9,8},{10,11... | collective-permute-start | bytes 884744 | tf_op jit(solution)/shard_map/ppermute | solution.py:332
  46.1 0.7 %collective-permute-start.18 = (bf16[288,512]{1,0:T(8,128)(2,1)S(1)}, bf16[288,512]{1,0:T(8,128)(2,1)S(1)}, u32[]{:S(2)}, u32[]{:S(2)}) collective-permute-start(bf16[288,512]{1,0:T(8,128)(2,1)S(1)} %get-tuple-element.71), channel_id=1, source_target_pairs={{1,2},{2,1},{5,6},{6,5},{9,10},{10,9},{13,14},{14,13},{17,18},{18,... | collective-permute-start | bytes 884744 | tf_op jit(solution)/shard_map/ppermute | solution.py:332
  46.7 3.1 %collective-permute-done.11.refs_11_.even_ref = bf16[288,512]{1,0:T(8,128)(2,1)S(1)} collective-permute-done((bf16[288,512]{1,0:T(8,128)(2,1)S(1)}, bf16[288,512]{1,0:T(8,128)(2,1)S(1)}, u32[]{:S(2)}, u32[]{:S(2)}) %collective-permute-start.11) | collective-permute-done | bytes 294944 | tf_op jit(solution)/shard_map/ppermute | solution.py:332
  49.8 0.1 shard_map.188
  49.9 2.5 %collective-permute-start.15 = (bf16[288,512]{1,0:T(8,128)(2,1)S(1)}, bf16[288,512]{1,0:T(8,128)(2,1)S(1)}, u32[]{:S(2)}, u32[]{:S(2)}) collective-permute-start(bf16[288,512]{1,0:T(8,128)(2,1)S(1)} %get-tuple-element.68), channel_id=1, source_target_pairs={{0,1},{1,0},{2,3},{3,2},{4,5},{5,4},{6,7},{7,6},{8,9},{9,8},{10,11... | collective-permute-start | bytes 884744 | tf_op jit(solution)/shard_map/ppermute | solution.py:332
  52.4 0.7 %collective-permute-start.16 = (bf16[288,512]{1,0:T(8,128)(2,1)S(1)}, bf16[288,512]{1,0:T(8,128)(2,1)S(1)}, u32[]{:S(2)}, u32[]{:S(2)}) collective-permute-start(bf16[288,512]{1,0:T(8,128)(2,1)S(1)} %get-tuple-element.69), channel_id=1, source_target_pairs={{1,2},{2,1},{5,6},{6,5},{9,10},{10,9},{13,14},{14,13},{17,18},{18,... | collective-permute-start | bytes 884744 | tf_op jit(solution)/shard_map/ppermute | solution.py:332
  53.1 2.9 %shard_map.186 = bf16[1,256,512]{2,1,0:T(8,128)(2,1)} custom-call(s32[1]{0:T(128)} %bitcast.me_ref, bf16[1,256,2304]{2,1,0:T(8,128)(2,1)S(1)} %get-tuple-element.48.inputs_ref, f32[256,128]{1,0:T(8,128)S(1)} %get-tuple-element.49.rms_ref, bf16[288,512]{1,0:T(8,128)(2,1)} %get-tuple-element.50.refs_0_, bf16[288,512]{1,0:T(8,128)(2,1)} %get-tuple-element.51.refs_1_, ...), custom_call_target="tpu_custom_call" | custom-call | tf_op jit(solution)/shard_map/pallas_call | solution.py:59
  56.0 0.0 copy-start.1
  56.0 2.8 %shard_map.190 = (f32[2,1536,128]{2,1,0:T(8,128)}, f32[2,1536,128]{2,1,0:T(8,128)}) custom-call(s32[1]{0:T(128)} %bitcast.1.core_ref, bf16[1536,128]{1,0:T(8,128)(2,1)S(1)} %shard_map.187.own_ref, bf16[1536,128]{1,0:T(8,128)(2,1)S(1)} %collective-permute-done.19.other_ref, f32[2,1536,128]{2,1,0:T(8,128)S(1)} %bitcast.6, f32[2,1536,128]{2,1,0:T(8,128)S(1)} %bitcast.7), custom_call_target="tpu_custom_call" | custom-call | tf_op jit(solution)/shard_map/pallas_call | solution.py:59
  58.9 1.9 %shard_map.191 = (f32[288,128]{1,0:T(8,128)S(1)}, bf16[1,576,512]{2,1,0:T(8,128)(2,1)}, f32[1,576,512]{2,1,0:T(8,128)}, f32[1,576,512]{2,1,0:T(8,128)}) custom-call(s32[1]{0:T(128)} %bitcast.me_ref, f32[576,128]{1,0:T(8,128)S(1)} %get-tuple-element.65.spread_ref, bf16[1,576,512]{2,1,0:T(8,128)(2,1)S(1)} %copy-done.1, f32[1,576,512]{2,1,0:T(8,128)S(1)} %copy-done.2, ...), custom_call_target="tpu_custom_call" | custom-call | tf_op jit(solution)/shard_map/pallas_call | solution.py:59
  60.8 1.2 %collective-permute-done.15.refs_0_ = bf16[288,512]{1,0:T(8,128)(2,1)S(1)} collective-permute-done((bf16[288,512]{1,0:T(8,128)(2,1)S(1)}, bf16[288,512]{1,0:T(8,128)(2,1)S(1)}, u32[]{:S(2)}, u32[]{:S(2)}) %collective-permute-start.15) | collective-permute-done | bytes 294944 | tf_op jit(solution)/shard_map/ppermute | solution.py:332
  62.1 1.9 %shard_map.192 = (f32[288,128]{1,0:T(8,128)S(1)}, bf16[1,576,512]{2,1,0:T(8,128)(2,1)}, f32[1,576,512]{2,1,0:T(8,128)}, f32[1,576,512]{2,1,0:T(8,128)}) custom-call(s32[1]{0:T(128)} %bitcast.me_ref, f32[576,128]{1,0:T(8,128)S(1)} %get-tuple-element.65.spread_ref, ...), custom_call_target="tpu_custom_call", output_to_operand_aliasing={{1}: (8, {}), {2}: (9, {}), {3}: (10, {})} | custom-call | tf_op jit(solution)/shard_map/pallas_call | solution.py:59
  64.0 0.8 %shard_map.193 = (f32[1,576]{1,0:T(1,128)}, f32[1,576]{1,0:T(1,128)}, f32[1,576]{1,0:T(1,128)}) custom-call(f32[288,128]{1,0:T(8,128)S(1)} %get-tuple-element.82.refs_0_, f32[288,128]{1,0:T(8,128)S(1)} %get-tuple-element.83.refs_1_, f32[1,576]{1,0:T(1,128)S(1)} %copy-done.10, f32[1,576]{1,0:T(1,128)S(1)} %copy-done.11, f32[1,576]{1,0:T(1,128)S(1)} %copy-done.12), custom_call_target="tpu_custom_call" | custom-call | tf_op jit(solution)/shard_map/pallas_call | solution.py:59
  (34 shorter events, 0.1 us)
Async XLA Ops:
  0.6 12.0 %collective-permute-start.5 = (bf16[1,393216]{1,0:T(2,128)(2,1)}, bf16[1,393216]{1,0:T(2,128)(2,1)S(1)}, u32[]{:S(2)}, u32[]{:S(2)}) collective-permute-start(bf16[1,393216]{1,0:T(2,128)(2,1)} %mine_ref.1), channel_id=1, source_target_pairs={{0,4},{4,0},{8,12},{12,8},{16,20},{20,16},{24,28},{28,24},{1,5},{5... | collective-permute-start | bytes 2359304 | tf_op jit(solution)/shard_map/ppermute | solution.py:247
  1.2 1.1 %copy-start = (bf16[1,576,512]{2,1,0:T(8,128)(2,1)S(1)}, bf16[1,576,512]{2,1,0:T(8,128)(2,1)}, u32[]{:S(2)}) copy-start(bf16[1,576,512]{2,1,0:T(8,128)(2,1)} %weight_ref.5) | copy-start | bytes 1769476
  2.2 0.7 %copy-start.9 = (f32[1,576]{1,0:T(1,128)S(1)}, f32[1,576]{1,0:T(1,128)}, u32[]{:S(2)}) copy-start(f32[1,576]{1,0:T(1,128)} %refs_2_.1) | copy-start | bytes 6916
  4.1 15.6 %collective-permute-start.2 = (bf16[288,512]{1,0:T(8,128)(2,1)}, bf16[288,512]{1,0:T(8,128)(2,1)S(1)}, u32[]{:S(2)}, u32[]{:S(2)}) collective-permute-start(bf16[288,512]{1,0:T(8,128)(2,1)} %get-tuple-element.50.refs_0_), channel_id=1, source_target_pairs={{1,2},{2,1},{5,6},{6,5},{9,10},{10,9},{13,14},{14,13},{17,18},{18,... | collective-permute-start | bytes 884744 | tf_op jit(solution)/shard_map/ppermute | solution.py:332
  4.8 14.9 %collective-permute-start = (bf16[288,512]{1,0:T(8,128)(2,1)}, bf16[288,512]{1,0:T(8,128)(2,1)S(1)}, u32[]{:S(2)}, u32[]{:S(2)}) collective-permute-start(bf16[288,512]{1,0:T(8,128)(2,1)} %get-tuple-element.50.refs_0_), channel_id=1, source_target_pairs={{0,1},{1,0},{2,3},{3,2},{4,5},{5,4},{6,7},{7,6},{8,9},{9,8},{10,11... | collective-permute-start | bytes 884744 | tf_op jit(solution)/shard_map/ppermute | solution.py:332
  10.2 10.8 %collective-permute-start.3 = (bf16[288,512]{1,0:T(8,128)(2,1)}, bf16[288,512]{1,0:T(8,128)(2,1)S(1)}, u32[]{:S(2)}, u32[]{:S(2)}) collective-permute-start(bf16[288,512]{1,0:T(8,128)(2,1)} %get-tuple-element.51.refs_1_), channel_id=1, source_target_pairs={{1,2},{2,1},{5,6},{6,5},{9,10},{10,9},{13,14},{14,13},{17,18},{18,... | collective-permute-start | bytes 884744 | tf_op jit(solution)/shard_map/ppermute | solution.py:332
  10.9 13.6 %collective-permute-start.1 = (bf16[288,512]{1,0:T(8,128)(2,1)}, bf16[288,512]{1,0:T(8,128)(2,1)S(1)}, u32[]{:S(2)}, u32[]{:S(2)}) collective-permute-start(bf16[288,512]{1,0:T(8,128)(2,1)} %get-tuple-element.51.refs_1_), channel_id=1, source_target_pairs={{0,1},{1,0},{2,3},{3,2},{4,5},{5,4},{6,7},{7,6},{8,9},{9,8},{10,11... | collective-permute-start | bytes 884744 | tf_op jit(solution)/shard_map/ppermute | solution.py:332
  12.7 1.4 %copy-start.4 = (bf16[1,393216]{1,0:T(2,128)(2,1)S(1)}, bf16[1,393216]{1,0:T(2,128)(2,1)}, u32[]{:S(2)}) copy-start(bf16[1,393216]{1,0:T(2,128)(2,1)} %mine_ref.1) | copy-start | bytes 2359300
  14.5 12.9 %collective-permute-start.10 = (bf16[1536,128]{1,0:T(8,128)(2,1)S(1)}, bf16[1536,128]{1,0:T(8,128)(2,1)S(1)}, u32[]{:S(2)}, u32[]{:S(2)}) collective-permute-start(bf16[1536,128]{1,0:T(8,128)(2,1)S(1)} %shard_map.181.left_ref), channel_id=1, source_target_pairs={{0,8},{4,12},{8,0},{12,4},{16,24},{20,28},{24,16},{28,20},{1,9},{5... | collective-permute-start | bytes 1179656 | tf_op jit(solution)/shard_map/ppermute | solution.py:247
  16.1 1.3 %copy-start.7 = (bf16[1,256,2304]{2,1,0:T(8,128)(2,1)S(1)}, bf16[1,256,2304]{2,1,0:T(8,128)(2,1)}, u32[]{:S(2)}) copy-start(bf16[1,256,2304]{2,1,0:T(8,128)(2,1)} %inputs_ref.1) | copy-start | bytes 3538948
  17.3 0.9 %copy-start.8 = (bf16[1,256,512]{2,1,0:T(8,128)(2,1)S(1)}, bf16[1,256,512]{2,1,0:T(8,128)(2,1)}, u32[]{:S(2)}) copy-start(bf16[1,256,512]{2,1,0:T(8,128)(2,1)} %cot_ref.1) | copy-start | bytes 786436
  19.8 11.1 %collective-permute-start.4 = (bf16[288,512]{1,0:T(8,128)(2,1)S(1)}, bf16[288,512]{1,0:T(8,128)(2,1)S(1)}, u32[]{:S(2)}, u32[]{:S(2)}) collective-permute-start(bf16[288,512]{1,0:T(8,128)(2,1)S(1)} %get-tuple-element.53), channel_id=1, source_target_pairs={{0,1},{1,0},{2,3},{3,2},{4,5},{5,4},{6,7},{7,6},{8,9},{9,8},{10,11... | collective-permute-start | bytes 884744 | tf_op jit(solution)/shard_map/ppermute | solution.py:332
  20.4 10.5 %collective-permute-start.7 = (bf16[288,512]{1,0:T(8,128)(2,1)S(1)}, bf16[288,512]{1,0:T(8,128)(2,1)S(1)}, u32[]{:S(2)}, u32[]{:S(2)}) collective-permute-start(bf16[288,512]{1,0:T(8,128)(2,1)S(1)} %get-tuple-element.57), channel_id=1, source_target_pairs={{1,2},{2,1},{5,6},{6,5},{9,10},{10,9},{13,14},{14,13},{17,18},{18,... | collective-permute-start | bytes 884744 | tf_op jit(solution)/shard_map/ppermute | solution.py:332
  24.6 12.5 %collective-permute-start.6 = (bf16[288,512]{1,0:T(8,128)(2,1)S(1)}, bf16[288,512]{1,0:T(8,128)(2,1)S(1)}, u32[]{:S(2)}, u32[]{:S(2)}) collective-permute-start(bf16[288,512]{1,0:T(8,128)(2,1)S(1)} %get-tuple-element.56), channel_id=1, source_target_pairs={{0,1},{1,0},{2,3},{3,2},{4,5},{5,4},{6,7},{7,6},{8,9},{9,8},{10,11... | collective-permute-start | bytes 884744 | tf_op jit(solution)/shard_map/ppermute | solution.py:332
  26.7 10.5 %collective-permute-start.8 = (bf16[288,512]{1,0:T(8,128)(2,1)S(1)}, bf16[288,512]{1,0:T(8,128)(2,1)S(1)}, u32[]{:S(2)}, u32[]{:S(2)}) collective-permute-start(bf16[288,512]{1,0:T(8,128)(2,1)S(1)} %get-tuple-element.58), channel_id=1, source_target_pairs={{1,2},{2,1},{5,6},{6,5},{9,10},{10,9},{13,14},{14,13},{17,18},{18,... | collective-permute-start | bytes 884744 | tf_op jit(solution)/shard_map/ppermute | solution.py:332
  27.5 12.9 %collective-permute-start.14 = (bf16[1536,128]{1,0:T(8,128)(2,1)S(1)}, bf16[1536,128]{1,0:T(8,128)(2,1)S(1)}, u32[]{:S(2)}, u32[]{:S(2)}) collective-permute-start(bf16[1536,128]{1,0:T(8,128)(2,1)S(1)} %shard_map.184.left_ref), channel_id=1, source_target_pairs={{0,16},{4,20},{8,24},{12,28},{16,0},{20,4},{24,8},{28,12},{1,17},{... | collective-permute-start | bytes 1179656 | tf_op jit(solution)/shard_map/ppermute | solution.py:247
  31.0 12.5 %collective-permute-start.9 = (bf16[288,512]{1,0:T(8,128)(2,1)S(1)}, bf16[288,512]{1,0:T(8,128)(2,1)S(1)}, u32[]{:S(2)}, u32[]{:S(2)}) collective-permute-start(bf16[288,512]{1,0:T(8,128)(2,1)S(1)} %get-tuple-element.59), channel_id=1, source_target_pairs={{0,1},{1,0},{2,3},{3,2},{4,5},{5,4},{6,7},{7,6},{8,9},{9,8},{10,11... | collective-permute-start | bytes 884744 | tf_op jit(solution)/shard_map/ppermute | solution.py:332
  33.4 10.1 %collective-permute-start.12 = (bf16[288,512]{1,0:T(8,128)(2,1)S(1)}, bf16[288,512]{1,0:T(8,128)(2,1)S(1)}, u32[]{:S(2)}, u32[]{:S(2)}) collective-permute-start(bf16[288,512]{1,0:T(8,128)(2,1)S(1)} %get-tuple-element.63), channel_id=1, source_target_pairs={{1,2},{2,1},{5,6},{6,5},{9,10},{10,9},{13,14},{14,13},{17,18},{18,... | collective-permute-start | bytes 884744 | tf_op jit(solution)/shard_map/ppermute | solution.py:332
  37.3 12.5 %collective-permute-start.11 = (bf16[288,512]{1,0:T(8,128)(2,1)S(1)}, bf16[288,512]{1,0:T(8,128)(2,1)S(1)}, u32[]{:S(2)}, u32[]{:S(2)}) collective-permute-start(bf16[288,512]{1,0:T(8,128)(2,1)S(1)} %get-tuple-element.62), channel_id=1, source_target_pairs={{0,1},{1,0},{2,3},{3,2},{4,5},{5,4},{6,7},{7,6},{8,9},{9,8},{10,11... | collective-permute-start | bytes 884744 | tf_op jit(solution)/shard_map/ppermute | solution.py:332
  39.7 10.1 %collective-permute-start.13 = (bf16[288,512]{1,0:T(8,128)(2,1)S(1)}, bf16[288,512]{1,0:T(8,128)(2,1)S(1)}, u32[]{:S(2)}, u32[]{:S(2)}) collective-permute-start(bf16[288,512]{1,0:T(8,128)(2,1)S(1)} %get-tuple-element.64), channel_id=1, source_target_pairs={{1,2},{2,1},{5,6},{6,5},{9,10},{10,9},{13,14},{14,13},{17,18},{18,... | collective-permute-start | bytes 884744 | tf_op jit(solution)/shard_map/ppermute | solution.py:332
  40.5 15.5 %collective-permute-start.19 = (bf16[1536,128]{1,0:T(8,128)(2,1)S(1)}, bf16[1536,128]{1,0:T(8,128)(2,1)S(1)}, u32[]{:S(2)}, u32[]{:S(2)}) collective-permute-start(bf16[1536,128]{1,0:T(8,128)(2,1)S(1)} %shard_map.187.own_ref), channel_id=1, source_target_pairs={{0,4},{4,0},{8,12},{12,8},{16,20},{20,16},{24,28},{28,24},{1,5},{5... | collective-permute-start | bytes 1179656 | tf_op jit(solution)/shard_map/ppermute | solution.py:247
  43.6 15.3 %collective-permute-start.17 = (bf16[288,512]{1,0:T(8,128)(2,1)S(1)}, bf16[288,512]{1,0:T(8,128)(2,1)S(1)}, u32[]{:S(2)}, u32[]{:S(2)}) collective-permute-start(bf16[288,512]{1,0:T(8,128)(2,1)S(1)} %get-tuple-element.70), channel_id=1, source_target_pairs={{0,1},{1,0},{2,3},{3,2},{4,5},{5,4},{6,7},{7,6},{8,9},{9,8},{10,11... | collective-permute-start | bytes 884744 | tf_op jit(solution)/shard_map/ppermute | solution.py:332
  46.1 12.8 %collective-permute-start.18 = (bf16[288,512]{1,0:T(8,128)(2,1)S(1)}, bf16[288,512]{1,0:T(8,128)(2,1)S(1)}, u32[]{:S(2)}, u32[]{:S(2)}) collective-permute-start(bf16[288,512]{1,0:T(8,128)(2,1)S(1)} %get-tuple-element.71), channel_id=1, source_target_pairs={{1,2},{2,1},{5,6},{6,5},{9,10},{10,9},{13,14},{14,13},{17,18},{18,... | collective-permute-start | bytes 884744 | tf_op jit(solution)/shard_map/ppermute | solution.py:332
  49.9 12.1 %collective-permute-start.15 = (bf16[288,512]{1,0:T(8,128)(2,1)S(1)}, bf16[288,512]{1,0:T(8,128)(2,1)S(1)}, u32[]{:S(2)}, u32[]{:S(2)}) collective-permute-start(bf16[288,512]{1,0:T(8,128)(2,1)S(1)} %get-tuple-element.68), channel_id=1, source_target_pairs={{0,1},{1,0},{2,3},{3,2},{4,5},{5,4},{6,7},{7,6},{8,9},{9,8},{10,11... | collective-permute-start | bytes 884744 | tf_op jit(solution)/shard_map/ppermute | solution.py:332
  52.4 9.7 %collective-permute-start.16 = (bf16[288,512]{1,0:T(8,128)(2,1)S(1)}, bf16[288,512]{1,0:T(8,128)(2,1)S(1)}, u32[]{:S(2)}, u32[]{:S(2)}) collective-permute-start(bf16[288,512]{1,0:T(8,128)(2,1)S(1)} %get-tuple-element.69), channel_id=1, source_target_pairs={{1,2},{2,1},{5,6},{6,5},{9,10},{10,9},{13,14},{14,13},{17,18},{18,... | collective-permute-start | bytes 884744 | tf_op jit(solution)/shard_map/ppermute | solution.py:332
  53.1 2.9 %copy-start.5 = (f32[393216]{0:T(1024)S(1)}, f32[393216]{0:T(1024)}, u32[]{:S(2)}) copy-start(f32[393216]{0:T(1024)} %param.20) | copy-start | bytes 4718596
  53.1 2.9 %copy-start.6 = (f32[393216]{0:T(1024)S(1)}, f32[393216]{0:T(1024)}, u32[]{:S(2)}) copy-start(f32[393216]{0:T(1024)} %param.21) | copy-start | bytes 4718596
  56.0 2.9 %copy-start.1 = (bf16[1,576,512]{2,1,0:T(8,128)(2,1)S(1)}, bf16[1,576,512]{2,1,0:T(8,128)(2,1)}, u32[]{:S(2)}) copy-start(bf16[1,576,512]{2,1,0:T(8,128)(2,1)} %weight_ref.5) | copy-start | bytes 1769476
  56.0 2.9 %copy-start.2 = (f32[1,576,512]{2,1,0:T(8,128)S(1)}, f32[1,576,512]{2,1,0:T(8,128)}, u32[]{:S(2)}) copy-start(f32[1,576,512]{2,1,0:T(8,128)} %first_ref.3) | copy-start | bytes 3538948
  56.0 2.9 %copy-start.3 = (f32[1,576,512]{2,1,0:T(8,128)S(1)}, f32[1,576,512]{2,1,0:T(8,128)}, u32[]{:S(2)}) copy-start(f32[1,576,512]{2,1,0:T(8,128)} %second_ref.3) | copy-start | bytes 3538948
  62.1 1.9 %copy-start.10 = (f32[1,576]{1,0:T(1,128)S(1)}, f32[1,576]{1,0:T(1,128)}, u32[]{:S(2)}) copy-start(f32[1,576]{1,0:T(1,128)} %refs_2_.1) | copy-start | bytes 6916
  62.1 1.9 %copy-start.11 = (f32[1,576]{1,0:T(1,128)S(1)}, f32[1,576]{1,0:T(1,128)}, u32[]{:S(2)}) copy-start(f32[1,576]{1,0:T(1,128)} %refs_3_.1) | copy-start | bytes 6916
  62.1 1.9 %copy-start.12 = (f32[1,576]{1,0:T(1,128)S(1)}, f32[1,576]{1,0:T(1,128)}, u32[]{:S(2)}) copy-start(f32[1,576]{1,0:T(1,128)} %refs_4_.1) | copy-start | bytes 6916

commit v3 on v2

--- a/solution.py
+++ b/solution.py
@@ -23,12 +23,14 @@
 chunk_count = 2
 lanes = 128
 vmem_limit = 12 * 1024 * 1024
+moved_scale, moved_partial, moved_pair, moved_sum = 0, 0, 0, 0
+moved_onward, moved_keys, moved_adam, moved_outer = 0, 0, 0, 0
 
 wide = jnp.float32
 narrow = jnp.bfloat16
 VMEM = pl.BlockSpec(memory_space=pltpu.VMEM)
-SMEM = pl.BlockSpec(memory_space=pltpu.SMEM)
 HBM = pl.BlockSpec(memory_space=pltpu.HBM)
+held_shape = pltpu.VMEM
 
 
 def adam_step(params, gradient, first_moment, second_moment):
@@ -44,6 +46,10 @@
     return (new_params, new_mom)
 
 
+def core_of_chip():
+    return lax.axis_index("silo") & 1
+
+
 def add_narrow(left, right):
     return (left.astype(wide) + right.astype(wide)).astype(narrow)
 
@@ -55,7 +61,7 @@
     return 1
 
 
-def call(kernel, out_shape, inputs, flops=0, moved=0, scratch=(), aliases=None, specs=None, outs=None, grid=(), limit=vmem_limit):
+def call(kernel, out_shape, inputs, moved=0, scratch=(), aliases=None, specs=None, outs=None, grid=(), limit=vmem_limit):
     return pl.pallas_call(
         kernel,
         out_shape=out_shape,
@@ -64,13 +70,14 @@
         out_specs=outs if outs is not None else jax.tree.map(lambda _: VMEM, out_shape),
         scratch_shapes=list(scratch),
         compiler_params=pltpu.CompilerParams(vmem_limit_bytes=limit),
+        cost_estimate=pl.CostEstimate(flops=0, bytes_accessed=moved, transcendentals=0) if moved else None,
 
         input_output_aliases=aliases or {},
     )(*inputs)
 
 
 def scale_kernel(chunks, weight_ref, gain_ref, spread_ref, *refs):
-    sent_refs, (held, sems) = refs[:chunks], refs[chunks:]
+    sent_refs, (held, gain_held, sems) = refs[:chunks], refs[chunks:]
     rows = weight_ref.shape[1]
     depth = rows // chunks
     spans = [slice(c * depth, (c + 1) * depth) for c in range(chunks)]
@@ -78,9 +85,11 @@
         pltpu.make_async_copy(weight_ref.at[0, span], held.at[span], sems.at[c])
         for c, span in enumerate(spans)
     ]
-    for copy in copies:
+    gain_copy = pltpu.make_async_copy(gain_ref, gain_held, sems.at[chunks])
+    for copy in (gain_copy, *copies):
         copy.start()
-    spread = jnp.broadcast_to(gain_ref[...], (lanes, rows)).T
+    gain_copy.wait()
+    spread = jnp.broadcast_to(gain_held[...], (lanes, rows)).T
     spread_ref[...] = spread
     used = spread.astype(narrow).astype(wide)
     for c, span in enumerate(spans):
@@ -116,8 +125,8 @@
         ).astype(narrow)
 
 
-def onward_kernel(n, c, chunks, s, me_ref, partial_ref, even_ref, odd_ref, to_even_ref, to_odd_ref):
-    me = me_ref[0]
+def onward_kernel(n, c, chunks, s, partial_ref, even_ref, odd_ref, to_even_ref, to_odd_ref):
+    me = lax.axis_index("fsdp")
     depth = even_ref.shape[0]
     even = (me & 1) == 0
     for came_ref, sent_ref, right in (
@@ -137,18 +146,21 @@
             sent_ref[...] = came_ref[...]
 
 
-def keys_kernel(n, chunks, me_ref, inputs_ref, rms_ref, *refs):
-    own, got = refs[:chunks], refs[chunks:-2]
-    keys_ref, weights = refs[-2:]
-    me = me_ref[0]
-    depth, cols = own[0].shape
-    rows = depth * chunks
+def keys_kernel(n, chunks, inputs_ref, rms_ref, weight_ref, spread_ref, *refs):
+    got, (keys_ref, weights) = refs[:-2], refs[-2:]
+    me = lax.axis_index("fsdp")
+    rows, cols = weight_ref.shape[1:]
+    depth = rows // chunks
+    used = spread_ref[...].astype(narrow).astype(wide)
+    for k in range(cols // lanes):
+        part = slice(k * lanes, (k + 1) * lanes)
+        weights[pl.ds(pl.multiple_of(me * rows, 16), rows), part] = (
+            weight_ref[0, :, part].astype(wide) * used
+        ).astype(narrow)
 
     def put(block, c, ref):
         weights[pl.ds(pl.multiple_of(block * rows + c * depth, 16), depth), :] = ref[...]
 
-    for c in range(chunks):
-        put(me, c, own[c])
     even = (me & 1) == 0
     for s in range(n - 1):
         for w in range(2):
@@ -178,12 +190,18 @@
         copy.wait()
 
 
-def adam_kernel(c, chunks, me_ref, spread_ref, weight_ref, first_ref, second_ref, partial_ref, *refs):
-    came, outs = refs[:2], refs[-4:]
-    share_ref, new_weight_ref, new_first_ref, new_second_ref = outs
+def adam_kernel(c, chunks, spread_ref, weight_ref, first_ref, second_ref, partial_ref, *refs):
+    last = c == chunks - 1
+    came = refs[:2]
+    if last:
+        shares, gains = refs[2 : 2 + c], refs[2 + c : 5 + c]
+        new_gains, share_ref = refs[-4:-1], refs[-1]
+        new_weight_ref, new_first_ref, new_second_ref = refs[-7:-4]
+    else:
+        share_ref, new_weight_ref, new_first_ref, new_second_ref = refs[-4:]
     depth, cols = weight_ref.shape[1:]
-    steps = pl.num_programs(0)
-    start = pl.multiple_of(((me_ref[0] * chunks + c) * steps + pl.program_id(0)) * depth, 16)
+    step, steps = pl.program_id(0), pl.num_programs(0)
+    start = pl.multiple_of(((lax.axis_index("fsdp") * chunks + c) * steps + step) * depth, 16)
     share = jnp.zeros((depth, lanes), wide)
     used = spread_ref[...].astype(narrow).astype(wide)
     for k in range(cols // lanes):
@@ -199,26 +217,35 @@
         new_weight_ref[0, :, part] = new_weight.astype(narrow)
         new_first_ref[0, :, part] = new_first
         new_second_ref[0, :, part] = new_second
-    share_ref[...] = share
-
-
-def gain_kernel(chunks, *refs):
-    gain_ref, first_ref, second_ref = refs[chunks : chunks + 3]
-    news = refs[chunks + 3 :]
-    share = jnp.concatenate([ref[...] for ref in refs[:chunks]], axis=0)
-    gradient = jnp.sum(share.T, axis=0, keepdims=True)
-    for ref, value in zip(news, adam_step(gain_ref[...], gradient, first_ref[...], second_ref[...])):
-        ref[...] = value
-
-
-def pair_kernel(core_ref, mine_ref, other_ref, half_ref):
+    if not last:
+        share_ref[...] = share
+        return
+    share_ref[pl.ds(pl.multiple_of(step * depth, 16), depth), :] = share
+
+    @pl.when(step == steps - 1)
+    def _():
+        whole = jnp.concatenate([ref[...] for ref in (*shares, share_ref)], axis=0)
+        gradient = jnp.sum(whole.T, axis=0, keepdims=True)
+        for ref, value in zip(new_gains, adam_step(gains[0][...], gradient, gains[1][...], gains[2][...])):
+            ref[...] = value
+
+
+def pair_kernel(mine_ref, other_ref, half_ref, mine_held, other_held, sems):
     half, step = half_ref.shape[0], 16
-    start = core_ref[0] * half
+    whole = pl.ds(pl.multiple_of(core_of_chip() * (half * lanes), half * lanes), half * lanes)
+    copies = [
+        pltpu.make_async_copy(mine_ref.at[:, whole], mine_held, sems.at[0]),
+        pltpu.make_async_copy(other_ref.at[:, whole], other_held, sems.at[1]),
+    ]
+    for copy in copies:
+        copy.start()
+    for copy in copies:
+        copy.wait()
 
     @pl.loop(0, half // step, unroll=4)
     def _(i):
-        span = pl.ds(pl.multiple_of((start + i * step) * lanes, step * lanes), step * lanes)
-        total = mine_ref[:, span].astype(wide) + other_ref[:, span].astype(wide)
+        span = pl.ds(pl.multiple_of(i * (step * lanes), step * lanes), step * lanes)
+        total = mine_held[:, span].astype(wide) + other_held[:, span].astype(wide)
         half_ref[pl.ds(pl.multiple_of(i * step, step), step), :] = total.reshape(step, lanes).astype(narrow)
 
 
@@ -226,17 +253,29 @@
     total_ref[...] = add_narrow(left_ref[...], right_ref[...])
 
 
-def nesterov_kernel(silos, core_ref, own_ref, other_ref, params_ref, mom_ref, new_params_ref, new_mom_ref):
-    mine = core_ref[0] == pl.program_id(0)
+def nesterov_kernel(silos, own_ref, other_ref, params_ref, mom_ref, new_params_ref, new_mom_ref):
+    mine = core_of_chip() == pl.program_id(0)
     delta = jnp.where(mine, own_ref[...], other_ref[...]).astype(wide) / silos
     new_params_ref[0], new_mom_ref[0] = nesterov(delta, params_ref[0], mom_ref[0])
 
 
+def in_hbm(array):
+    return pltpu.with_memory_space_constraint(array, pltpu.HBM)
+
+
+def in_vmem(arrays):
+    return [pltpu.with_memory_space_constraint(array, pltpu.VMEM) for array in arrays]
+
+
 def tie(values, other):
     return lax.optimization_barrier((values, other))[0]
 
 
-def outer_steps(pseudo_grad, outer_params, outer_mom, silos):
+def pair_operands(mine, other):
+    return [in_hbm(mine), other]
+
+
+def outer_steps(pseudo_grad, outer_params, outer_mom, silos, after):
     size = pseudo_grad.shape[1]
     half = size // 2 // lanes
     if silos < 2 or silos & (silos - 1) != 0 or size % (32 * lanes) != 0:
@@ -246,16 +285,19 @@
     def swap(part, bit):
         return lax.ppermute(part, "silo", [(i, i ^ bit) for i in range(silos)])
 
-    core = (lax.axis_index("silo") & 1).astype(jnp.int32).reshape(1)
-    part = jax.ShapeDtypeStruct((half, lanes), narrow)
-    cost = dict(flops=half * lanes, moved=6 * half * lanes)
+    part = held_shape((half, lanes), narrow)
     total = call(
-        pair_kernel, part, [core, pseudo_grad, swap(pseudo_grad, 1)], specs=[SMEM, VMEM, VMEM], **cost
+        pair_kernel,
+        part,
+        pair_operands(*tie([pseudo_grad, swap(pseudo_grad, 1)], after)),
+        moved=moved_pair,
+        specs=[HBM, HBM],
+        scratch=[pltpu.VMEM((1, half * lanes), narrow)] * 2 + [pltpu.SemaphoreType.DMA((2,))],
     )
     yield total
     bit = 2
     while bit < silos:
-        total = call(sum_kernel, part, [total, swap(total, bit)], **cost)
+        total = call(sum_kernel, part, in_vmem([total, swap(total, bit)]), moved=moved_sum)
         yield total
         bit *= 2
     other = swap(total, 1)
@@ -265,10 +307,9 @@
     new_params, new_mom = call(
         functools.partial(nesterov_kernel, silos),
         [jax.ShapeDtypeStruct((2, half, lanes), wide)] * 2,
-        [core, total, other, outer_params.reshape(2, half, lanes), outer_mom.reshape(2, half, lanes)],
-        flops=12 * size,
-        moved=20 * size,
-        specs=[SMEM, line, line, block, block],
+        [total, other, outer_params.reshape(2, half, lanes), outer_mom.reshape(2, half, lanes)],
+        moved=moved_outer,
+        specs=[line, line, block, block],
         outs=[block, block],
         grid=(2, steps),
     )
@@ -289,8 +330,6 @@
         outer_params,
         outer_mom,
     ):
-        me = lax.axis_index("fsdp")
-        me_word = me.astype(jnp.int32).reshape(1)
         tokens, feats = activations.shape[1:]
         rows, cols = key_weight.shape[1:]
         chunks = chunk_count if rows % (16 * chunk_count) == 0 else 1
@@ -299,12 +338,15 @@
 
         spread, *own = call(
             functools.partial(scale_kernel, chunks),
-            [shape((rows, lanes), wide)] + [shape((depth, cols), narrow)] * chunks,
-            [key_weight, norm_gain],
-            flops=rows * cols,
-            moved=4 * rows * cols,
-            specs=[HBM, VMEM],
-            scratch=[pltpu.VMEM((rows, cols), narrow), pltpu.SemaphoreType.DMA((chunks,))],
+            [held_shape((rows, lanes), wide)] + [held_shape((depth, cols), narrow)] * chunks,
+            [in_hbm(key_weight), in_hbm(norm_gain)],
+            moved=moved_scale,
+            specs=[HBM, HBM],
+            scratch=[
+                pltpu.VMEM((rows, cols), narrow),
+                pltpu.VMEM((1, rows), wide),
+                pltpu.SemaphoreType.DMA((chunks + 1,)),
+            ],
         )
         links = [
             [pair for i in range(start, n - 1, 2) for pair in ((i, i + 1), (i + 1, i))]
@@ -322,11 +364,10 @@
                         came = tie(came, outer_part)
                     sent = call(
                         functools.partial(onward_kernel, n, c, chunks, s),
-                        [shape((depth, cols), narrow)] * 2,
-                        [me_word, partial, *came],
-                        flops=2 * depth * cols,
-                        moved=12 * depth * cols,
-                        specs=[SMEM] + [VMEM] * 3,
+                        [held_shape((depth, cols), narrow)] * 2,
+                        [partial, *in_vmem(came)],
+                        moved=moved_onward,
+                        specs=[VMEM] * 3,
                     )
                 for w in range(2):
                     got[w][c] = lax.ppermute(sent[w], "fsdp", links[w])
@@ -335,28 +376,26 @@
                 partial, inv_rms, inputs = call(
                     partial_kernel,
                     [
-                        shape((feats, cols), narrow),
-                        shape((tokens, lanes), wide),
-                        shape(activations.shape, narrow),
+                        held_shape((feats, cols), narrow),
+                        held_shape((tokens, lanes), wide),
+                        held_shape(activations.shape, narrow),
                     ],
-                    [activations, key_cot],
+                    [in_hbm(activations), in_hbm(key_cot)],
+                    moved=moved_partial,
                     specs=[HBM, HBM],
                     scratch=[pltpu.VMEM(key_cot.shape, narrow), pltpu.SemaphoreType.DMA((2,))],
-                    flops=2 * tokens * feats * cols,
-                    moved=2 * (tokens * feats + feats * cols + tokens * cols),
                 )
-                outer = outer_steps(pseudo_grad, outer_params, outer_mom, silos)
+                outer = outer_steps(pseudo_grad, outer_params, outer_mom, silos, partial)
                 outer_part = partial
 
         keys = call(
             functools.partial(keys_kernel, n, chunks),
             shape((1, tokens, cols), narrow),
-            [me_word, inputs, inv_rms, *own]
+            [inputs, inv_rms, key_weight, spread]
             + [slots[s][w][c] for s in range(n - 1) for w in range(2) for c in range(chunks)],
-            flops=2 * tokens * feats * cols,
-            moved=2 * (tokens * feats + feats * cols + tokens * cols),
+            moved=moved_keys,
             scratch=[pltpu.VMEM((feats, cols), narrow)],
-            specs=[SMEM] + [VMEM] * (2 + chunks + (n - 1) * 2 * chunks),
+            specs=[VMEM] * (4 + (n - 1) * 2 * chunks),
         )
 
         for outer_part in outer:
@@ -369,30 +408,35 @@
             if c == 0:
                 came = tie(came, outer_part)
             block = pl.BlockSpec((1, tall, cols), lambda i, c=c: (0, c * steps + i, 0))
-            share, *news = call(
+            last = c == chunks - 1
+            extra = [*shares, norm_gain, gain_first, gain_second] if last else []
+            gain_outs = [shape((1, rows), wide)] * 3
+            count = len(extra)
+            outs = call(
                 functools.partial(adam_kernel, c, chunks),
-                [shape((depth, lanes), wide)]
-                + [shape((1, rows, cols), kind) for kind in (narrow, wide, wide)],
-                [me_word, spread, key_weight, weight_first, weight_second, partial, *came, *news],
-                flops=20 * depth * cols,
-                moved=20 * depth * cols,
-                specs=[SMEM, pl.BlockSpec((tall, lanes), lambda i, c=c: (c * steps + i, 0))]
+                ([] if last else [shape((depth, lanes), wide)])
+                + [shape((1, rows, cols), kind) for kind in (narrow, wide, wide)]
+                + (gain_outs if last else []),
+                [spread, key_weight, weight_first, weight_second, partial, *came, *extra, *news],
+                moved=moved_adam,
+                specs=[pl.BlockSpec((tall, lanes), lambda i, c=c: (c * steps + i, 0))]
                 + [block] * 3
                 + [VMEM]
                 + [pl.BlockSpec((tall, cols), lambda i: (i, 0))] * 2
+                + [VMEM] * count
                 + [pl.BlockSpec(memory_space=pl.ANY)] * len(news),
-                outs=[pl.BlockSpec((tall, lanes), lambda i: (i, 0))] + [block] * 3,
-                aliases={8 + i: 1 + i for i in range(len(news))},
+                outs=([] if last else [pl.BlockSpec((tall, lanes), lambda i: (i, 0))])
+                + [block] * 3
+                + ([VMEM] * 3 if last else []),
+                aliases={7 + count + i: (0 if last else 1) + i for i in range(len(news))},
+                scratch=[pltpu.VMEM((depth, lanes), wide)] if last else [],
                 grid=(steps,),
             )
-            shares.append(share)
-        new_gains = call(
-            functools.partial(gain_kernel, chunks),
-            [shape((1, rows), wide)] * 3,
-            [*shares, norm_gain, gain_first, gain_second],
-            flops=20 * rows,
-            moved=4 * rows * (lanes + 6),
-        )
+            if last:
+                news, new_gains = outs[:3], outs[3:]
+            else:
+                shares.append(outs[0])
+                news = outs[1:]
         return (
             keys,
             *news,

time: 65.3 us -> 62.8 us (0.962)
  local copies, waits for them, and re-layouts: 5.42 us -> 0.13 us
  waiting for transfers between devices: 15.7 us -> 17.7 us
    unnamed x26 -> x16, local copies, waits for them, and re-layouts: 5.42 us -> 0.13 us
    ppermute x16, waiting for transfers between devices: 15.6 us -> 17.5 us  [per_device(): got[w][c] = lax.ppermute(sent[w], 'fsdp', links[w])]
    pallas_call x16 -> x15, Pallas kernels: 14.1 us -> 14.6 us  [call(): pl.pallas_call(kernel, out_shape=out_shape, grid=grid, in_specs=specs if...]
  transfers between devices with their start and end apart: 20 -> 20, of which waited for: 6 -> 7; matrix products, arithmetic and copies ran while one was open for 0% -> 0% of each run, Pallas kernels for 18% -> 20%
where the time goes in v3:
time: 62.8 us; the launch traced here: 62.4 us
  starting transfers between devices  29 us (46%)
  waiting for transfers between devices  17.7 us (28%)
  Pallas kernels  14.6 us (23%)
  between operations  0.91 us (1%)
    ppermute x16, starting transfers between devices, per_device(): got[w][c] = lax.ppermute(sent[w], 'fsdp', links[w])  25.2 us
    ppermute x16, waiting for transfers between devices, per_device(): got[w][c] = lax.ppermute(sent[w], 'fsdp', links[w])  17.5 us
    pallas_call x15, Pallas kernels, call(): pl.pallas_call(kernel, out_shape=out_shape, grid=grid, in_specs=specs if...  14.6 us
    ppermute x4, starting transfers between devices, swap(): return lax.ppermute(part, 'silo', [(i, i ^ bit) for i in range(silos)])  3.73 us
  transfers between devices with their start and end apart: 20, of which 7 were waited for; matrix products, arithmetic and copies ran while one was open for 0% of the time, Pallas kernels for 20%

profile of v3, /device:TPU:0, one launch (start us, length us, event | category | flops | bytes accessed | tf_op | source)
XLA Modules:
  0.0 62.4 jit_solution(8190086488374249745)
XLA Ops:
  0.6 0.5 collective-permute-start.5
  1.2 1.2 %shard_map.179 = (f32[576,128]{1,0:T(8,128)S(1)}, bf16[288,512]{1,0:T(8,128)(2,1)S(1)}, bf16[288,512]{1,0:T(8,128)(2,1)S(1)}) custom-call(bf16[1,576,512]{2,1,0:T(8,128)(2,1)} %weight_ref.7, f32[1,576]{1,0:T(1,128)} %refs_3_.1), custom_call_target="tpu_custom_call" | custom-call | tf_op jit(solution)/shard_map/pallas_call | solution.py:65
  2.3 0.7 %collective-permute-start.2 = (bf16[288,512]{1,0:T(8,128)(2,1)S(1)}, bf16[288,512]{1,0:T(8,128)(2,1)S(1)}, u32[]{:S(2)}, u32[]{:S(2)}) collective-permute-start(bf16[288,512]{1,0:T(8,128)(2,1)S(1)} %get-tuple-element.52), channel_id=1, source_target_pairs={{1,2},{2,1},{5,6},{6,5},{9,10},{10,9},{13,14},{14,13},{17,18},{18,... | collective-permute-start | bytes 884744 | tf_op jit(solution)/shard_map/ppermute | solution.py:373
  3.0 5.5 %collective-permute-start = (bf16[288,512]{1,0:T(8,128)(2,1)S(1)}, bf16[288,512]{1,0:T(8,128)(2,1)S(1)}, u32[]{:S(2)}, u32[]{:S(2)}) collective-permute-start(bf16[288,512]{1,0:T(8,128)(2,1)S(1)} %get-tuple-element.52), channel_id=1, source_target_pairs={{0,1},{1,0},{2,3},{3,2},{4,5},{5,4},{6,7},{7,6},{8,9},{9,8},{10,11... | collective-permute-start | bytes 884744 | tf_op jit(solution)/shard_map/ppermute | solution.py:373
  8.5 0.7 %collective-permute-start.3 = (bf16[288,512]{1,0:T(8,128)(2,1)S(1)}, bf16[288,512]{1,0:T(8,128)(2,1)S(1)}, u32[]{:S(2)}, u32[]{:S(2)}) collective-permute-start(bf16[288,512]{1,0:T(8,128)(2,1)S(1)} %get-tuple-element.53), channel_id=1, source_target_pairs={{1,2},{2,1},{5,6},{6,5},{9,10},{10,9},{13,14},{14,13},{17,18},{18,... | collective-permute-start | bytes 884744 | tf_op jit(solution)/shard_map/ppermute | solution.py:373
  9.1 1.8 %collective-permute-start.1 = (bf16[288,512]{1,0:T(8,128)(2,1)S(1)}, bf16[288,512]{1,0:T(8,128)(2,1)S(1)}, u32[]{:S(2)}, u32[]{:S(2)}) collective-permute-start(bf16[288,512]{1,0:T(8,128)(2,1)S(1)} %get-tuple-element.53), channel_id=1, source_target_pairs={{0,1},{1,0},{2,3},{3,2},{4,5},{5,4},{6,7},{7,6},{8,9},{9,8},{10,11... | collective-permute-start | bytes 884744 | tf_op jit(solution)/shard_map/ppermute | solution.py:373
  10.9 2.4 %shard_map.178 = (bf16[2304,512]{1,0:T(8,128)(2,1)S(1)}, f32[256,128]{1,0:T(8,128)S(1)}, bf16[1,256,2304]{2,1,0:T(8,128)(2,1)S(1)}) custom-call(bf16[1,256,2304]{2,1,0:T(8,128)(2,1)} %inputs_ref.1, bf16[1,256,512]{2,1,0:T(8,128)(2,1)} %cot_ref.1), custom_call_target="tpu_custom_call" | custom-call | tf_op jit(solution)/shard_map/pallas_call | solution.py:65
  13.3 1.5 %shard_map.181.left_ref = bf16[1536,128]{1,0:T(8,128)(2,1)S(1)} custom-call(bf16[1,393216]{1,0:T(2,128)(2,1)} %mine_ref, bf16[1,393216]{1,0:T(2,128)(2,1)S(1)} %collective-permute-done.5.other_ref), custom_call_target="tpu_custom_call" | custom-call | tf_op jit(solution)/shard_map/pallas_call | solution.py:65
  14.9 1.6 %collective-permute-start.10 = (bf16[1536,128]{1,0:T(8,128)(2,1)S(1)}, bf16[1536,128]{1,0:T(8,128)(2,1)S(1)}, u32[]{:S(2)}, u32[]{:S(2)}) collective-permute-start(bf16[1536,128]{1,0:T(8,128)(2,1)S(1)} %shard_map.181.left_ref), channel_id=1, source_target_pairs={{0,8},{4,12},{8,0},{12,4},{16,24},{20,28},{24,16},{28,20},{1,9},{5... | collective-permute-start | bytes 1179656 | tf_op jit(solution)/shard_map/ppermute | solution.py:286
  16.4 0.1 shard_map.180
  16.5 1.9 %collective-permute-start.4 = (bf16[288,512]{1,0:T(8,128)(2,1)S(1)}, bf16[288,512]{1,0:T(8,128)(2,1)S(1)}, u32[]{:S(2)}, u32[]{:S(2)}) collective-permute-start(bf16[288,512]{1,0:T(8,128)(2,1)S(1)} %get-tuple-element.55), channel_id=1, source_target_pairs={{0,1},{1,0},{2,3},{3,2},{4,5},{5,4},{6,7},{7,6},{8,9},{9,8},{10,11... | collective-permute-start | bytes 884744 | tf_op jit(solution)/shard_map/ppermute | solution.py:373
  18.4 0.7 %collective-permute-start.7 = (bf16[288,512]{1,0:T(8,128)(2,1)S(1)}, bf16[288,512]{1,0:T(8,128)(2,1)S(1)}, u32[]{:S(2)}, u32[]{:S(2)}) collective-permute-start(bf16[288,512]{1,0:T(8,128)(2,1)S(1)} %get-tuple-element.61), channel_id=1, source_target_pairs={{1,2},{2,1},{5,6},{6,5},{9,10},{10,9},{13,14},{14,13},{17,18},{18,... | collective-permute-start | bytes 884744 | tf_op jit(solution)/shard_map/ppermute | solution.py:373
  19.1 3.5 %collective-permute-done.1.even_ref.refs_1_ = bf16[288,512]{1,0:T(8,128)(2,1)S(1)} collective-permute-done((bf16[288,512]{1,0:T(8,128)(2,1)S(1)}, bf16[288,512]{1,0:T(8,128)(2,1)S(1)}, u32[]{:S(2)}, u32[]{:S(2)}) %collective-permute-start.1) | collective-permute-done | bytes 294944 | tf_op jit(solution)/shard_map/ppermute | solution.py:373
  22.6 0.1 shard_map.182
  22.7 2.1 %collective-permute-start.6 = (bf16[288,512]{1,0:T(8,128)(2,1)S(1)}, bf16[288,512]{1,0:T(8,128)(2,1)S(1)}, u32[]{:S(2)}, u32[]{:S(2)}) collective-permute-start(bf16[288,512]{1,0:T(8,128)(2,1)S(1)} %get-tuple-element.60), channel_id=1, source_target_pairs={{0,1},{1,0},{2,3},{3,2},{4,5},{5,4},{6,7},{7,6},{8,9},{9,8},{10,11... | collective-permute-start | bytes 884744 | tf_op jit(solution)/shard_map/ppermute | solution.py:373
  24.7 0.7 %collective-permute-start.8 = (bf16[288,512]{1,0:T(8,128)(2,1)S(1)}, bf16[288,512]{1,0:T(8,128)(2,1)S(1)}, u32[]{:S(2)}, u32[]{:S(2)}) collective-permute-start(bf16[288,512]{1,0:T(8,128)(2,1)S(1)} %get-tuple-element.62), channel_id=1, source_target_pairs={{1,2},{2,1},{5,6},{6,5},{9,10},{10,9},{13,14},{14,13},{17,18},{18,... | collective-permute-start | bytes 884744 | tf_op jit(solution)/shard_map/ppermute | solution.py:373
  25.4 0.2 collective-permute-done.10.right_ref
  25.6 0.1 shard_map.184.left_ref
  25.7 1.6 %collective-permute-start.14 = (bf16[1536,128]{1,0:T(8,128)(2,1)S(1)}, bf16[1536,128]{1,0:T(8,128)(2,1)S(1)}, u32[]{:S(2)}, u32[]{:S(2)}) collective-permute-start(bf16[1536,128]{1,0:T(8,128)(2,1)S(1)} %shard_map.184.left_ref), channel_id=1, source_target_pairs={{0,16},{4,20},{8,24},{12,28},{16,0},{20,4},{24,8},{28,12},{1,17},{... | collective-permute-start | bytes 1179656 | tf_op jit(solution)/shard_map/ppermute | solution.py:286
  27.3 1.6 %collective-permute-done.4.even_ref.refs_4_ = bf16[288,512]{1,0:T(8,128)(2,1)S(1)} collective-permute-done((bf16[288,512]{1,0:T(8,128)(2,1)S(1)}, bf16[288,512]{1,0:T(8,128)(2,1)S(1)}, u32[]{:S(2)}, u32[]{:S(2)}) %collective-permute-start.4) | collective-permute-done | bytes 294944 | tf_op jit(solution)/shard_map/ppermute | solution.py:373
  28.9 0.1 shard_map.183
  29.0 2.1 %collective-permute-start.9 = (bf16[288,512]{1,0:T(8,128)(2,1)S(1)}, bf16[288,512]{1,0:T(8,128)(2,1)S(1)}, u32[]{:S(2)}, u32[]{:S(2)}) collective-permute-start(bf16[288,512]{1,0:T(8,128)(2,1)S(1)} %get-tuple-element.63), channel_id=1, source_target_pairs={{0,1},{1,0},{2,3},{3,2},{4,5},{5,4},{6,7},{7,6},{8,9},{9,8},{10,11... | collective-permute-start | bytes 884744 | tf_op jit(solution)/shard_map/ppermute | solution.py:373
  31.1 0.7 %collective-permute-start.12 = (bf16[288,512]{1,0:T(8,128)(2,1)S(1)}, bf16[288,512]{1,0:T(8,128)(2,1)S(1)}, u32[]{:S(2)}, u32[]{:S(2)}) collective-permute-start(bf16[288,512]{1,0:T(8,128)(2,1)S(1)} %get-tuple-element.67), channel_id=1, source_target_pairs={{1,2},{2,1},{5,6},{6,5},{9,10},{10,9},{13,14},{14,13},{17,18},{18,... | collective-permute-start | bytes 884744 | tf_op jit(solution)/shard_map/ppermute | solution.py:373
  31.8 3.4 %collective-permute-done.6.even_ref.refs_5_ = bf16[288,512]{1,0:T(8,128)(2,1)S(1)} collective-permute-done((bf16[288,512]{1,0:T(8,128)(2,1)S(1)}, bf16[288,512]{1,0:T(8,128)(2,1)S(1)}, u32[]{:S(2)}, u32[]{:S(2)}) %collective-permute-start.6) | collective-permute-done | bytes 294944 | tf_op jit(solution)/shard_map/ppermute | solution.py:373
  35.2 0.1 shard_map.185
  35.3 2.1 %collective-permute-start.11 = (bf16[288,512]{1,0:T(8,128)(2,1)S(1)}, bf16[288,512]{1,0:T(8,128)(2,1)S(1)}, u32[]{:S(2)}, u32[]{:S(2)}) collective-permute-start(bf16[288,512]{1,0:T(8,128)(2,1)S(1)} %get-tuple-element.66), channel_id=1, source_target_pairs={{0,1},{1,0},{2,3},{3,2},{4,5},{5,4},{6,7},{7,6},{8,9},{9,8},{10,11... | collective-permute-start | bytes 884744 | tf_op jit(solution)/shard_map/ppermute | solution.py:373
  37.4 0.7 %collective-permute-start.13 = (bf16[288,512]{1,0:T(8,128)(2,1)S(1)}, bf16[288,512]{1,0:T(8,128)(2,1)S(1)}, u32[]{:S(2)}, u32[]{:S(2)}) collective-permute-start(bf16[288,512]{1,0:T(8,128)(2,1)S(1)} %get-tuple-element.68), channel_id=1, source_target_pairs={{1,2},{2,1},{5,6},{6,5},{9,10},{10,9},{13,14},{14,13},{17,18},{18,... | collective-permute-start | bytes 884744 | tf_op jit(solution)/shard_map/ppermute | solution.py:373
  38.1 0.1 shard_map.187.own_ref
  38.2 0.1 collective-permute-start.19
  38.3 3.2 %collective-permute-done.9.refs_8_.even_ref = bf16[288,512]{1,0:T(8,128)(2,1)S(1)} collective-permute-done((bf16[288,512]{1,0:T(8,128)(2,1)S(1)}, bf16[288,512]{1,0:T(8,128)(2,1)S(1)}, u32[]{:S(2)}, u32[]{:S(2)}) %collective-permute-start.9) | collective-permute-done | bytes 294944 | tf_op jit(solution)/shard_map/ppermute | solution.py:373
  41.5 0.1 shard_map.189
  41.6 2.2 %collective-permute-start.17 = (bf16[288,512]{1,0:T(8,128)(2,1)S(1)}, bf16[288,512]{1,0:T(8,128)(2,1)S(1)}, u32[]{:S(2)}, u32[]{:S(2)}) collective-permute-start(bf16[288,512]{1,0:T(8,128)(2,1)S(1)} %get-tuple-element.73), channel_id=1, source_target_pairs={{0,1},{1,0},{2,3},{3,2},{4,5},{5,4},{6,7},{7,6},{8,9},{9,8},{10,11... | collective-permute-start | bytes 884744 | tf_op jit(solution)/shard_map/ppermute | solution.py:373
  43.8 0.8 %collective-permute-start.18 = (bf16[288,512]{1,0:T(8,128)(2,1)S(1)}, bf16[288,512]{1,0:T(8,128)(2,1)S(1)}, u32[]{:S(2)}, u32[]{:S(2)}) collective-permute-start(bf16[288,512]{1,0:T(8,128)(2,1)S(1)} %get-tuple-element.74), channel_id=1, source_target_pairs={{1,2},{2,1},{5,6},{6,5},{9,10},{10,9},{13,14},{14,13},{17,18},{18,... | collective-permute-start | bytes 884744 | tf_op jit(solution)/shard_map/ppermute | solution.py:373
  44.6 3.2 %collective-permute-done.11.refs_9_.even_ref = bf16[288,512]{1,0:T(8,128)(2,1)S(1)} collective-permute-done((bf16[288,512]{1,0:T(8,128)(2,1)S(1)}, bf16[288,512]{1,0:T(8,128)(2,1)S(1)}, u32[]{:S(2)}, u32[]{:S(2)}) %collective-permute-start.11) | collective-permute-done | bytes 294944 | tf_op jit(solution)/shard_map/ppermute | solution.py:373
  47.9 0.1 shard_map.188
  48.0 2.2 %collective-permute-start.15 = (bf16[288,512]{1,0:T(8,128)(2,1)S(1)}, bf16[288,512]{1,0:T(8,128)(2,1)S(1)}, u32[]{:S(2)}, u32[]{:S(2)}) collective-permute-start(bf16[288,512]{1,0:T(8,128)(2,1)S(1)} %get-tuple-element.71), channel_id=1, source_target_pairs={{0,1},{1,0},{2,3},{3,2},{4,5},{5,4},{6,7},{7,6},{8,9},{9,8},{10,11... | collective-permute-start | bytes 884744 | tf_op jit(solution)/shard_map/ppermute | solution.py:373
  50.1 0.7 %collective-permute-start.16 = (bf16[288,512]{1,0:T(8,128)(2,1)S(1)}, bf16[288,512]{1,0:T(8,128)(2,1)S(1)}, u32[]{:S(2)}, u32[]{:S(2)}) collective-permute-start(bf16[288,512]{1,0:T(8,128)(2,1)S(1)} %get-tuple-element.72), channel_id=1, source_target_pairs={{1,2},{2,1},{5,6},{6,5},{9,10},{10,9},{13,14},{14,13},{17,18},{18,... | collective-permute-start | bytes 884744 | tf_op jit(solution)/shard_map/ppermute | solution.py:373
  50.8 0.0 copy-start.3
  50.8 0.0 copy-start.4
  50.8 1.8 %shard_map.186 = bf16[1,256,512]{2,1,0:T(8,128)(2,1)} custom-call(bf16[1,256,2304]{2,1,0:T(8,128)(2,1)S(1)} %get-tuple-element.49.inputs_ref, f32[256,128]{1,0:T(8,128)S(1)} %get-tuple-element.50.rms_ref, bf16[1,576,512]{2,1,0:T(8,128)(2,1)S(1)} %copy-done, f32[576,128]{1,0:T(8,128)S(1)} %get-tuple-element.51.spread_ref, ...), custom_call_target="tpu_custom_call" | custom-call | tf_op jit(solution)/shard_map/pallas_call | solution.py:65
  52.6 0.1 copy-done.4
  52.7 2.8 %shard_map.190 = (f32[2,1536,128]{2,1,0:T(8,128)}, f32[2,1536,128]{2,1,0:T(8,128)}) custom-call(bf16[1536,128]{1,0:T(8,128)(2,1)S(1)} %shard_map.187.own_ref, bf16[1536,128]{1,0:T(8,128)(2,1)S(1)} %collective-permute-done.19.other_ref, f32[2,1536,128]{2,1,0:T(8,128)S(1)} %bitcast.4, f32[2,1536,128]{2,1,0:T(8,128)S(1)} %bitcast.5), custom_call_target="tpu_custom_call" | custom-call | tf_op jit(solution)/shard_map/pallas_call | solution.py:65
  55.6 0.0 copy-start.5
  55.6 0.0 copy-start.6
  55.6 0.0 copy-start.7
  55.6 1.9 %shard_map.191 = (f32[288,128]{1,0:T(8,128)S(1)}, bf16[1,576,512]{2,1,0:T(8,128)(2,1)}, f32[1,576,512]{2,1,0:T(8,128)}, f32[1,576,512]{2,1,0:T(8,128)}) custom-call(f32[576,128]{1,0:T(8,128)S(1)} %get-tuple-element.51.spread_ref, bf16[1,576,512]{2,1,0:T(8,128)(2,1)S(1)} %copy-done, f32[1,576,512]{2,1,0:T(8,128)S(1)} %copy-done.1, ...), custom_call_target="tpu_custom_call" | custom-call | tf_op jit(solution)/shard_map/pallas_call | solution.py:65
  57.5 2.5 %collective-permute-done.15.refs_0_ = bf16[288,512]{1,0:T(8,128)(2,1)S(1)} collective-permute-done((bf16[288,512]{1,0:T(8,128)(2,1)S(1)}, bf16[288,512]{1,0:T(8,128)(2,1)S(1)}, u32[]{:S(2)}, u32[]{:S(2)}) %collective-permute-start.15) | collective-permute-done | bytes 294944 | tf_op jit(solution)/shard_map/ppermute | solution.py:373
  60.1 2.2 %shard_map.192 = (bf16[1,576,512]{2,1,0:T(8,128)(2,1)}, f32[1,576,512]{2,1,0:T(8,128)}, f32[1,576,512]{2,1,0:T(8,128)}, f32[1,576]{1,0:T(1,128)}, f32[1,576]{1,0:T(1,128)}, /*index=5*/f32[1,576]{1,0:T(1,128)}) custom-call(f32[576,128]{1,0:T(8,128)S(1)} %get-tuple-element.51.spread_ref, ...), custom_call_target="tpu_custom_call", output_to_operand_aliasing={{0}: (11, {}), {1}: (12, {}), {2}: (13, {})} | custom-call | tf_op jit(solution)/shard_map/pallas_call | solution.py:65
  (23 shorter events, 0.1 us)
Async XLA Ops:
  0.6 12.7 %collective-permute-start.5 = (bf16[1,393216]{1,0:T(2,128)(2,1)}, bf16[1,393216]{1,0:T(2,128)(2,1)S(1)}, u32[]{:S(2)}, u32[]{:S(2)}) collective-permute-start(bf16[1,393216]{1,0:T(2,128)(2,1)} %mine_ref), channel_id=1, source_target_pairs={{0,4},{4,0},{8,12},{12,8},{16,20},{20,16},{24,28},{28,24},{1,5},{5... | collective-permute-start | bytes 2359304 | tf_op jit(solution)/shard_map/ppermute | solution.py:286
  2.3 14.1 %collective-permute-start.2 = (bf16[288,512]{1,0:T(8,128)(2,1)S(1)}, bf16[288,512]{1,0:T(8,128)(2,1)S(1)}, u32[]{:S(2)}, u32[]{:S(2)}) collective-permute-start(bf16[288,512]{1,0:T(8,128)(2,1)S(1)} %get-tuple-element.52), channel_id=1, source_target_pairs={{1,2},{2,1},{5,6},{6,5},{9,10},{10,9},{13,14},{14,13},{17,18},{18,... | collective-permute-start | bytes 884744 | tf_op jit(solution)/shard_map/ppermute | solution.py:373
  3.0 13.4 %collective-permute-start = (bf16[288,512]{1,0:T(8,128)(2,1)S(1)}, bf16[288,512]{1,0:T(8,128)(2,1)S(1)}, u32[]{:S(2)}, u32[]{:S(2)}) collective-permute-start(bf16[288,512]{1,0:T(8,128)(2,1)S(1)} %get-tuple-element.52), channel_id=1, source_target_pairs={{0,1},{1,0},{2,3},{3,2},{4,5},{5,4},{6,7},{7,6},{8,9},{9,8},{10,11... | collective-permute-start | bytes 884744 | tf_op jit(solution)/shard_map/ppermute | solution.py:373
  8.5 10.6 %collective-permute-start.3 = (bf16[288,512]{1,0:T(8,128)(2,1)S(1)}, bf16[288,512]{1,0:T(8,128)(2,1)S(1)}, u32[]{:S(2)}, u32[]{:S(2)}) collective-permute-start(bf16[288,512]{1,0:T(8,128)(2,1)S(1)} %get-tuple-element.53), channel_id=1, source_target_pairs={{1,2},{2,1},{5,6},{6,5},{9,10},{10,9},{13,14},{14,13},{17,18},{18,... | collective-permute-start | bytes 884744 | tf_op jit(solution)/shard_map/ppermute | solution.py:373
  9.1 13.4 %collective-permute-start.1 = (bf16[288,512]{1,0:T(8,128)(2,1)S(1)}, bf16[288,512]{1,0:T(8,128)(2,1)S(1)}, u32[]{:S(2)}, u32[]{:S(2)}) collective-permute-start(bf16[288,512]{1,0:T(8,128)(2,1)S(1)} %get-tuple-element.53), channel_id=1, source_target_pairs={{0,1},{1,0},{2,3},{3,2},{4,5},{5,4},{6,7},{7,6},{8,9},{9,8},{10,11... | collective-permute-start | bytes 884744 | tf_op jit(solution)/shard_map/ppermute | solution.py:373
  14.9 10.7 %collective-permute-start.10 = (bf16[1536,128]{1,0:T(8,128)(2,1)S(1)}, bf16[1536,128]{1,0:T(8,128)(2,1)S(1)}, u32[]{:S(2)}, u32[]{:S(2)}) collective-permute-start(bf16[1536,128]{1,0:T(8,128)(2,1)S(1)} %shard_map.181.left_ref), channel_id=1, source_target_pairs={{0,8},{4,12},{8,0},{12,4},{16,24},{20,28},{24,16},{28,20},{1,9},{5... | collective-permute-start | bytes 1179656 | tf_op jit(solution)/shard_map/ppermute | solution.py:286
  16.5 12.3 %collective-permute-start.4 = (bf16[288,512]{1,0:T(8,128)(2,1)S(1)}, bf16[288,512]{1,0:T(8,128)(2,1)S(1)}, u32[]{:S(2)}, u32[]{:S(2)}) collective-permute-start(bf16[288,512]{1,0:T(8,128)(2,1)S(1)} %get-tuple-element.55), channel_id=1, source_target_pairs={{0,1},{1,0},{2,3},{3,2},{4,5},{5,4},{6,7},{7,6},{8,9},{9,8},{10,11... | collective-permute-start | bytes 884744 | tf_op jit(solution)/shard_map/ppermute | solution.py:373
  18.4 10.5 %collective-permute-start.7 = (bf16[288,512]{1,0:T(8,128)(2,1)S(1)}, bf16[288,512]{1,0:T(8,128)(2,1)S(1)}, u32[]{:S(2)}, u32[]{:S(2)}) collective-permute-start(bf16[288,512]{1,0:T(8,128)(2,1)S(1)} %get-tuple-element.61), channel_id=1, source_target_pairs={{1,2},{2,1},{5,6},{6,5},{9,10},{10,9},{13,14},{14,13},{17,18},{18,... | collective-permute-start | bytes 884744 | tf_op jit(solution)/shard_map/ppermute | solution.py:373
  22.7 12.5 %collective-permute-start.6 = (bf16[288,512]{1,0:T(8,128)(2,1)S(1)}, bf16[288,512]{1,0:T(8,128)(2,1)S(1)}, u32[]{:S(2)}, u32[]{:S(2)}) collective-permute-start(bf16[288,512]{1,0:T(8,128)(2,1)S(1)} %get-tuple-element.60), channel_id=1, source_target_pairs={{0,1},{1,0},{2,3},{3,2},{4,5},{5,4},{6,7},{7,6},{8,9},{9,8},{10,11... | collective-permute-start | bytes 884744 | tf_op jit(solution)/shard_map/ppermute | solution.py:373
  24.7 10.5 %collective-permute-start.8 = (bf16[288,512]{1,0:T(8,128)(2,1)S(1)}, bf16[288,512]{1,0:T(8,128)(2,1)S(1)}, u32[]{:S(2)}, u32[]{:S(2)}) collective-permute-start(bf16[288,512]{1,0:T(8,128)(2,1)S(1)} %get-tuple-element.62), channel_id=1, source_target_pairs={{1,2},{2,1},{5,6},{6,5},{9,10},{10,9},{13,14},{14,13},{17,18},{18,... | collective-permute-start | bytes 884744 | tf_op jit(solution)/shard_map/ppermute | solution.py:373
  25.7 12.4 %collective-permute-start.14 = (bf16[1536,128]{1,0:T(8,128)(2,1)S(1)}, bf16[1536,128]{1,0:T(8,128)(2,1)S(1)}, u32[]{:S(2)}, u32[]{:S(2)}) collective-permute-start(bf16[1536,128]{1,0:T(8,128)(2,1)S(1)} %shard_map.184.left_ref), channel_id=1, source_target_pairs={{0,16},{4,20},{8,24},{12,28},{16,0},{20,4},{24,8},{28,12},{1,17},{... | collective-permute-start | bytes 1179656 | tf_op jit(solution)/shard_map/ppermute | solution.py:286
  29.0 12.5 %collective-permute-start.9 = (bf16[288,512]{1,0:T(8,128)(2,1)S(1)}, bf16[288,512]{1,0:T(8,128)(2,1)S(1)}, u32[]{:S(2)}, u32[]{:S(2)}) collective-permute-start(bf16[288,512]{1,0:T(8,128)(2,1)S(1)} %get-tuple-element.63), channel_id=1, source_target_pairs={{0,1},{1,0},{2,3},{3,2},{4,5},{5,4},{6,7},{7,6},{8,9},{9,8},{10,11... | collective-permute-start | bytes 884744 | tf_op jit(solution)/shard_map/ppermute | solution.py:373
  31.1 10.4 %collective-permute-start.12 = (bf16[288,512]{1,0:T(8,128)(2,1)S(1)}, bf16[288,512]{1,0:T(8,128)(2,1)S(1)}, u32[]{:S(2)}, u32[]{:S(2)}) collective-permute-start(bf16[288,512]{1,0:T(8,128)(2,1)S(1)} %get-tuple-element.67), channel_id=1, source_target_pairs={{1,2},{2,1},{5,6},{6,5},{9,10},{10,9},{13,14},{14,13},{17,18},{18,... | collective-permute-start | bytes 884744 | tf_op jit(solution)/shard_map/ppermute | solution.py:373
  35.3 12.5 %collective-permute-start.11 = (bf16[288,512]{1,0:T(8,128)(2,1)S(1)}, bf16[288,512]{1,0:T(8,128)(2,1)S(1)}, u32[]{:S(2)}, u32[]{:S(2)}) collective-permute-start(bf16[288,512]{1,0:T(8,128)(2,1)S(1)} %get-tuple-element.66), channel_id=1, source_target_pairs={{0,1},{1,0},{2,3},{3,2},{4,5},{5,4},{6,7},{7,6},{8,9},{9,8},{10,11... | collective-permute-start | bytes 884744 | tf_op jit(solution)/shard_map/ppermute | solution.py:373
  37.4 10.4 %collective-permute-start.13 = (bf16[288,512]{1,0:T(8,128)(2,1)S(1)}, bf16[288,512]{1,0:T(8,128)(2,1)S(1)}, u32[]{:S(2)}, u32[]{:S(2)}) collective-permute-start(bf16[288,512]{1,0:T(8,128)(2,1)S(1)} %get-tuple-element.68), channel_id=1, source_target_pairs={{1,2},{2,1},{5,6},{6,5},{9,10},{10,9},{13,14},{14,13},{17,18},{18,... | collective-permute-start | bytes 884744 | tf_op jit(solution)/shard_map/ppermute | solution.py:373
  38.2 14.4 %collective-permute-start.19 = (bf16[1536,128]{1,0:T(8,128)(2,1)S(1)}, bf16[1536,128]{1,0:T(8,128)(2,1)S(1)}, u32[]{:S(2)}, u32[]{:S(2)}) collective-permute-start(bf16[1536,128]{1,0:T(8,128)(2,1)S(1)} %shard_map.187.own_ref), channel_id=1, source_target_pairs={{0,4},{4,0},{8,12},{12,8},{16,20},{20,16},{24,28},{28,24},{1,5},{5... | collective-permute-start | bytes 1179656 | tf_op jit(solution)/shard_map/ppermute | solution.py:286
  41.6 13.9 %collective-permute-start.17 = (bf16[288,512]{1,0:T(8,128)(2,1)S(1)}, bf16[288,512]{1,0:T(8,128)(2,1)S(1)}, u32[]{:S(2)}, u32[]{:S(2)}) collective-permute-start(bf16[288,512]{1,0:T(8,128)(2,1)S(1)} %get-tuple-element.73), channel_id=1, source_target_pairs={{0,1},{1,0},{2,3},{3,2},{4,5},{5,4},{6,7},{7,6},{8,9},{9,8},{10,11... | collective-permute-start | bytes 884744 | tf_op jit(solution)/shard_map/ppermute | solution.py:373
  43.8 7.0 %copy-start = (bf16[1,576,512]{2,1,0:T(8,128)(2,1)S(1)}, bf16[1,576,512]{2,1,0:T(8,128)(2,1)}, u32[]{:S(2)}) copy-start(bf16[1,576,512]{2,1,0:T(8,128)(2,1)} %weight_ref.7) | copy-start | bytes 1769476
  43.8 11.7 %collective-permute-start.18 = (bf16[288,512]{1,0:T(8,128)(2,1)S(1)}, bf16[288,512]{1,0:T(8,128)(2,1)S(1)}, u32[]{:S(2)}, u32[]{:S(2)}) collective-permute-start(bf16[288,512]{1,0:T(8,128)(2,1)S(1)} %get-tuple-element.74), channel_id=1, source_target_pairs={{1,2},{2,1},{5,6},{6,5},{9,10},{10,9},{13,14},{14,13},{17,18},{18,... | collective-permute-start | bytes 884744 | tf_op jit(solution)/shard_map/ppermute | solution.py:373
  48.0 12.1 %collective-permute-start.15 = (bf16[288,512]{1,0:T(8,128)(2,1)S(1)}, bf16[288,512]{1,0:T(8,128)(2,1)S(1)}, u32[]{:S(2)}, u32[]{:S(2)}) collective-permute-start(bf16[288,512]{1,0:T(8,128)(2,1)S(1)} %get-tuple-element.71), channel_id=1, source_target_pairs={{0,1},{1,0},{2,3},{3,2},{4,5},{5,4},{6,7},{7,6},{8,9},{9,8},{10,11... | collective-permute-start | bytes 884744 | tf_op jit(solution)/shard_map/ppermute | solution.py:373
  50.1 10.0 %collective-permute-start.16 = (bf16[288,512]{1,0:T(8,128)(2,1)S(1)}, bf16[288,512]{1,0:T(8,128)(2,1)S(1)}, u32[]{:S(2)}, u32[]{:S(2)}) collective-permute-start(bf16[288,512]{1,0:T(8,128)(2,1)S(1)} %get-tuple-element.72), channel_id=1, source_target_pairs={{1,2},{2,1},{5,6},{6,5},{9,10},{10,9},{13,14},{14,13},{17,18},{18,... | collective-permute-start | bytes 884744 | tf_op jit(solution)/shard_map/ppermute | solution.py:373
  50.8 1.8 %copy-start.3 = (f32[393216]{0:T(1024)S(1)}, f32[393216]{0:T(1024)}, u32[]{:S(2)}) copy-start(f32[393216]{0:T(1024)} %param.20) | copy-start | bytes 4718596
  50.8 1.9 %copy-start.4 = (f32[393216]{0:T(1024)S(1)}, f32[393216]{0:T(1024)}, u32[]{:S(2)}) copy-start(f32[393216]{0:T(1024)} %param.21) | copy-start | bytes 4718596
  52.7 2.9 %copy-start.1 = (f32[1,576,512]{2,1,0:T(8,128)S(1)}, f32[1,576,512]{2,1,0:T(8,128)}, u32[]{:S(2)}) copy-start(f32[1,576,512]{2,1,0:T(8,128)} %first_ref.3) | copy-start | bytes 3538948
  52.7 2.9 %copy-start.2 = (f32[1,576,512]{2,1,0:T(8,128)S(1)}, f32[1,576,512]{2,1,0:T(8,128)}, u32[]{:S(2)}) copy-start(f32[1,576,512]{2,1,0:T(8,128)} %second_ref.3) | copy-start | bytes 3538948
  55.6 4.5 %copy-start.5 = (f32[1,576]{1,0:T(1,128)S(1)}, f32[1,576]{1,0:T(1,128)}, u32[]{:S(2)}) copy-start(f32[1,576]{1,0:T(1,128)} %refs_3_.1) | copy-start | bytes 6916
  55.6 4.5 %copy-start.6 = (f32[1,576]{1,0:T(1,128)S(1)}, f32[1,576]{1,0:T(1,128)}, u32[]{:S(2)}) copy-start(f32[1,576]{1,0:T(1,128)} %refs_4_.1) | copy-start | bytes 6916
  55.6 4.5 %copy-start.7 = (f32[1,576]{1,0:T(1,128)S(1)}, f32[1,576]{1,0:T(1,128)}, u32[]{:S(2)}) copy-start(f32[1,576]{1,0:T(1,128)} %refs_5_.1) | copy-start | bytes 6916

commit v4 on v3

--- a/solution.py
+++ b/solution.py
@@ -20,17 +20,15 @@
 outer_rate = 0.7
 root_scale = 1.0 / math.sqrt(corr_two)
 rate_scale = learn_rate / corr_one
-chunk_count = 2
+chunk_parts = (1, 1)
+adam_rows = 512
 lanes = 128
 vmem_limit = 12 * 1024 * 1024
-moved_scale, moved_partial, moved_pair, moved_sum = 0, 0, 0, 0
-moved_onward, moved_keys, moved_adam, moved_outer = 0, 0, 0, 0
 
 wide = jnp.float32
 narrow = jnp.bfloat16
 VMEM = pl.BlockSpec(memory_space=pltpu.VMEM)
 HBM = pl.BlockSpec(memory_space=pltpu.HBM)
-held_shape = pltpu.VMEM
 
 
 def adam_step(params, gradient, first_moment, second_moment):
@@ -46,6 +44,14 @@
     return (new_params, new_mom)
 
 
+def split_rows(rows, unit=16):
+    units, whole, ends = rows // unit, sum(chunk_parts), [0]
+    for k in range(1, len(chunk_parts)):
+        ends.append(units * sum(chunk_parts[:k]) // whole * unit)
+    ends.append(rows)
+    return [(a, b - a) for a, b in zip(ends, ends[1:]) if b > a]
+
+
 def core_of_chip():
     return lax.axis_index("silo") & 1
 
@@ -61,7 +67,7 @@
     return 1
 
 
-def call(kernel, out_shape, inputs, moved=0, scratch=(), aliases=None, specs=None, outs=None, grid=(), limit=vmem_limit):
+def call(kernel, out_shape, inputs, scratch=(), aliases=None, specs=None, outs=None, grid=()):
     return pl.pallas_call(
         kernel,
         out_shape=out_shape,
@@ -69,23 +75,22 @@
         in_specs=specs if specs is not None else [VMEM] * len(inputs),
         out_specs=outs if outs is not None else jax.tree.map(lambda _: VMEM, out_shape),
         scratch_shapes=list(scratch),
-        compiler_params=pltpu.CompilerParams(vmem_limit_bytes=limit),
-        cost_estimate=pl.CostEstimate(flops=0, bytes_accessed=moved, transcendentals=0) if moved else None,
+        compiler_params=pltpu.CompilerParams(vmem_limit_bytes=vmem_limit),
 
         input_output_aliases=aliases or {},
     )(*inputs)
 
 
 def scale_kernel(chunks, weight_ref, gain_ref, spread_ref, *refs):
-    sent_refs, (held, gain_held, sems) = refs[:chunks], refs[chunks:]
+    count = len(chunks)
+    sent_refs, (held, gain_held, sems) = refs[: 2 * count], refs[2 * count :]
     rows = weight_ref.shape[1]
-    depth = rows // chunks
-    spans = [slice(c * depth, (c + 1) * depth) for c in range(chunks)]
+    spans = [slice(start, start + depth) for start, depth in chunks]
     copies = [
         pltpu.make_async_copy(weight_ref.at[0, span], held.at[span], sems.at[c])
         for c, span in enumerate(spans)
     ]
-    gain_copy = pltpu.make_async_copy(gain_ref, gain_held, sems.at[chunks])
+    gain_copy = pltpu.make_async_copy(gain_ref, gain_held, sems.at[count])
     for copy in (gain_copy, *copies):
         copy.start()
     gain_copy.wait()
@@ -96,7 +101,9 @@
         copies[c].wait()
         for k in range(weight_ref.shape[2] // lanes):
             part = slice(k * lanes, (k + 1) * lanes)
-            sent_refs[c][:, part] = (held[span, part].astype(wide) * used[span]).astype(narrow)
+            piece = (held[span, part].astype(wide) * used[span]).astype(narrow)
+            sent_refs[2 * c][:, part] = piece
+            sent_refs[2 * c + 1][:, part] = piece
 
 
 def partial_kernel(inputs_ref, cot_ref, partial_ref, rms_ref, held_ref, cot_held, sems):
@@ -125,7 +132,7 @@
         ).astype(narrow)
 
 
-def onward_kernel(n, c, chunks, s, partial_ref, even_ref, odd_ref, to_even_ref, to_odd_ref):
+def onward_kernel(n, rows, first, s, partial_ref, even_ref, odd_ref, to_even_ref, to_odd_ref):
     me = lax.axis_index("fsdp")
     depth = even_ref.shape[0]
     even = (me & 1) == 0
@@ -138,7 +145,7 @@
 
         @pl.when(s > place)
         def _():
-            start = pl.multiple_of((owner * chunks + c) * depth, 16)
+            start = pl.multiple_of(owner * rows + first, 16)
             sent_ref[...] = add_narrow(came_ref[...], partial_ref[pl.ds(start, depth), :])
 
         @pl.when(s <= place)
@@ -150,7 +157,6 @@
     got, (keys_ref, weights) = refs[:-2], refs[-2:]
     me = lax.axis_index("fsdp")
     rows, cols = weight_ref.shape[1:]
-    depth = rows // chunks
     used = spread_ref[...].astype(narrow).astype(wide)
     for k in range(cols // lanes):
         part = slice(k * lanes, (k + 1) * lanes)
@@ -159,7 +165,8 @@
         ).astype(narrow)
 
     def put(block, c, ref):
-        weights[pl.ds(pl.multiple_of(block * rows + c * depth, 16), depth), :] = ref[...]
+        first, depth = chunks[c]
+        weights[pl.ds(pl.multiple_of(block * rows + first, 16), depth), :] = ref[...]
 
     even = (me & 1) == 0
     for s in range(n - 1):
@@ -169,8 +176,8 @@
 
             @pl.when((block >= 0) & (block < n))
             def _():
-                for c in range(chunks):
-                    put(block, c, got[(s * 2 + w) * chunks + c])
+                for c in range(len(chunks)):
+                    put(block, c, got[(s * 2 + w) * len(chunks) + c])
 
     total = jnp.dot(inputs_ref[0], weights[...], preferred_element_type=wide)
     for k in range(cols // lanes):
@@ -191,7 +198,7 @@
 
 
 def adam_kernel(c, chunks, spread_ref, weight_ref, first_ref, second_ref, partial_ref, *refs):
-    last = c == chunks - 1
+    last = c == len(chunks) - 1
     came = refs[:2]
     if last:
         shares, gains = refs[2 : 2 + c], refs[2 + c : 5 + c]
@@ -201,7 +208,8 @@
         share_ref, new_weight_ref, new_first_ref, new_second_ref = refs[-4:]
     depth, cols = weight_ref.shape[1:]
     step, steps = pl.program_id(0), pl.num_programs(0)
-    start = pl.multiple_of(((lax.axis_index("fsdp") * chunks + c) * steps + step) * depth, 16)
+    whole = sum(size for _, size in chunks)
+    start = pl.multiple_of(lax.axis_index("fsdp") * whole + chunks[c][0] + step * depth, 16)
     share = jnp.zeros((depth, lanes), wide)
     used = spread_ref[...].astype(narrow).astype(wide)
     for k in range(cols // lanes):
@@ -224,8 +232,8 @@
 
     @pl.when(step == steps - 1)
     def _():
-        whole = jnp.concatenate([ref[...] for ref in (*shares, share_ref)], axis=0)
-        gradient = jnp.sum(whole.T, axis=0, keepdims=True)
+        joined = jnp.concatenate([ref[...] for ref in (*shares, share_ref)], axis=0)
+        gradient = jnp.sum(joined.T, axis=0, keepdims=True)
         for ref, value in zip(new_gains, adam_step(gains[0][...], gradient, gains[1][...], gains[2][...])):
             ref[...] = value
 
@@ -285,19 +293,18 @@
     def swap(part, bit):
         return lax.ppermute(part, "silo", [(i, i ^ bit) for i in range(silos)])
 
-    part = held_shape((half, lanes), narrow)
+    part = pltpu.VMEM((half, lanes), narrow)
     total = call(
         pair_kernel,
         part,
         pair_operands(*tie([pseudo_grad, swap(pseudo_grad, 1)], after)),
-        moved=moved_pair,
         specs=[HBM, HBM],
         scratch=[pltpu.VMEM((1, half * lanes), narrow)] * 2 + [pltpu.SemaphoreType.DMA((2,))],
     )
     yield total
     bit = 2
     while bit < silos:
-        total = call(sum_kernel, part, in_vmem([total, swap(total, bit)]), moved=moved_sum)
+        total = call(sum_kernel, part, in_vmem([total, swap(total, bit)]))
         yield total
         bit *= 2
     other = swap(total, 1)
@@ -308,7 +315,6 @@
         functools.partial(nesterov_kernel, silos),
         [jax.ShapeDtypeStruct((2, half, lanes), wide)] * 2,
         [total, other, outer_params.reshape(2, half, lanes), outer_mom.reshape(2, half, lanes)],
-        moved=moved_outer,
         specs=[line, line, block, block],
         outs=[block, block],
         grid=(2, steps),
@@ -332,20 +338,20 @@
     ):
         tokens, feats = activations.shape[1:]
         rows, cols = key_weight.shape[1:]
-        chunks = chunk_count if rows % (16 * chunk_count) == 0 else 1
-        depth = rows // chunks
+        chunks = split_rows(rows)
+        count = len(chunks)
         shape = jax.ShapeDtypeStruct
 
         spread, *own = call(
             functools.partial(scale_kernel, chunks),
-            [held_shape((rows, lanes), wide)] + [held_shape((depth, cols), narrow)] * chunks,
+            [pltpu.VMEM((rows, lanes), wide)]
+            + [pltpu.VMEM((depth, cols), narrow) for _, depth in chunks for _ in range(2)],
             [in_hbm(key_weight), in_hbm(norm_gain)],
-            moved=moved_scale,
             specs=[HBM, HBM],
             scratch=[
                 pltpu.VMEM((rows, cols), narrow),
                 pltpu.VMEM((1, rows), wide),
-                pltpu.SemaphoreType.DMA((chunks + 1,)),
+                pltpu.SemaphoreType.DMA((count + 1,)),
             ],
         )
         links = [
@@ -354,19 +360,18 @@
         ]
         slots = []
         for s in range(n):
-            got = [[None for _ in range(chunks)] for _ in links]
-            for c in range(chunks):
-                sent = [own[c], own[c]]
+            got = [[None for _ in range(count)] for _ in links]
+            for c, (_, depth) in enumerate(chunks):
+                sent = own[2 * c : 2 * c + 2]
                 if s > 0:
                     came = [slots[-1][w][c] for w in range(2)]
-                    if c == chunks - 1:
+                    if c == count - 1:
                         outer_part = next(outer, outer_part)
                         came = tie(came, outer_part)
                     sent = call(
-                        functools.partial(onward_kernel, n, c, chunks, s),
-                        [held_shape((depth, cols), narrow)] * 2,
+                        functools.partial(onward_kernel, n, rows, chunks[c][0], s),
+                        [pltpu.VMEM((depth, cols), narrow)] * 2,
                         [partial, *in_vmem(came)],
-                        moved=moved_onward,
                         specs=[VMEM] * 3,
                     )
                 for w in range(2):
@@ -376,12 +381,11 @@
                 partial, inv_rms, inputs = call(
                     partial_kernel,
                     [
-                        held_shape((feats, cols), narrow),
-                        held_shape((tokens, lanes), wide),
-                        held_shape(activations.shape, narrow),
+                        pltpu.VMEM((feats, cols), narrow),
+                        pltpu.VMEM((tokens, lanes), wide),
+                        pltpu.VMEM(activations.shape, narrow),
                     ],
                     [in_hbm(activations), in_hbm(key_cot)],
-                    moved=moved_partial,
                     specs=[HBM, HBM],
                     scratch=[pltpu.VMEM(key_cot.shape, narrow), pltpu.SemaphoreType.DMA((2,))],
                 )
@@ -392,43 +396,42 @@
             functools.partial(keys_kernel, n, chunks),
             shape((1, tokens, cols), narrow),
             [inputs, inv_rms, key_weight, spread]
-            + [slots[s][w][c] for s in range(n - 1) for w in range(2) for c in range(chunks)],
-            moved=moved_keys,
+            + [slots[s][w][c] for s in range(n - 1) for w in range(2) for c in range(count)],
             scratch=[pltpu.VMEM((feats, cols), narrow)],
-            specs=[VMEM] * (4 + (n - 1) * 2 * chunks),
+            specs=[VMEM] * (4 + (n - 1) * 2 * count),
         )
 
         for outer_part in outer:
             pass
         shares, news = [], []
-        steps = blocks_of(depth, 96, 16)
-        tall = depth // steps
-        for c in range(chunks):
+        unit = math.gcd(*[x for span in chunks for x in span])
+        for c, (first, depth) in enumerate(chunks):
+            tall = max(x for x in range(16, adam_rows + 1, 16) if unit % x == 0 or x == 16)
+            steps, before = depth // tall, first // tall
             came = [slots[n - 1][w][c] for w in range(2)]
             if c == 0:
                 came = tie(came, outer_part)
-            block = pl.BlockSpec((1, tall, cols), lambda i, c=c: (0, c * steps + i, 0))
-            last = c == chunks - 1
+            block = pl.BlockSpec((1, tall, cols), lambda i, before=before: (0, before + i, 0))
+            last = c == count - 1
             extra = [*shares, norm_gain, gain_first, gain_second] if last else []
             gain_outs = [shape((1, rows), wide)] * 3
-            count = len(extra)
+            extras = len(extra)
             outs = call(
                 functools.partial(adam_kernel, c, chunks),
                 ([] if last else [shape((depth, lanes), wide)])
                 + [shape((1, rows, cols), kind) for kind in (narrow, wide, wide)]
                 + (gain_outs if last else []),
                 [spread, key_weight, weight_first, weight_second, partial, *came, *extra, *news],
-                moved=moved_adam,
-                specs=[pl.BlockSpec((tall, lanes), lambda i, c=c: (c * steps + i, 0))]
+                specs=[pl.BlockSpec((tall, lanes), lambda i, before=before: (before + i, 0))]
                 + [block] * 3
                 + [VMEM]
                 + [pl.BlockSpec((tall, cols), lambda i: (i, 0))] * 2
-                + [VMEM] * count
+                + [VMEM] * extras
                 + [pl.BlockSpec(memory_space=pl.ANY)] * len(news),
                 outs=([] if last else [pl.BlockSpec((tall, lanes), lambda i: (i, 0))])
                 + [block] * 3
                 + ([VMEM] * 3 if last else []),
-                aliases={7 + count + i: (0 if last else 1) + i for i in range(len(news))},
+                aliases={7 + extras + i: (0 if last else 1) + i for i in range(len(news))},
                 scratch=[pltpu.VMEM((depth, lanes), wide)] if last else [],
                 grid=(steps,),
             )

time: 62.8 us -> 61.1 us (0.973)
  the two profiles are of different devices: /device:TPU:0 before, /device:TPU:8 now
where the time goes in v4:
time: 61.1 us; the launch traced here: 60.7 us
  starting transfers between devices  32.7 us (54%)
  Pallas kernels  13.6 us (22%)
  waiting for transfers between devices  13.3 us (22%)
  between operations  1.01 us (2%)
    ppermute x16, starting transfers between devices, per_device(): got[w][c] = lax.ppermute(sent[w], 'fsdp', links[w])  29.4 us
    pallas_call x15, Pallas kernels, call(): pl.pallas_call(kernel, out_shape=out_shape, grid=grid, in_specs=specs if...  13.6 us
    ppermute x16, waiting for transfers between devices, per_device(): got[w][c] = lax.ppermute(sent[w], 'fsdp', links[w])  13.3 us
    ppermute x4, starting transfers between devices, swap(): return lax.ppermute(part, 'silo', [(i, i ^ bit) for i in range(silos)])  3.29 us
  transfers between devices with their start and end apart: 20, of which 7 were waited for; matrix products, arithmetic and copies ran while one was open for 0% of the time, Pallas kernels for 20%

profile of v4, /device:TPU:8, one launch (start us, length us, event | category | flops | bytes accessed | tf_op | source)
XLA Modules:
  0.0 60.7 jit_solution(17462815656117587119)
XLA Ops:
  0.6 0.1 collective-permute-start.5
  0.7 1.2 %shard_map.179 = (f32[576,128]{1,0:T(8,128)S(1)}, bf16[288,512]{1,0:T(8,128)(2,1)S(1)}, bf16[288,512]{1,0:T(8,128)(2,1)S(1)}, bf16[288,512]{1,0:T(8,128)(2,1)S(1)}, bf16[288,512]{1,0:T(8,128)(2,1)S(1)}) custom-call(bf16[1,576,512]{2,1,0:T(8,128)(2,1)} %weight_ref.7, f32[1,576]{1,0:T(1,128)} %refs_3_.1), custom_call_target="tpu_custom_call" | custom-call | tf_op jit(solution)/shard_map/pallas_call | solution.py:71
  1.9 0.1 collective-permute-start
  2.0 2.0 %collective-permute-start.1 = (bf16[288,512]{1,0:T(8,128)(2,1)S(1)}, bf16[288,512]{1,0:T(8,128)(2,1)S(1)}, u32[]{:S(2)}, u32[]{:S(2)}) collective-permute-start(bf16[288,512]{1,0:T(8,128)(2,1)S(1)} %get-tuple-element.55), channel_id=1, source_target_pairs={{0,1},{1,0},{2,3},{3,2},{4,5},{5,4},{6,7},{7,6},{8,9},{9,8},{10,11... | collective-permute-start | bytes 884744 | tf_op jit(solution)/shard_map/ppermute | solution.py:378
  4.0 3.5 %collective-permute-start.2 = (bf16[288,512]{1,0:T(8,128)(2,1)S(1)}, bf16[288,512]{1,0:T(8,128)(2,1)S(1)}, u32[]{:S(2)}, u32[]{:S(2)}) collective-permute-start(bf16[288,512]{1,0:T(8,128)(2,1)S(1)} %get-tuple-element.56), channel_id=1, source_target_pairs={{1,2},{2,1},{5,6},{6,5},{9,10},{10,9},{13,14},{14,13},{17,18},{18,... | collective-permute-start | bytes 884744 | tf_op jit(solution)/shard_map/ppermute | solution.py:378
  7.5 2.4 %collective-permute-start.3 = (bf16[288,512]{1,0:T(8,128)(2,1)S(1)}, bf16[288,512]{1,0:T(8,128)(2,1)S(1)}, u32[]{:S(2)}, u32[]{:S(2)}) collective-permute-start(bf16[288,512]{1,0:T(8,128)(2,1)S(1)} %get-tuple-element.57), channel_id=1, source_target_pairs={{1,2},{2,1},{5,6},{6,5},{9,10},{10,9},{13,14},{14,13},{17,18},{18,... | collective-permute-start | bytes 884744 | tf_op jit(solution)/shard_map/ppermute | solution.py:378
  9.9 2.4 %shard_map.178 = (bf16[2304,512]{1,0:T(8,128)(2,1)S(1)}, f32[256,128]{1,0:T(8,128)S(1)}, bf16[1,256,2304]{2,1,0:T(8,128)(2,1)S(1)}) custom-call(bf16[1,256,2304]{2,1,0:T(8,128)(2,1)} %inputs_ref.1, bf16[1,256,512]{2,1,0:T(8,128)(2,1)} %cot_ref.1), custom_call_target="tpu_custom_call" | custom-call | tf_op jit(solution)/shard_map/pallas_call | solution.py:71
  12.3 0.0 collective-permute-done.5.other_ref
  12.3 1.5 %shard_map.181.left_ref = bf16[1536,128]{1,0:T(8,128)(2,1)S(1)} custom-call(bf16[1,393216]{1,0:T(2,128)(2,1)} %mine_ref, bf16[1,393216]{1,0:T(2,128)(2,1)S(1)} %collective-permute-done.5.other_ref), custom_call_target="tpu_custom_call" | custom-call | tf_op jit(solution)/shard_map/pallas_call | solution.py:71
  13.8 1.6 %collective-permute-start.10 = (bf16[1536,128]{1,0:T(8,128)(2,1)S(1)}, bf16[1536,128]{1,0:T(8,128)(2,1)S(1)}, u32[]{:S(2)}, u32[]{:S(2)}) collective-permute-start(bf16[1536,128]{1,0:T(8,128)(2,1)S(1)} %shard_map.181.left_ref), channel_id=1, source_target_pairs={{0,8},{4,12},{8,0},{12,4},{16,24},{20,28},{24,16},{28,20},{1,9},{5... | collective-permute-start | bytes 1179656 | tf_op jit(solution)/shard_map/ppermute | solution.py:294
  15.4 0.4 collective-permute-done.2.odd_ref.refs_2_
  15.8 0.1 collective-permute-start.4
  15.9 3.5 %collective-permute-start.7 = (bf16[288,512]{1,0:T(8,128)(2,1)S(1)}, bf16[288,512]{1,0:T(8,128)(2,1)S(1)}, u32[]{:S(2)}, u32[]{:S(2)}) collective-permute-start(bf16[288,512]{1,0:T(8,128)(2,1)S(1)} %get-tuple-element.65), channel_id=1, source_target_pairs={{1,2},{2,1},{5,6},{6,5},{9,10},{10,9},{13,14},{14,13},{17,18},{18,... | collective-permute-start | bytes 884744 | tf_op jit(solution)/shard_map/ppermute | solution.py:378
  19.4 2.7 %collective-permute-done.3.odd_ref.refs_3_ = bf16[288,512]{1,0:T(8,128)(2,1)S(1)} collective-permute-done((bf16[288,512]{1,0:T(8,128)(2,1)S(1)}, bf16[288,512]{1,0:T(8,128)(2,1)S(1)}, u32[]{:S(2)}, u32[]{:S(2)}) %collective-permute-start.3) | collective-permute-done | bytes 294944 | tf_op jit(solution)/shard_map/ppermute | solution.py:378
  22.1 0.1 collective-permute-start.6
  22.2 3.5 %collective-permute-start.8 = (bf16[288,512]{1,0:T(8,128)(2,1)S(1)}, bf16[288,512]{1,0:T(8,128)(2,1)S(1)}, u32[]{:S(2)}, u32[]{:S(2)}) collective-permute-start(bf16[288,512]{1,0:T(8,128)(2,1)S(1)} %get-tuple-element.66), channel_id=1, source_target_pairs={{1,2},{2,1},{5,6},{6,5},{9,10},{10,9},{13,14},{14,13},{17,18},{18,... | collective-permute-start | bytes 884744 | tf_op jit(solution)/shard_map/ppermute | solution.py:378
  25.7 0.1 shard_map.184.left_ref
  25.8 1.6 %collective-permute-start.14 = (bf16[1536,128]{1,0:T(8,128)(2,1)S(1)}, bf16[1536,128]{1,0:T(8,128)(2,1)S(1)}, u32[]{:S(2)}, u32[]{:S(2)}) collective-permute-start(bf16[1536,128]{1,0:T(8,128)(2,1)S(1)} %shard_map.184.left_ref), channel_id=1, source_target_pairs={{0,16},{4,20},{8,24},{12,28},{16,0},{20,4},{24,8},{28,12},{1,17},{... | collective-permute-start | bytes 1179656 | tf_op jit(solution)/shard_map/ppermute | solution.py:294
  27.4 1.0 %collective-permute-done.7.odd_ref.refs_6_ = bf16[288,512]{1,0:T(8,128)(2,1)S(1)} collective-permute-done((bf16[288,512]{1,0:T(8,128)(2,1)S(1)}, bf16[288,512]{1,0:T(8,128)(2,1)S(1)}, u32[]{:S(2)}, u32[]{:S(2)}) %collective-permute-start.7) | collective-permute-done | bytes 294944 | tf_op jit(solution)/shard_map/ppermute | solution.py:378
  28.4 0.1 shard_map.183
  28.5 0.1 collective-permute-start.9
  28.6 3.5 %collective-permute-start.12 = (bf16[288,512]{1,0:T(8,128)(2,1)S(1)}, bf16[288,512]{1,0:T(8,128)(2,1)S(1)}, u32[]{:S(2)}, u32[]{:S(2)}) collective-permute-start(bf16[288,512]{1,0:T(8,128)(2,1)S(1)} %get-tuple-element.71), channel_id=1, source_target_pairs={{1,2},{2,1},{5,6},{6,5},{9,10},{10,9},{13,14},{14,13},{17,18},{18,... | collective-permute-start | bytes 884744 | tf_op jit(solution)/shard_map/ppermute | solution.py:378
  32.1 2.6 %collective-permute-done.8.odd_ref.refs_7_ = bf16[288,512]{1,0:T(8,128)(2,1)S(1)} collective-permute-done((bf16[288,512]{1,0:T(8,128)(2,1)S(1)}, bf16[288,512]{1,0:T(8,128)(2,1)S(1)}, u32[]{:S(2)}, u32[]{:S(2)}) %collective-permute-start.8) | collective-permute-done | bytes 294944 | tf_op jit(solution)/shard_map/ppermute | solution.py:378
  34.7 0.1 shard_map.185
  34.8 0.1 collective-permute-start.11
  34.9 3.5 %collective-permute-start.13 = (bf16[288,512]{1,0:T(8,128)(2,1)S(1)}, bf16[288,512]{1,0:T(8,128)(2,1)S(1)}, u32[]{:S(2)}, u32[]{:S(2)}) collective-permute-start(bf16[288,512]{1,0:T(8,128)(2,1)S(1)} %get-tuple-element.72), channel_id=1, source_target_pairs={{1,2},{2,1},{5,6},{6,5},{9,10},{10,9},{13,14},{14,13},{17,18},{18,... | collective-permute-start | bytes 884744 | tf_op jit(solution)/shard_map/ppermute | solution.py:378
  38.4 0.1 shard_map.187.own_ref
  38.5 0.1 collective-permute-start.19
  38.6 2.4 %collective-permute-done.12.refs_10_.odd_ref = bf16[288,512]{1,0:T(8,128)(2,1)S(1)} collective-permute-done((bf16[288,512]{1,0:T(8,128)(2,1)S(1)}, bf16[288,512]{1,0:T(8,128)(2,1)S(1)}, u32[]{:S(2)}, u32[]{:S(2)}) %collective-permute-start.12) | collective-permute-done | bytes 294944 | tf_op jit(solution)/shard_map/ppermute | solution.py:378
  41.1 0.1 shard_map.189
  41.2 0.1 collective-permute-start.17
  41.3 0.0 copy-start
  41.3 3.6 %collective-permute-start.18 = (bf16[288,512]{1,0:T(8,128)(2,1)S(1)}, bf16[288,512]{1,0:T(8,128)(2,1)S(1)}, u32[]{:S(2)}, u32[]{:S(2)}) collective-permute-start(bf16[288,512]{1,0:T(8,128)(2,1)S(1)} %get-tuple-element.78), channel_id=1, source_target_pairs={{1,2},{2,1},{5,6},{6,5},{9,10},{10,9},{13,14},{14,13},{17,18},{18,... | collective-permute-start | bytes 884744 | tf_op jit(solution)/shard_map/ppermute | solution.py:378
  44.9 2.4 %collective-permute-done.13.refs_11_.odd_ref = bf16[288,512]{1,0:T(8,128)(2,1)S(1)} collective-permute-done((bf16[288,512]{1,0:T(8,128)(2,1)S(1)}, bf16[288,512]{1,0:T(8,128)(2,1)S(1)}, u32[]{:S(2)}, u32[]{:S(2)}) %collective-permute-start.13) | collective-permute-done | bytes 294944 | tf_op jit(solution)/shard_map/ppermute | solution.py:378
  47.4 0.1 shard_map.188
  47.5 0.1 collective-permute-start.15
  47.6 3.5 %collective-permute-start.16 = (bf16[288,512]{1,0:T(8,128)(2,1)S(1)}, bf16[288,512]{1,0:T(8,128)(2,1)S(1)}, u32[]{:S(2)}, u32[]{:S(2)}) collective-permute-start(bf16[288,512]{1,0:T(8,128)(2,1)S(1)} %get-tuple-element.76), channel_id=1, source_target_pairs={{1,2},{2,1},{5,6},{6,5},{9,10},{10,9},{13,14},{14,13},{17,18},{18,... | collective-permute-start | bytes 884744 | tf_op jit(solution)/shard_map/ppermute | solution.py:378
  51.1 0.0 copy-start.3
  51.1 0.0 copy-start.4
  51.1 1.8 %shard_map.186 = bf16[1,256,512]{2,1,0:T(8,128)(2,1)} custom-call(bf16[1,256,2304]{2,1,0:T(8,128)(2,1)S(1)} %get-tuple-element.51.inputs_ref, f32[256,128]{1,0:T(8,128)S(1)} %get-tuple-element.52.rms_ref, bf16[1,576,512]{2,1,0:T(8,128)(2,1)S(1)} %copy-done, f32[576,128]{1,0:T(8,128)S(1)} %get-tuple-element.53.spread_ref, ...), custom_call_target="tpu_custom_call" | custom-call | tf_op jit(solution)/shard_map/pallas_call | solution.py:71
  52.9 0.1 copy-done.4
  53.0 2.8 %shard_map.190 = (f32[2,1536,128]{2,1,0:T(8,128)}, f32[2,1536,128]{2,1,0:T(8,128)}) custom-call(bf16[1536,128]{1,0:T(8,128)(2,1)S(1)} %shard_map.187.own_ref, bf16[1536,128]{1,0:T(8,128)(2,1)S(1)} %collective-permute-done.19.other_ref, f32[2,1536,128]{2,1,0:T(8,128)S(1)} %bitcast.4, f32[2,1536,128]{2,1,0:T(8,128)S(1)} %bitcast.5), custom_call_target="tpu_custom_call" | custom-call | tf_op jit(solution)/shard_map/pallas_call | solution.py:71
  55.9 0.0 copy-start.5
  55.9 0.0 copy-start.6
  55.9 0.0 copy-start.7
  55.9 1.4 %shard_map.191 = (f32[288,128]{1,0:T(8,128)S(1)}, bf16[1,576,512]{2,1,0:T(8,128)(2,1)}, f32[1,576,512]{2,1,0:T(8,128)}, f32[1,576,512]{2,1,0:T(8,128)}) custom-call(f32[576,128]{1,0:T(8,128)S(1)} %get-tuple-element.53.spread_ref, bf16[1,576,512]{2,1,0:T(8,128)(2,1)S(1)} %copy-done, f32[1,576,512]{2,1,0:T(8,128)S(1)} %copy-done.1, ...), custom_call_target="tpu_custom_call" | custom-call | tf_op jit(solution)/shard_map/pallas_call | solution.py:71
  57.3 1.7 %collective-permute-done.16.refs_1_ = bf16[288,512]{1,0:T(8,128)(2,1)S(1)} collective-permute-done((bf16[288,512]{1,0:T(8,128)(2,1)S(1)}, bf16[288,512]{1,0:T(8,128)(2,1)S(1)}, u32[]{:S(2)}, u32[]{:S(2)}) %collective-permute-start.16) | collective-permute-done | bytes 294944 | tf_op jit(solution)/shard_map/ppermute | solution.py:378
  59.0 1.7 %shard_map.192 = (bf16[1,576,512]{2,1,0:T(8,128)(2,1)}, f32[1,576,512]{2,1,0:T(8,128)}, f32[1,576,512]{2,1,0:T(8,128)}, f32[1,576]{1,0:T(1,128)}, f32[1,576]{1,0:T(1,128)}, /*index=5*/f32[1,576]{1,0:T(1,128)}) custom-call(f32[576,128]{1,0:T(8,128)S(1)} %get-tuple-element.53.spread_ref, ...), custom_call_target="tpu_custom_call", output_to_operand_aliasing={{0}: (11, {}), {1}: (12, {}), {2}: (13, {})} | custom-call | tf_op jit(solution)/shard_map/pallas_call | solution.py:71
  (23 shorter events, 0.1 us)
Async XLA Ops:
  0.6 11.6 %collective-permute-start.5 = (bf16[1,393216]{1,0:T(2,128)(2,1)}, bf16[1,393216]{1,0:T(2,128)(2,1)S(1)}, u32[]{:S(2)}, u32[]{:S(2)}) collective-permute-start(bf16[1,393216]{1,0:T(2,128)(2,1)} %mine_ref), channel_id=1, source_target_pairs={{0,4},{4,0},{8,12},{12,8},{16,20},{20,16},{24,28},{28,24},{1,5},{5... | collective-permute-start | bytes 2359304 | tf_op jit(solution)/shard_map/ppermute | solution.py:294
  1.9 13.5 %collective-permute-start = (bf16[288,512]{1,0:T(8,128)(2,1)S(1)}, bf16[288,512]{1,0:T(8,128)(2,1)S(1)}, u32[]{:S(2)}, u32[]{:S(2)}) collective-permute-start(bf16[288,512]{1,0:T(8,128)(2,1)S(1)} %get-tuple-element.54), channel_id=1, source_target_pairs={{0,1},{1,0},{2,3},{3,2},{4,5},{5,4},{6,7},{7,6},{8,9},{9,8},{10,11... | collective-permute-start | bytes 884744 | tf_op jit(solution)/shard_map/ppermute | solution.py:378
  2.0 17.4 %collective-permute-start.1 = (bf16[288,512]{1,0:T(8,128)(2,1)S(1)}, bf16[288,512]{1,0:T(8,128)(2,1)S(1)}, u32[]{:S(2)}, u32[]{:S(2)}) collective-permute-start(bf16[288,512]{1,0:T(8,128)(2,1)S(1)} %get-tuple-element.55), channel_id=1, source_target_pairs={{0,1},{1,0},{2,3},{3,2},{4,5},{5,4},{6,7},{7,6},{8,9},{9,8},{10,11... | collective-permute-start | bytes 884744 | tf_op jit(solution)/shard_map/ppermute | solution.py:378
  4.0 11.8 %collective-permute-start.2 = (bf16[288,512]{1,0:T(8,128)(2,1)S(1)}, bf16[288,512]{1,0:T(8,128)(2,1)S(1)}, u32[]{:S(2)}, u32[]{:S(2)}) collective-permute-start(bf16[288,512]{1,0:T(8,128)(2,1)S(1)} %get-tuple-element.56), channel_id=1, source_target_pairs={{1,2},{2,1},{5,6},{6,5},{9,10},{10,9},{13,14},{14,13},{17,18},{18,... | collective-permute-start | bytes 884744 | tf_op jit(solution)/shard_map/ppermute | solution.py:378
  7.5 14.6 %collective-permute-start.3 = (bf16[288,512]{1,0:T(8,128)(2,1)S(1)}, bf16[288,512]{1,0:T(8,128)(2,1)S(1)}, u32[]{:S(2)}, u32[]{:S(2)}) collective-permute-start(bf16[288,512]{1,0:T(8,128)(2,1)S(1)} %get-tuple-element.57), channel_id=1, source_target_pairs={{1,2},{2,1},{5,6},{6,5},{9,10},{10,9},{13,14},{14,13},{17,18},{18,... | collective-permute-start | bytes 884744 | tf_op jit(solution)/shard_map/ppermute | solution.py:378
  13.8 11.9 %collective-permute-start.10 = (bf16[1536,128]{1,0:T(8,128)(2,1)S(1)}, bf16[1536,128]{1,0:T(8,128)(2,1)S(1)}, u32[]{:S(2)}, u32[]{:S(2)}) collective-permute-start(bf16[1536,128]{1,0:T(8,128)(2,1)S(1)} %shard_map.181.left_ref), channel_id=1, source_target_pairs={{0,8},{4,12},{8,0},{12,4},{16,24},{20,28},{24,16},{28,20},{1,9},{5... | collective-permute-start | bytes 1179656 | tf_op jit(solution)/shard_map/ppermute | solution.py:294
  15.8 11.6 %collective-permute-start.4 = (bf16[288,512]{1,0:T(8,128)(2,1)S(1)}, bf16[288,512]{1,0:T(8,128)(2,1)S(1)}, u32[]{:S(2)}, u32[]{:S(2)}) collective-permute-start(bf16[288,512]{1,0:T(8,128)(2,1)S(1)} %get-tuple-element.59), channel_id=1, source_target_pairs={{0,1},{1,0},{2,3},{3,2},{4,5},{5,4},{6,7},{7,6},{8,9},{9,8},{10,11... | collective-permute-start | bytes 884744 | tf_op jit(solution)/shard_map/ppermute | solution.py:378
  15.9 12.5 %collective-permute-start.7 = (bf16[288,512]{1,0:T(8,128)(2,1)S(1)}, bf16[288,512]{1,0:T(8,128)(2,1)S(1)}, u32[]{:S(2)}, u32[]{:S(2)}) collective-permute-start(bf16[288,512]{1,0:T(8,128)(2,1)S(1)} %get-tuple-element.65), channel_id=1, source_target_pairs={{1,2},{2,1},{5,6},{6,5},{9,10},{10,9},{13,14},{14,13},{17,18},{18,... | collective-permute-start | bytes 884744 | tf_op jit(solution)/shard_map/ppermute | solution.py:378
  22.1 9.9 %collective-permute-start.6 = (bf16[288,512]{1,0:T(8,128)(2,1)S(1)}, bf16[288,512]{1,0:T(8,128)(2,1)S(1)}, u32[]{:S(2)}, u32[]{:S(2)}) collective-permute-start(bf16[288,512]{1,0:T(8,128)(2,1)S(1)} %get-tuple-element.64), channel_id=1, source_target_pairs={{0,1},{1,0},{2,3},{3,2},{4,5},{5,4},{6,7},{7,6},{8,9},{9,8},{10,11... | collective-permute-start | bytes 884744 | tf_op jit(solution)/shard_map/ppermute | solution.py:378
  22.2 12.5 %collective-permute-start.8 = (bf16[288,512]{1,0:T(8,128)(2,1)S(1)}, bf16[288,512]{1,0:T(8,128)(2,1)S(1)}, u32[]{:S(2)}, u32[]{:S(2)}) collective-permute-start(bf16[288,512]{1,0:T(8,128)(2,1)S(1)} %get-tuple-element.66), channel_id=1, source_target_pairs={{1,2},{2,1},{5,6},{6,5},{9,10},{10,9},{13,14},{14,13},{17,18},{18,... | collective-permute-start | bytes 884744 | tf_op jit(solution)/shard_map/ppermute | solution.py:378
  25.8 12.6 %collective-permute-start.14 = (bf16[1536,128]{1,0:T(8,128)(2,1)S(1)}, bf16[1536,128]{1,0:T(8,128)(2,1)S(1)}, u32[]{:S(2)}, u32[]{:S(2)}) collective-permute-start(bf16[1536,128]{1,0:T(8,128)(2,1)S(1)} %shard_map.184.left_ref), channel_id=1, source_target_pairs={{0,16},{4,20},{8,24},{12,28},{16,0},{20,4},{24,8},{28,12},{1,17},{... | collective-permute-start | bytes 1179656 | tf_op jit(solution)/shard_map/ppermute | solution.py:294
  28.5 10.1 %collective-permute-start.9 = (bf16[288,512]{1,0:T(8,128)(2,1)S(1)}, bf16[288,512]{1,0:T(8,128)(2,1)S(1)}, u32[]{:S(2)}, u32[]{:S(2)}) collective-permute-start(bf16[288,512]{1,0:T(8,128)(2,1)S(1)} %get-tuple-element.67), channel_id=1, source_target_pairs={{0,1},{1,0},{2,3},{3,2},{4,5},{5,4},{6,7},{7,6},{8,9},{9,8},{10,11... | collective-permute-start | bytes 884744 | tf_op jit(solution)/shard_map/ppermute | solution.py:378
  28.6 12.5 %collective-permute-start.12 = (bf16[288,512]{1,0:T(8,128)(2,1)S(1)}, bf16[288,512]{1,0:T(8,128)(2,1)S(1)}, u32[]{:S(2)}, u32[]{:S(2)}) collective-permute-start(bf16[288,512]{1,0:T(8,128)(2,1)S(1)} %get-tuple-element.71), channel_id=1, source_target_pairs={{1,2},{2,1},{5,6},{6,5},{9,10},{10,9},{13,14},{14,13},{17,18},{18,... | collective-permute-start | bytes 884744 | tf_op jit(solution)/shard_map/ppermute | solution.py:378
  34.8 10.1 %collective-permute-start.11 = (bf16[288,512]{1,0:T(8,128)(2,1)S(1)}, bf16[288,512]{1,0:T(8,128)(2,1)S(1)}, u32[]{:S(2)}, u32[]{:S(2)}) collective-permute-start(bf16[288,512]{1,0:T(8,128)(2,1)S(1)} %get-tuple-element.70), channel_id=1, source_target_pairs={{0,1},{1,0},{2,3},{3,2},{4,5},{5,4},{6,7},{7,6},{8,9},{9,8},{10,11... | collective-permute-start | bytes 884744 | tf_op jit(solution)/shard_map/ppermute | solution.py:378
  34.9 12.5 %collective-permute-start.13 = (bf16[288,512]{1,0:T(8,128)(2,1)S(1)}, bf16[288,512]{1,0:T(8,128)(2,1)S(1)}, u32[]{:S(2)}, u32[]{:S(2)}) collective-permute-start(bf16[288,512]{1,0:T(8,128)(2,1)S(1)} %get-tuple-element.72), channel_id=1, source_target_pairs={{1,2},{2,1},{5,6},{6,5},{9,10},{10,9},{13,14},{14,13},{17,18},{18,... | collective-permute-start | bytes 884744 | tf_op jit(solution)/shard_map/ppermute | solution.py:378
  38.5 14.4 %collective-permute-start.19 = (bf16[1536,128]{1,0:T(8,128)(2,1)S(1)}, bf16[1536,128]{1,0:T(8,128)(2,1)S(1)}, u32[]{:S(2)}, u32[]{:S(2)}) collective-permute-start(bf16[1536,128]{1,0:T(8,128)(2,1)S(1)} %shard_map.187.own_ref), channel_id=1, source_target_pairs={{0,4},{4,0},{8,12},{12,8},{16,20},{20,16},{24,28},{28,24},{1,5},{5... | collective-permute-start | bytes 1179656 | tf_op jit(solution)/shard_map/ppermute | solution.py:294
  41.2 14.6 %collective-permute-start.17 = (bf16[288,512]{1,0:T(8,128)(2,1)S(1)}, bf16[288,512]{1,0:T(8,128)(2,1)S(1)}, u32[]{:S(2)}, u32[]{:S(2)}) collective-permute-start(bf16[288,512]{1,0:T(8,128)(2,1)S(1)} %get-tuple-element.77), channel_id=1, source_target_pairs={{0,1},{1,0},{2,3},{3,2},{4,5},{5,4},{6,7},{7,6},{8,9},{9,8},{10,11... | collective-permute-start | bytes 884744 | tf_op jit(solution)/shard_map/ppermute | solution.py:378
  41.3 9.8 %copy-start = (bf16[1,576,512]{2,1,0:T(8,128)(2,1)S(1)}, bf16[1,576,512]{2,1,0:T(8,128)(2,1)}, u32[]{:S(2)}) copy-start(bf16[1,576,512]{2,1,0:T(8,128)(2,1)} %weight_ref.7) | copy-start | bytes 1769476
  41.3 14.6 %collective-permute-start.18 = (bf16[288,512]{1,0:T(8,128)(2,1)S(1)}, bf16[288,512]{1,0:T(8,128)(2,1)S(1)}, u32[]{:S(2)}, u32[]{:S(2)}) collective-permute-start(bf16[288,512]{1,0:T(8,128)(2,1)S(1)} %get-tuple-element.78), channel_id=1, source_target_pairs={{1,2},{2,1},{5,6},{6,5},{9,10},{10,9},{13,14},{14,13},{17,18},{18,... | collective-permute-start | bytes 884744 | tf_op jit(solution)/shard_map/ppermute | solution.py:378
  47.5 9.8 %collective-permute-start.15 = (bf16[288,512]{1,0:T(8,128)(2,1)S(1)}, bf16[288,512]{1,0:T(8,128)(2,1)S(1)}, u32[]{:S(2)}, u32[]{:S(2)}) collective-permute-start(bf16[288,512]{1,0:T(8,128)(2,1)S(1)} %get-tuple-element.75), channel_id=1, source_target_pairs={{0,1},{1,0},{2,3},{3,2},{4,5},{5,4},{6,7},{7,6},{8,9},{9,8},{10,11... | collective-permute-start | bytes 884744 | tf_op jit(solution)/shard_map/ppermute | solution.py:378
  47.6 11.4 %collective-permute-start.16 = (bf16[288,512]{1,0:T(8,128)(2,1)S(1)}, bf16[288,512]{1,0:T(8,128)(2,1)S(1)}, u32[]{:S(2)}, u32[]{:S(2)}) collective-permute-start(bf16[288,512]{1,0:T(8,128)(2,1)S(1)} %get-tuple-element.76), channel_id=1, source_target_pairs={{1,2},{2,1},{5,6},{6,5},{9,10},{10,9},{13,14},{14,13},{17,18},{18,... | collective-permute-start | bytes 884744 | tf_op jit(solution)/shard_map/ppermute | solution.py:378
  51.1 1.8 %copy-start.3 = (f32[393216]{0:T(1024)S(1)}, f32[393216]{0:T(1024)}, u32[]{:S(2)}) copy-start(f32[393216]{0:T(1024)} %param.20) | copy-start | bytes 4718596
  51.1 1.9 %copy-start.4 = (f32[393216]{0:T(1024)S(1)}, f32[393216]{0:T(1024)}, u32[]{:S(2)}) copy-start(f32[393216]{0:T(1024)} %param.21) | copy-start | bytes 4718596
  53.0 2.9 %copy-start.1 = (f32[1,576,512]{2,1,0:T(8,128)S(1)}, f32[1,576,512]{2,1,0:T(8,128)}, u32[]{:S(2)}) copy-start(f32[1,576,512]{2,1,0:T(8,128)} %first_ref.3) | copy-start | bytes 3538948
  53.0 2.9 %copy-start.2 = (f32[1,576,512]{2,1,0:T(8,128)S(1)}, f32[1,576,512]{2,1,0:T(8,128)}, u32[]{:S(2)}) copy-start(f32[1,576,512]{2,1,0:T(8,128)} %second_ref.3) | copy-start | bytes 3538948
  55.9 3.1 %copy-start.5 = (f32[1,576]{1,0:T(1,128)S(1)}, f32[1,576]{1,0:T(1,128)}, u32[]{:S(2)}) copy-start(f32[1,576]{1,0:T(1,128)} %refs_3_.1) | copy-start | bytes 6916
  55.9 3.1 %copy-start.6 = (f32[1,576]{1,0:T(1,128)S(1)}, f32[1,576]{1,0:T(1,128)}, u32[]{:S(2)}) copy-start(f32[1,576]{1,0:T(1,128)} %refs_4_.1) | copy-start | bytes 6916
  55.9 3.1 %copy-start.7 = (f32[1,576]{1,0:T(1,128)S(1)}, f32[1,576]{1,0:T(1,128)}, u32[]{:S(2)}) copy-start(f32[1,576]{1,0:T(1,128)} %refs_5_.1) | copy-start | bytes 6916

commit v5 on v4

--- a/solution.py
+++ b/solution.py
@@ -34,7 +34,8 @@
 def adam_step(params, gradient, first_moment, second_moment):
     first_new = beta_one * first_moment + (1.0 - beta_one) * gradient
     second_new = beta_two * second_moment + (1.0 - beta_two) * gradient * gradient
-    ratio = first_new / (jnp.sqrt(second_new) * root_scale + adam_eps)
+    root = second_new * lax.rsqrt(second_new)
+    ratio = first_new / (root * root_scale + adam_eps)
     return (params * (1.0 - learn_rate * weight_decay) - ratio * rate_scale, first_new, second_new)
 
 
@@ -143,9 +144,14 @@
         place = jnp.where(right, me, n - 1 - me)
         owner = jnp.where(right, n - s + place, s - 1 - place)
 
-        @pl.when(s > place)
+        start = pl.multiple_of(owner * rows + first, 16)
+
+        @pl.when(place == 0)
         def _():
-            start = pl.multiple_of(owner * rows + first, 16)
+            sent_ref[...] = partial_ref[pl.ds(start, depth), :]
+
+        @pl.when((place > 0) & (s > place))
+        def _():
             sent_ref[...] = add_narrow(came_ref[...], partial_ref[pl.ds(start, depth), :])
 
         @pl.when(s <= place)
@@ -177,7 +183,7 @@
             @pl.when((block >= 0) & (block < n))
             def _():
                 for c in range(len(chunks)):
-                    put(block, c, got[(s * 2 + w) * len(chunks) + c])
+                    put(block, c, got[(s * len(chunks) + c) * 2 + w])
 
     total = jnp.dot(inputs_ref[0], weights[...], preferred_element_type=wide)
     for k in range(cols // lanes):
@@ -210,13 +216,15 @@
     step, steps = pl.program_id(0), pl.num_programs(0)
     whole = sum(size for _, size in chunks)
     start = pl.multiple_of(lax.axis_index("fsdp") * whole + chunks[c][0] + step * depth, 16)
+    me, count = lax.axis_index("fsdp"), lax.axis_size("fsdp")
+    mates = (me ^ 1, jnp.where((me & 1) == 0, me - 1, me + 1))
     share = jnp.zeros((depth, lanes), wide)
     used = spread_ref[...].astype(narrow).astype(wide)
     for k in range(cols // lanes):
         part = slice(k * lanes, (k + 1) * lanes)
         total = partial_ref[pl.ds(start, depth), part].astype(wide)
-        for ref in came:
-            total = total + ref[:, part].astype(wide)
+        for mate, ref in zip(mates, came):
+            total = total + jnp.where((mate >= 0) & (mate < count), ref[:, part].astype(wide), 0.0)
         weight = weight_ref[0, :, part].astype(wide)
         share = share + total * weight
         new_weight, new_first, new_second = adam_step(
@@ -354,10 +362,19 @@
                 pltpu.SemaphoreType.DMA((count + 1,)),
             ],
         )
-        links = [
-            [pair for i in range(start, n - 1, 2) for pair in ((i, i + 1), (i + 1, i))]
-            for start in (0, 1)
-        ]
+        links = []
+        for start in (0, 1):
+            mate = {}
+            for i in range(start, n - 1, 2):
+                mate[i], mate[i + 1] = i + 1, i
+            links.append(
+                [
+                    (silo * n + i, silo * n + mate[i] if i in mate else (silo ^ 1) * n + i)
+                    for silo in range(silos)
+                    for i in range(n)
+                    if i in mate or silos % 2 == 0
+                ]
+            )
         slots = []
         for s in range(n):
             got = [[None for _ in range(count)] for _ in links]
@@ -375,7 +392,7 @@
                         specs=[VMEM] * 3,
                     )
                 for w in range(2):
-                    got[w][c] = lax.ppermute(sent[w], "fsdp", links[w])
+                    got[w][c] = lax.ppermute(sent[w], ("silo", "fsdp"), links[w])
             slots.append(got)
             if s == 0:
                 partial, inv_rms, inputs = call(
@@ -396,7 +413,7 @@
             functools.partial(keys_kernel, n, chunks),
             shape((1, tokens, cols), narrow),
             [inputs, inv_rms, key_weight, spread]
-            + [slots[s][w][c] for s in range(n - 1) for w in range(2) for c in range(count)],
+            + [slots[s][w][c] for s in range(n - 1) for c in range(count) for w in range(2)],
             scratch=[pltpu.VMEM((feats, cols), narrow)],
             specs=[VMEM] * (4 + (n - 1) * 2 * count),
         )

time: 61.1 us -> 58.8 us (0.962)
  the two profiles are of different devices: /device:TPU:8 before, /device:TPU:0 now
where the time goes in v5:
time: 58.8 us; the launch traced here: 58.6 us
  starting transfers between devices  28.3 us (48%)
  waiting for transfers between devices  16 us (27%)
  Pallas kernels  13.4 us (23%)
  between operations  0.81 us (1%)
    ppermute x16, starting transfers between devices, per_device(): got[w][c] = lax.ppermute(sent[w], ('silo', 'fsdp'), links[w])  24.1 us
    ppermute x16, waiting for transfers between devices, per_device(): got[w][c] = lax.ppermute(sent[w], ('silo', 'fsdp'), links[w])  14.6 us
    pallas_call x15, Pallas kernels, call(): pl.pallas_call(kernel, out_shape=out_shape, grid=grid, in_specs=specs if...  13.4 us
    ppermute x4, starting transfers between devices, swap(): return lax.ppermute(part, 'silo', [(i, i ^ bit) for i in range(silos)])  4.24 us
    ppermute x4, waiting for transfers between devices, swap(): return lax.ppermute(part, 'silo', [(i, i ^ bit) for i in range(silos)])  1.34 us
  transfers between devices with their start and end apart: 20, of which 7 were waited for; matrix products, arithmetic and copies ran while one was open for 0% of the time, Pallas kernels for 20%

profile of v5, /device:TPU:0, one launch (start us, length us, event | category | flops | bytes accessed | tf_op | source)
XLA Modules:
  0.0 58.6 jit_solution(8383776412770490528)
XLA Ops:
  0.6 0.5 collective-permute-start.6
  1.2 1.2 %shard_map.179 = (f32[576,128]{1,0:T(8,128)S(1)}, bf16[288,512]{1,0:T(8,128)(2,1)S(1)}, bf16[288,512]{1,0:T(8,128)(2,1)S(1)}, bf16[288,512]{1,0:T(8,128)(2,1)S(1)}, bf16[288,512]{1,0:T(8,128)(2,1)S(1)}) custom-call(bf16[1,576,512]{2,1,0:T(8,128)(2,1)} %weight_ref.7, f32[1,576]{1,0:T(1,128)} %refs_3_.1), custom_call_target="tpu_custom_call" | custom-call | tf_op jit(solution)/shard_map/pallas_call | solution.py:72
  2.3 2.7 %collective-permute-start = (bf16[288,512]{1,0:T(8,128)(2,1)S(1)}, bf16[288,512]{1,0:T(8,128)(2,1)S(1)}, u32[]{:S(2)}, u32[]{:S(2)}) collective-permute-start(bf16[288,512]{1,0:T(8,128)(2,1)S(1)} %get-tuple-element.54), channel_id=1, source_target_pairs={{0,1},{1,0},{2,3},{3,2},{4,5},{5,4},{6,7},{7,6},{8,9},{9,8},{10,11... | collective-permute-start | bytes 884744 | tf_op jit(solution)/shard_map/ppermute | solution.py:395
  5.0 0.2 collective-permute-start.1
  5.2 2.9 %collective-permute-start.2 = (bf16[288,512]{1,0:T(8,128)(2,1)S(1)}, bf16[288,512]{1,0:T(8,128)(2,1)S(1)}, u32[]{:S(2)}, u32[]{:S(2)}) collective-permute-start(bf16[288,512]{1,0:T(8,128)(2,1)S(1)} %get-tuple-element.56), channel_id=1, source_target_pairs={{0,1},{1,0},{2,3},{3,2},{4,5},{5,4},{6,7},{7,6},{8,9},{9,8},{10,11... | collective-permute-start | bytes 884744 | tf_op jit(solution)/shard_map/ppermute | solution.py:395
  8.2 2.4 %shard_map.178 = (bf16[2304,512]{1,0:T(8,128)(2,1)S(1)}, f32[256,128]{1,0:T(8,128)S(1)}, bf16[1,256,2304]{2,1,0:T(8,128)(2,1)S(1)}) custom-call(bf16[1,256,2304]{2,1,0:T(8,128)(2,1)} %inputs_ref.1, bf16[1,256,512]{2,1,0:T(8,128)(2,1)} %cot_ref.1), custom_call_target="tpu_custom_call" | custom-call | tf_op jit(solution)/shard_map/pallas_call | solution.py:72
  10.6 0.0 collective-permute-done.6.other_ref
  10.6 1.5 %shard_map.181.left_ref = bf16[1536,128]{1,0:T(8,128)(2,1)S(1)} custom-call(bf16[1,393216]{1,0:T(2,128)(2,1)} %mine_ref, bf16[1,393216]{1,0:T(2,128)(2,1)S(1)} %collective-permute-done.6.other_ref), custom_call_target="tpu_custom_call" | custom-call | tf_op jit(solution)/shard_map/pallas_call | solution.py:72
  12.1 1.6 %collective-permute-start.11 = (bf16[1536,128]{1,0:T(8,128)(2,1)S(1)}, bf16[1536,128]{1,0:T(8,128)(2,1)S(1)}, u32[]{:S(2)}, u32[]{:S(2)}) collective-permute-start(bf16[1536,128]{1,0:T(8,128)(2,1)S(1)} %shard_map.181.left_ref), channel_id=1, source_target_pairs={{0,8},{4,12},{8,0},{12,4},{16,24},{20,28},{24,16},{28,20},{1,9},{5... | collective-permute-start | bytes 1179656 | tf_op jit(solution)/shard_map/ppermute | solution.py:302
  13.7 0.0 collective-permute-done.1.odd_ref.refs_1_
  13.7 0.1 shard_map.180
  13.8 2.3 %collective-permute-start.4 = (bf16[288,512]{1,0:T(8,128)(2,1)S(1)}, bf16[288,512]{1,0:T(8,128)(2,1)S(1)}, u32[]{:S(2)}, u32[]{:S(2)}) collective-permute-start(bf16[288,512]{1,0:T(8,128)(2,1)S(1)} %get-tuple-element.59), channel_id=1, source_target_pairs={{0,1},{1,0},{2,3},{3,2},{4,5},{5,4},{6,7},{7,6},{8,9},{9,8},{10,11... | collective-permute-start | bytes 884744 | tf_op jit(solution)/shard_map/ppermute | solution.py:395
  16.1 0.0 collective-permute-start.5
  16.1 3.1 %collective-permute-done.2.even_ref.refs_2_ = bf16[288,512]{1,0:T(8,128)(2,1)S(1)} collective-permute-done((bf16[288,512]{1,0:T(8,128)(2,1)S(1)}, bf16[288,512]{1,0:T(8,128)(2,1)S(1)}, u32[]{:S(2)}, u32[]{:S(2)}) %collective-permute-start.2) | collective-permute-done | bytes 294944 | tf_op jit(solution)/shard_map/ppermute | solution.py:395
  19.2 0.1 shard_map.182
  19.3 3.1 %collective-permute-start.7 = (bf16[288,512]{1,0:T(8,128)(2,1)S(1)}, bf16[288,512]{1,0:T(8,128)(2,1)S(1)}, u32[]{:S(2)}, u32[]{:S(2)}) collective-permute-start(bf16[288,512]{1,0:T(8,128)(2,1)S(1)} %get-tuple-element.65), channel_id=1, source_target_pairs={{0,1},{1,0},{2,3},{3,2},{4,5},{5,4},{6,7},{7,6},{8,9},{9,8},{10,11... | collective-permute-start | bytes 884744 | tf_op jit(solution)/shard_map/ppermute | solution.py:395
  22.4 0.0 collective-permute-start.8
  22.4 1.3 %collective-permute-done.11.right_ref = bf16[1536,128]{1,0:T(8,128)(2,1)S(1)} collective-permute-done((bf16[1536,128]{1,0:T(8,128)(2,1)S(1)}, bf16[1536,128]{1,0:T(8,128)(2,1)S(1)}, u32[]{:S(2)}, u32[]{:S(2)}) %collective-permute-start.11) | collective-permute-done | bytes 393248 | tf_op jit(solution)/shard_map/ppermute | solution.py:302
  23.7 0.1 shard_map.184.left_ref
  23.8 1.6 %collective-permute-start.14 = (bf16[1536,128]{1,0:T(8,128)(2,1)S(1)}, bf16[1536,128]{1,0:T(8,128)(2,1)S(1)}, u32[]{:S(2)}, u32[]{:S(2)}) collective-permute-start(bf16[1536,128]{1,0:T(8,128)(2,1)S(1)} %shard_map.184.left_ref), channel_id=1, source_target_pairs={{0,16},{4,20},{8,24},{12,28},{16,0},{20,4},{24,8},{28,12},{1,17},{... | collective-permute-start | bytes 1179656 | tf_op jit(solution)/shard_map/ppermute | solution.py:302
  25.4 0.1 collective-permute-done.4.even_ref.refs_4_
  25.5 0.1 shard_map.183
  25.6 3.2 %collective-permute-start.9 = (bf16[288,512]{1,0:T(8,128)(2,1)S(1)}, bf16[288,512]{1,0:T(8,128)(2,1)S(1)}, u32[]{:S(2)}, u32[]{:S(2)}) collective-permute-start(bf16[288,512]{1,0:T(8,128)(2,1)S(1)} %get-tuple-element.67), channel_id=1, source_target_pairs={{0,1},{1,0},{2,3},{3,2},{4,5},{5,4},{6,7},{7,6},{8,9},{9,8},{10,11... | collective-permute-start | bytes 884744 | tf_op jit(solution)/shard_map/ppermute | solution.py:395
  28.7 0.0 collective-permute-start.10
  28.7 3.1 %collective-permute-done.7.even_ref.refs_6_ = bf16[288,512]{1,0:T(8,128)(2,1)S(1)} collective-permute-done((bf16[288,512]{1,0:T(8,128)(2,1)S(1)}, bf16[288,512]{1,0:T(8,128)(2,1)S(1)}, u32[]{:S(2)}, u32[]{:S(2)}) %collective-permute-start.7) | collective-permute-done | bytes 294944 | tf_op jit(solution)/shard_map/ppermute | solution.py:395
  31.8 0.1 shard_map.185
  31.9 3.2 %collective-permute-start.12 = (bf16[288,512]{1,0:T(8,128)(2,1)S(1)}, bf16[288,512]{1,0:T(8,128)(2,1)S(1)}, u32[]{:S(2)}, u32[]{:S(2)}) collective-permute-start(bf16[288,512]{1,0:T(8,128)(2,1)S(1)} %get-tuple-element.71), channel_id=1, source_target_pairs={{0,1},{1,0},{2,3},{3,2},{4,5},{5,4},{6,7},{7,6},{8,9},{9,8},{10,11... | collective-permute-start | bytes 884744 | tf_op jit(solution)/shard_map/ppermute | solution.py:395
  35.1 0.0 collective-permute-start.13
  35.1 0.0 collective-permute-done.14.right_ref
  35.1 0.1 shard_map.187.own_ref
  35.2 0.6 collective-permute-start.19
  35.7 2.4 %collective-permute-done.9.refs_8_.even_ref = bf16[288,512]{1,0:T(8,128)(2,1)S(1)} collective-permute-done((bf16[288,512]{1,0:T(8,128)(2,1)S(1)}, bf16[288,512]{1,0:T(8,128)(2,1)S(1)}, u32[]{:S(2)}, u32[]{:S(2)}) %collective-permute-start.9) | collective-permute-done | bytes 294944 | tf_op jit(solution)/shard_map/ppermute | solution.py:395
  38.1 0.1 shard_map.189
  38.2 3.2 %collective-permute-start.17 = (bf16[288,512]{1,0:T(8,128)(2,1)S(1)}, bf16[288,512]{1,0:T(8,128)(2,1)S(1)}, u32[]{:S(2)}, u32[]{:S(2)}) collective-permute-start(bf16[288,512]{1,0:T(8,128)(2,1)S(1)} %get-tuple-element.77), channel_id=1, source_target_pairs={{0,1},{1,0},{2,3},{3,2},{4,5},{5,4},{6,7},{7,6},{8,9},{9,8},{10,11... | collective-permute-start | bytes 884744 | tf_op jit(solution)/shard_map/ppermute | solution.py:395
  41.4 0.0 collective-permute-start.18
  41.4 3.0 %collective-permute-done.12.refs_10_.even_ref = bf16[288,512]{1,0:T(8,128)(2,1)S(1)} collective-permute-done((bf16[288,512]{1,0:T(8,128)(2,1)S(1)}, bf16[288,512]{1,0:T(8,128)(2,1)S(1)}, u32[]{:S(2)}, u32[]{:S(2)}) %collective-permute-start.12) | collective-permute-done | bytes 294944 | tf_op jit(solution)/shard_map/ppermute | solution.py:395
  44.5 0.1 shard_map.188
  44.5 3.2 %collective-permute-start.15 = (bf16[288,512]{1,0:T(8,128)(2,1)S(1)}, bf16[288,512]{1,0:T(8,128)(2,1)S(1)}, u32[]{:S(2)}, u32[]{:S(2)}) collective-permute-start(bf16[288,512]{1,0:T(8,128)(2,1)S(1)} %get-tuple-element.75), channel_id=1, source_target_pairs={{0,1},{1,0},{2,3},{3,2},{4,5},{5,4},{6,7},{7,6},{8,9},{9,8},{10,11... | collective-permute-start | bytes 884744 | tf_op jit(solution)/shard_map/ppermute | solution.py:395
  47.8 1.8 %shard_map.186 = bf16[1,256,512]{2,1,0:T(8,128)(2,1)} custom-call(bf16[1,256,2304]{2,1,0:T(8,128)(2,1)S(1)} %get-tuple-element.51.inputs_ref, f32[256,128]{1,0:T(8,128)S(1)} %get-tuple-element.52.rms_ref, bf16[1,576,512]{2,1,0:T(8,128)(2,1)S(1)} %copy-done, f32[576,128]{1,0:T(8,128)S(1)} %get-tuple-element.53.spread_ref, ...), custom_call_target="tpu_custom_call" | custom-call | tf_op jit(solution)/shard_map/pallas_call | solution.py:72
  49.5 0.0 collective-permute-done.19.other_ref
  49.5 0.1 copy-done.4
  49.7 2.8 %shard_map.190 = (f32[2,1536,128]{2,1,0:T(8,128)}, f32[2,1536,128]{2,1,0:T(8,128)}) custom-call(bf16[1536,128]{1,0:T(8,128)(2,1)S(1)} %shard_map.187.own_ref, bf16[1536,128]{1,0:T(8,128)(2,1)S(1)} %collective-permute-done.19.other_ref, f32[2,1536,128]{2,1,0:T(8,128)S(1)} %bitcast.4, f32[2,1536,128]{2,1,0:T(8,128)S(1)} %bitcast.5), custom_call_target="tpu_custom_call" | custom-call | tf_op jit(solution)/shard_map/pallas_call | solution.py:72
  52.5 0.0 copy-start.5
  52.5 0.0 copy-start.6
  52.5 0.0 copy-start.7
  52.6 1.5 %shard_map.191 = (f32[288,128]{1,0:T(8,128)S(1)}, bf16[1,576,512]{2,1,0:T(8,128)(2,1)}, f32[1,576,512]{2,1,0:T(8,128)}, f32[1,576,512]{2,1,0:T(8,128)}) custom-call(f32[576,128]{1,0:T(8,128)S(1)} %get-tuple-element.53.spread_ref, bf16[1,576,512]{2,1,0:T(8,128)(2,1)S(1)} %copy-done, f32[1,576,512]{2,1,0:T(8,128)S(1)} %copy-done.1, ...), custom_call_target="tpu_custom_call" | custom-call | tf_op jit(solution)/shard_map/pallas_call | solution.py:72
  54.0 2.9 %collective-permute-done.15.refs_0_ = bf16[288,512]{1,0:T(8,128)(2,1)S(1)} collective-permute-done((bf16[288,512]{1,0:T(8,128)(2,1)S(1)}, bf16[288,512]{1,0:T(8,128)(2,1)S(1)}, u32[]{:S(2)}, u32[]{:S(2)}) %collective-permute-start.15) | collective-permute-done | bytes 294944 | tf_op jit(solution)/shard_map/ppermute | solution.py:395
  56.9 1.7 %shard_map.192 = (bf16[1,576,512]{2,1,0:T(8,128)(2,1)}, f32[1,576,512]{2,1,0:T(8,128)}, f32[1,576,512]{2,1,0:T(8,128)}, f32[1,576]{1,0:T(1,128)}, f32[1,576]{1,0:T(1,128)}, /*index=5*/f32[1,576]{1,0:T(1,128)}) custom-call(f32[576,128]{1,0:T(8,128)S(1)} %get-tuple-element.53.spread_ref, ...), custom_call_target="tpu_custom_call", output_to_operand_aliasing={{0}: (11, {}), {1}: (12, {}), {2}: (13, {})} | custom-call | tf_op jit(solution)/shard_map/pallas_call | solution.py:72
  (23 shorter events, 0.1 us)
Async XLA Ops:
  0.6 9.9 %collective-permute-start.6 = (bf16[1,393216]{1,0:T(2,128)(2,1)}, bf16[1,393216]{1,0:T(2,128)(2,1)S(1)}, u32[]{:S(2)}, u32[]{:S(2)}) collective-permute-start(bf16[1,393216]{1,0:T(2,128)(2,1)} %mine_ref), channel_id=1, source_target_pairs={{0,4},{4,0},{8,12},{12,8},{16,20},{20,16},{24,28},{28,24},{1,5},{5... | collective-permute-start | bytes 2359304 | tf_op jit(solution)/shard_map/ppermute | solution.py:302
  2.3 11.3 %collective-permute-start = (bf16[288,512]{1,0:T(8,128)(2,1)S(1)}, bf16[288,512]{1,0:T(8,128)(2,1)S(1)}, u32[]{:S(2)}, u32[]{:S(2)}) collective-permute-start(bf16[288,512]{1,0:T(8,128)(2,1)S(1)} %get-tuple-element.54), channel_id=1, source_target_pairs={{0,1},{1,0},{2,3},{3,2},{4,5},{5,4},{6,7},{7,6},{8,9},{9,8},{10,11... | collective-permute-start | bytes 884744 | tf_op jit(solution)/shard_map/ppermute | solution.py:395
  5.0 8.7 %collective-permute-start.1 = (bf16[288,512]{1,0:T(8,128)(2,1)S(1)}, bf16[288,512]{1,0:T(8,128)(2,1)S(1)}, u32[]{:S(2)}, u32[]{:S(2)}) collective-permute-start(bf16[288,512]{1,0:T(8,128)(2,1)S(1)} %get-tuple-element.55), channel_id=1, source_target_pairs={{0,4},{1,2},{2,1},{3,7},{4,0},{5,6},{6,5},{7,3},{8,12},{9,10},{10,... | collective-permute-start | bytes 884744 | tf_op jit(solution)/shard_map/ppermute | solution.py:395
  5.2 14.0 %collective-permute-start.2 = (bf16[288,512]{1,0:T(8,128)(2,1)S(1)}, bf16[288,512]{1,0:T(8,128)(2,1)S(1)}, u32[]{:S(2)}, u32[]{:S(2)}) collective-permute-start(bf16[288,512]{1,0:T(8,128)(2,1)S(1)} %get-tuple-element.56), channel_id=1, source_target_pairs={{0,1},{1,0},{2,3},{3,2},{4,5},{5,4},{6,7},{7,6},{8,9},{9,8},{10,11... | collective-permute-start | bytes 884744 | tf_op jit(solution)/shard_map/ppermute | solution.py:395
  8.2 11.0 %collective-permute-start.3 = (bf16[288,512]{1,0:T(8,128)(2,1)S(1)}, bf16[288,512]{1,0:T(8,128)(2,1)S(1)}, u32[]{:S(2)}, u32[]{:S(2)}) collective-permute-start(bf16[288,512]{1,0:T(8,128)(2,1)S(1)} %get-tuple-element.57), channel_id=1, source_target_pairs={{0,4},{1,2},{2,1},{3,7},{4,0},{5,6},{6,5},{7,3},{8,12},{9,10},{10,... | collective-permute-start | bytes 884744 | tf_op jit(solution)/shard_map/ppermute | solution.py:395
  12.1 11.6 %collective-permute-start.11 = (bf16[1536,128]{1,0:T(8,128)(2,1)S(1)}, bf16[1536,128]{1,0:T(8,128)(2,1)S(1)}, u32[]{:S(2)}, u32[]{:S(2)}) collective-permute-start(bf16[1536,128]{1,0:T(8,128)(2,1)S(1)} %shard_map.181.left_ref), channel_id=1, source_target_pairs={{0,8},{4,12},{8,0},{12,4},{16,24},{20,28},{24,16},{28,20},{1,9},{5... | collective-permute-start | bytes 1179656 | tf_op jit(solution)/shard_map/ppermute | solution.py:302
  13.8 11.8 %collective-permute-start.4 = (bf16[288,512]{1,0:T(8,128)(2,1)S(1)}, bf16[288,512]{1,0:T(8,128)(2,1)S(1)}, u32[]{:S(2)}, u32[]{:S(2)}) collective-permute-start(bf16[288,512]{1,0:T(8,128)(2,1)S(1)} %get-tuple-element.59), channel_id=1, source_target_pairs={{0,1},{1,0},{2,3},{3,2},{4,5},{5,4},{6,7},{7,6},{8,9},{9,8},{10,11... | collective-permute-start | bytes 884744 | tf_op jit(solution)/shard_map/ppermute | solution.py:395
  16.1 9.4 %collective-permute-start.5 = (bf16[288,512]{1,0:T(8,128)(2,1)S(1)}, bf16[288,512]{1,0:T(8,128)(2,1)S(1)}, u32[]{:S(2)}, u32[]{:S(2)}) collective-permute-start(bf16[288,512]{1,0:T(8,128)(2,1)S(1)} %get-tuple-element.60), channel_id=1, source_target_pairs={{0,4},{1,2},{2,1},{3,7},{4,0},{5,6},{6,5},{7,3},{8,12},{9,10},{10,... | collective-permute-start | bytes 884744 | tf_op jit(solution)/shard_map/ppermute | solution.py:395
  19.3 12.6 %collective-permute-start.7 = (bf16[288,512]{1,0:T(8,128)(2,1)S(1)}, bf16[288,512]{1,0:T(8,128)(2,1)S(1)}, u32[]{:S(2)}, u32[]{:S(2)}) collective-permute-start(bf16[288,512]{1,0:T(8,128)(2,1)S(1)} %get-tuple-element.65), channel_id=1, source_target_pairs={{0,1},{1,0},{2,3},{3,2},{4,5},{5,4},{6,7},{7,6},{8,9},{9,8},{10,11... | collective-permute-start | bytes 884744 | tf_op jit(solution)/shard_map/ppermute | solution.py:395
  22.4 9.4 %collective-permute-start.8 = (bf16[288,512]{1,0:T(8,128)(2,1)S(1)}, bf16[288,512]{1,0:T(8,128)(2,1)S(1)}, u32[]{:S(2)}, u32[]{:S(2)}) collective-permute-start(bf16[288,512]{1,0:T(8,128)(2,1)S(1)} %get-tuple-element.66), channel_id=1, source_target_pairs={{0,4},{1,2},{2,1},{3,7},{4,0},{5,6},{6,5},{7,3},{8,12},{9,10},{10,... | collective-permute-start | bytes 884744 | tf_op jit(solution)/shard_map/ppermute | solution.py:395
  23.8 11.3 %collective-permute-start.14 = (bf16[1536,128]{1,0:T(8,128)(2,1)S(1)}, bf16[1536,128]{1,0:T(8,128)(2,1)S(1)}, u32[]{:S(2)}, u32[]{:S(2)}) collective-permute-start(bf16[1536,128]{1,0:T(8,128)(2,1)S(1)} %shard_map.184.left_ref), channel_id=1, source_target_pairs={{0,16},{4,20},{8,24},{12,28},{16,0},{20,4},{24,8},{28,12},{1,17},{... | collective-permute-start | bytes 1179656 | tf_op jit(solution)/shard_map/ppermute | solution.py:302
  25.6 12.6 %collective-permute-start.9 = (bf16[288,512]{1,0:T(8,128)(2,1)S(1)}, bf16[288,512]{1,0:T(8,128)(2,1)S(1)}, u32[]{:S(2)}, u32[]{:S(2)}) collective-permute-start(bf16[288,512]{1,0:T(8,128)(2,1)S(1)} %get-tuple-element.67), channel_id=1, source_target_pairs={{0,1},{1,0},{2,3},{3,2},{4,5},{5,4},{6,7},{7,6},{8,9},{9,8},{10,11... | collective-permute-start | bytes 884744 | tf_op jit(solution)/shard_map/ppermute | solution.py:395
  28.7 9.4 %collective-permute-start.10 = (bf16[288,512]{1,0:T(8,128)(2,1)S(1)}, bf16[288,512]{1,0:T(8,128)(2,1)S(1)}, u32[]{:S(2)}, u32[]{:S(2)}) collective-permute-start(bf16[288,512]{1,0:T(8,128)(2,1)S(1)} %get-tuple-element.68), channel_id=1, source_target_pairs={{0,4},{1,2},{2,1},{3,7},{4,0},{5,6},{6,5},{7,3},{8,12},{9,10},{10,... | collective-permute-start | bytes 884744 | tf_op jit(solution)/shard_map/ppermute | solution.py:395
  31.9 12.6 %collective-permute-start.12 = (bf16[288,512]{1,0:T(8,128)(2,1)S(1)}, bf16[288,512]{1,0:T(8,128)(2,1)S(1)}, u32[]{:S(2)}, u32[]{:S(2)}) collective-permute-start(bf16[288,512]{1,0:T(8,128)(2,1)S(1)} %get-tuple-element.71), channel_id=1, source_target_pairs={{0,1},{1,0},{2,3},{3,2},{4,5},{5,4},{6,7},{7,6},{8,9},{9,8},{10,11... | collective-permute-start | bytes 884744 | tf_op jit(solution)/shard_map/ppermute | solution.py:395
  35.1 9.4 %collective-permute-start.13 = (bf16[288,512]{1,0:T(8,128)(2,1)S(1)}, bf16[288,512]{1,0:T(8,128)(2,1)S(1)}, u32[]{:S(2)}, u32[]{:S(2)}) collective-permute-start(bf16[288,512]{1,0:T(8,128)(2,1)S(1)} %get-tuple-element.72), channel_id=1, source_target_pairs={{0,4},{1,2},{2,1},{3,7},{4,0},{5,6},{6,5},{7,3},{8,12},{9,10},{10,... | collective-permute-start | bytes 884744 | tf_op jit(solution)/shard_map/ppermute | solution.py:395
  35.2 14.4 %collective-permute-start.19 = (bf16[1536,128]{1,0:T(8,128)(2,1)S(1)}, bf16[1536,128]{1,0:T(8,128)(2,1)S(1)}, u32[]{:S(2)}, u32[]{:S(2)}) collective-permute-start(bf16[1536,128]{1,0:T(8,128)(2,1)S(1)} %shard_map.187.own_ref), channel_id=1, source_target_pairs={{0,4},{4,0},{8,12},{12,8},{16,20},{20,16},{24,28},{28,24},{1,5},{5... | collective-permute-start | bytes 1179656 | tf_op jit(solution)/shard_map/ppermute | solution.py:302
  38.2 14.3 %collective-permute-start.17 = (bf16[288,512]{1,0:T(8,128)(2,1)S(1)}, bf16[288,512]{1,0:T(8,128)(2,1)S(1)}, u32[]{:S(2)}, u32[]{:S(2)}) collective-permute-start(bf16[288,512]{1,0:T(8,128)(2,1)S(1)} %get-tuple-element.77), channel_id=1, source_target_pairs={{0,1},{1,0},{2,3},{3,2},{4,5},{5,4},{6,7},{7,6},{8,9},{9,8},{10,11... | collective-permute-start | bytes 884744 | tf_op jit(solution)/shard_map/ppermute | solution.py:395
  41.4 6.3 %copy-start = (bf16[1,576,512]{2,1,0:T(8,128)(2,1)S(1)}, bf16[1,576,512]{2,1,0:T(8,128)(2,1)}, u32[]{:S(2)}) copy-start(bf16[1,576,512]{2,1,0:T(8,128)(2,1)} %weight_ref.7) | copy-start | bytes 1769476
  41.4 11.1 %collective-permute-start.18 = (bf16[288,512]{1,0:T(8,128)(2,1)S(1)}, bf16[288,512]{1,0:T(8,128)(2,1)S(1)}, u32[]{:S(2)}, u32[]{:S(2)}) collective-permute-start(bf16[288,512]{1,0:T(8,128)(2,1)S(1)} %get-tuple-element.78), channel_id=1, source_target_pairs={{0,4},{1,2},{2,1},{3,7},{4,0},{5,6},{6,5},{7,3},{8,12},{9,10},{10,... | collective-permute-start | bytes 884744 | tf_op jit(solution)/shard_map/ppermute | solution.py:395
  44.5 12.4 %collective-permute-start.15 = (bf16[288,512]{1,0:T(8,128)(2,1)S(1)}, bf16[288,512]{1,0:T(8,128)(2,1)S(1)}, u32[]{:S(2)}, u32[]{:S(2)}) collective-permute-start(bf16[288,512]{1,0:T(8,128)(2,1)S(1)} %get-tuple-element.75), channel_id=1, source_target_pairs={{0,1},{1,0},{2,3},{3,2},{4,5},{5,4},{6,7},{7,6},{8,9},{9,8},{10,11... | collective-permute-start | bytes 884744 | tf_op jit(solution)/shard_map/ppermute | solution.py:395
  47.8 9.1 %collective-permute-start.16 = (bf16[288,512]{1,0:T(8,128)(2,1)S(1)}, bf16[288,512]{1,0:T(8,128)(2,1)S(1)}, u32[]{:S(2)}, u32[]{:S(2)}) collective-permute-start(bf16[288,512]{1,0:T(8,128)(2,1)S(1)} %get-tuple-element.76), channel_id=1, source_target_pairs={{0,4},{1,2},{2,1},{3,7},{4,0},{5,6},{6,5},{7,3},{8,12},{9,10},{10,... | collective-permute-start | bytes 884744 | tf_op jit(solution)/shard_map/ppermute | solution.py:395
  47.8 1.8 %copy-start.3 = (f32[393216]{0:T(1024)S(1)}, f32[393216]{0:T(1024)}, u32[]{:S(2)}) copy-start(f32[393216]{0:T(1024)} %param.20) | copy-start | bytes 4718596
  47.8 1.9 %copy-start.4 = (f32[393216]{0:T(1024)S(1)}, f32[393216]{0:T(1024)}, u32[]{:S(2)}) copy-start(f32[393216]{0:T(1024)} %param.21) | copy-start | bytes 4718596
  49.6 2.9 %copy-start.1 = (f32[1,576,512]{2,1,0:T(8,128)S(1)}, f32[1,576,512]{2,1,0:T(8,128)}, u32[]{:S(2)}) copy-start(f32[1,576,512]{2,1,0:T(8,128)} %first_ref.3) | copy-start | bytes 3538948
  49.6 2.9 %copy-start.2 = (f32[1,576,512]{2,1,0:T(8,128)S(1)}, f32[1,576,512]{2,1,0:T(8,128)}, u32[]{:S(2)}) copy-start(f32[1,576,512]{2,1,0:T(8,128)} %second_ref.3) | copy-start | bytes 3538948
  52.5 4.4 %copy-start.5 = (f32[1,576]{1,0:T(1,128)S(1)}, f32[1,576]{1,0:T(1,128)}, u32[]{:S(2)}) copy-start(f32[1,576]{1,0:T(1,128)} %refs_3_.1) | copy-start | bytes 6916
  52.5 4.4 %copy-start.6 = (f32[1,576]{1,0:T(1,128)S(1)}, f32[1,576]{1,0:T(1,128)}, u32[]{:S(2)}) copy-start(f32[1,576]{1,0:T(1,128)} %refs_4_.1) | copy-start | bytes 6916
  52.5 4.4 %copy-start.7 = (f32[1,576]{1,0:T(1,128)S(1)}, f32[1,576]{1,0:T(1,128)}, u32[]{:S(2)}) copy-start(f32[1,576]{1,0:T(1,128)} %refs_5_.1) | copy-start | bytes 6916

commit v6 on v5

--- a/solution.py
+++ b/solution.py
@@ -82,7 +82,7 @@
     )(*inputs)
 
 
-def scale_kernel(chunks, weight_ref, gain_ref, spread_ref, *refs):
+def scale_kernel(chunks, weight_ref, gain_ref, *refs):
     count = len(chunks)
     sent_refs, (held, gain_held, sems) = refs[: 2 * count], refs[2 * count :]
     rows = weight_ref.shape[1]
@@ -96,7 +96,6 @@
         copy.start()
     gain_copy.wait()
     spread = jnp.broadcast_to(gain_held[...], (lanes, rows)).T
-    spread_ref[...] = spread
     used = spread.astype(narrow).astype(wide)
     for c, span in enumerate(spans):
         copies[c].wait()
@@ -107,7 +106,7 @@
             sent_refs[2 * c + 1][:, part] = piece
 
 
-def partial_kernel(inputs_ref, cot_ref, partial_ref, rms_ref, held_ref, cot_held, sems):
+def partial_kernel(inputs_ref, cot_ref, gain_ref, spread_ref, partial_ref, rms_ref, held_ref, cot_held, sems):
     tokens, feats = inputs_ref.shape[1:]
     copies = [
         pltpu.make_async_copy(inputs_ref, held_ref, sems.at[0]),
@@ -117,6 +116,7 @@
         copy.start()
     for copy in copies:
         copy.wait()
+    spread_ref[...] = jnp.broadcast_to(gain_ref[...], spread_ref.shape[::-1]).T
     total = jnp.zeros((tokens, lanes), wide)
     for k in range(feats // lanes):
         part = held_ref[0, :, k * lanes : (k + 1) * lanes].astype(wide)
@@ -350,10 +350,9 @@
         count = len(chunks)
         shape = jax.ShapeDtypeStruct
 
-        spread, *own = call(
+        own = call(
             functools.partial(scale_kernel, chunks),
-            [pltpu.VMEM((rows, lanes), wide)]
-            + [pltpu.VMEM((depth, cols), narrow) for _, depth in chunks for _ in range(2)],
+            [pltpu.VMEM((depth, cols), narrow) for _, depth in chunks for _ in range(2)],
             [in_hbm(key_weight), in_hbm(norm_gain)],
             specs=[HBM, HBM],
             scratch=[
@@ -395,15 +394,16 @@
                     got[w][c] = lax.ppermute(sent[w], ("silo", "fsdp"), links[w])
             slots.append(got)
             if s == 0:
-                partial, inv_rms, inputs = call(
+                spread, partial, inv_rms, inputs = call(
                     partial_kernel,
                     [
+                        pltpu.VMEM((rows, lanes), wide),
                         pltpu.VMEM((feats, cols), narrow),
                         pltpu.VMEM((tokens, lanes), wide),
                         pltpu.VMEM(activations.shape, narrow),
                     ],
-                    [in_hbm(activations), in_hbm(key_cot)],
-                    specs=[HBM, HBM],
+                    [in_hbm(activations), in_hbm(key_cot), norm_gain],
+                    specs=[HBM, HBM, VMEM],
                     scratch=[pltpu.VMEM(key_cot.shape, narrow), pltpu.SemaphoreType.DMA((2,))],
                 )
                 outer = outer_steps(pseudo_grad, outer_params, outer_mom, silos, partial)

time: 58.8 us -> 58.8 us (level)
  starting transfers between devices: 28.3 us -> 26.8 us
  waiting for transfers between devices: 16 us -> 16.8 us
  local copies, waits for them, and re-layouts: 0.14 us -> 0.81 us
    ppermute x16, starting transfers between devices: 24.1 us -> 22.8 us  [per_device(): got[w][c] = lax.ppermute(sent[w], ('silo', 'fsdp'), links[w])]
    ppermute x4, waiting for transfers between devices: 1.34 us -> 2.24 us  [swap(): return lax.ppermute(part, 'silo', [(i, i ^ bit) for i in range(silos)])]
    unnamed x16, local copies, waits for them, and re-layouts: 0.14 us -> 0.81 us
where the time goes in v6:
time: 58.8 us; the launch traced here: 58.6 us
  starting transfers between devices  26.8 us (46%)
  waiting for transfers between devices  16.8 us (29%)
  Pallas kernels  13.4 us (23%)
  local copies, waits for them, and re-layouts  0.81 us (1%)
  between operations  0.8 us (1%)
    ppermute x16, starting transfers between devices, per_device(): got[w][c] = lax.ppermute(sent[w], ('silo', 'fsdp'), links[w])  22.8 us
    ppermute x16, waiting for transfers between devices, per_device(): got[w][c] = lax.ppermute(sent[w], ('silo', 'fsdp'), links[w])  14.5 us
    pallas_call x15, Pallas kernels, call(): pl.pallas_call(kernel, out_shape=out_shape, grid=grid, in_specs=specs if...  13.4 us
    ppermute x4, starting transfers between devices, swap(): return lax.ppermute(part, 'silo', [(i, i ^ bit) for i in range(silos)])  4.01 us
    ppermute x4, waiting for transfers between devices, swap(): return lax.ppermute(part, 'silo', [(i, i ^ bit) for i in range(silos)])  2.24 us
  transfers between devices with their start and end apart: 20, of which 7 were waited for; matrix products, arithmetic and copies ran while one was open for 0% of the time, Pallas kernels for 20%

profile of v6, /device:TPU:0, one launch (start us, length us, event | category | flops | bytes accessed | tf_op | source)
XLA Modules:
  0.0 58.6 jit_solution(14297576470257358751)
XLA Ops:
  0.6 0.5 collective-permute-start.6
  1.2 1.2 %shard_map.179 = (bf16[288,512]{1,0:T(8,128)(2,1)S(1)}, bf16[288,512]{1,0:T(8,128)(2,1)S(1)}, bf16[288,512]{1,0:T(8,128)(2,1)S(1)}, bf16[288,512]{1,0:T(8,128)(2,1)S(1)}) custom-call(bf16[1,576,512]{2,1,0:T(8,128)(2,1)} %weight_ref.7, f32[1,576]{1,0:T(1,128)} %refs_3_.1), custom_call_target="tpu_custom_call" | custom-call | tf_op jit(solution)/shard_map/pallas_call | solution.py:72
  2.4 2.7 %collective-permute-start = (bf16[288,512]{1,0:T(8,128)(2,1)S(1)}, bf16[288,512]{1,0:T(8,128)(2,1)S(1)}, u32[]{:S(2)}, u32[]{:S(2)}) collective-permute-start(bf16[288,512]{1,0:T(8,128)(2,1)S(1)} %get-tuple-element.54), channel_id=1, source_target_pairs={{0,1},{1,0},{2,3},{3,2},{4,5},{5,4},{6,7},{7,6},{8,9},{9,8},{10,11... | collective-permute-start | bytes 884744 | tf_op jit(solution)/shard_map/ppermute | solution.py:394
  5.0 0.2 collective-permute-start.1
  5.2 2.9 %collective-permute-start.2 = (bf16[288,512]{1,0:T(8,128)(2,1)S(1)}, bf16[288,512]{1,0:T(8,128)(2,1)S(1)}, u32[]{:S(2)}, u32[]{:S(2)}) collective-permute-start(bf16[288,512]{1,0:T(8,128)(2,1)S(1)} %get-tuple-element.56), channel_id=1, source_target_pairs={{0,1},{1,0},{2,3},{3,2},{4,5},{5,4},{6,7},{7,6},{8,9},{9,8},{10,11... | collective-permute-start | bytes 884744 | tf_op jit(solution)/shard_map/ppermute | solution.py:394
  8.2 0.7 %copy-done.5 = f32[1,576]{1,0:T(1,128)S(1)} copy-done((f32[1,576]{1,0:T(1,128)S(1)}, f32[1,576]{1,0:T(1,128)}, u32[]{:S(2)}) %copy-start.5) | copy-done | bytes 2328
  8.9 2.4 %shard_map.178 = (f32[576,128]{1,0:T(8,128)S(1)}, bf16[2304,512]{1,0:T(8,128)(2,1)S(1)}, f32[256,128]{1,0:T(8,128)S(1)}, bf16[1,256,2304]{2,1,0:T(8,128)(2,1)S(1)}) custom-call(bf16[1,256,2304]{2,1,0:T(8,128)(2,1)} %inputs_ref.1, bf16[1,256,512]{2,1,0:T(8,128)(2,1)} %cot_ref.1, f32[1,576]{1,0:T(1,128)S(1)} %copy-done.5), custom_call_target="tpu_custom_call" | custom-call | tf_op jit(solution)/shard_map/pallas_call | solution.py:72
  11.3 0.0 collective-permute-done.6.other_ref
  11.3 1.5 %shard_map.181.left_ref = bf16[1536,128]{1,0:T(8,128)(2,1)S(1)} custom-call(bf16[1,393216]{1,0:T(2,128)(2,1)} %mine_ref, bf16[1,393216]{1,0:T(2,128)(2,1)S(1)} %collective-permute-done.6.other_ref), custom_call_target="tpu_custom_call" | custom-call | tf_op jit(solution)/shard_map/pallas_call | solution.py:72
  12.8 1.6 %collective-permute-start.11 = (bf16[1536,128]{1,0:T(8,128)(2,1)S(1)}, bf16[1536,128]{1,0:T(8,128)(2,1)S(1)}, u32[]{:S(2)}, u32[]{:S(2)}) collective-permute-start(bf16[1536,128]{1,0:T(8,128)(2,1)S(1)} %shard_map.181.left_ref), channel_id=1, source_target_pairs={{0,8},{4,12},{8,0},{12,4},{16,24},{20,28},{24,16},{28,20},{1,9},{5... | collective-permute-start | bytes 1179656 | tf_op jit(solution)/shard_map/ppermute | solution.py:302
  14.4 0.0 collective-permute-done.even_ref.refs_0_
  14.4 0.1 shard_map.180
  14.4 1.6 %collective-permute-start.4 = (bf16[288,512]{1,0:T(8,128)(2,1)S(1)}, bf16[288,512]{1,0:T(8,128)(2,1)S(1)}, u32[]{:S(2)}, u32[]{:S(2)}) collective-permute-start(bf16[288,512]{1,0:T(8,128)(2,1)S(1)} %get-tuple-element.59), channel_id=1, source_target_pairs={{0,1},{1,0},{2,3},{3,2},{4,5},{5,4},{6,7},{7,6},{8,9},{9,8},{10,11... | collective-permute-start | bytes 884744 | tf_op jit(solution)/shard_map/ppermute | solution.py:394
  16.1 0.0 collective-permute-start.5
  16.1 3.1 %collective-permute-done.2.even_ref.refs_2_ = bf16[288,512]{1,0:T(8,128)(2,1)S(1)} collective-permute-done((bf16[288,512]{1,0:T(8,128)(2,1)S(1)}, bf16[288,512]{1,0:T(8,128)(2,1)S(1)}, u32[]{:S(2)}, u32[]{:S(2)}) %collective-permute-start.2) | collective-permute-done | bytes 294944 | tf_op jit(solution)/shard_map/ppermute | solution.py:394
  19.2 0.1 shard_map.182
  19.3 3.1 %collective-permute-start.7 = (bf16[288,512]{1,0:T(8,128)(2,1)S(1)}, bf16[288,512]{1,0:T(8,128)(2,1)S(1)}, u32[]{:S(2)}, u32[]{:S(2)}) collective-permute-start(bf16[288,512]{1,0:T(8,128)(2,1)S(1)} %get-tuple-element.65), channel_id=1, source_target_pairs={{0,1},{1,0},{2,3},{3,2},{4,5},{5,4},{6,7},{7,6},{8,9},{9,8},{10,11... | collective-permute-start | bytes 884744 | tf_op jit(solution)/shard_map/ppermute | solution.py:394
  22.4 0.0 collective-permute-start.8
  22.4 2.0 %collective-permute-done.11.right_ref = bf16[1536,128]{1,0:T(8,128)(2,1)S(1)} collective-permute-done((bf16[1536,128]{1,0:T(8,128)(2,1)S(1)}, bf16[1536,128]{1,0:T(8,128)(2,1)S(1)}, u32[]{:S(2)}, u32[]{:S(2)}) %collective-permute-start.11) | collective-permute-done | bytes 393248 | tf_op jit(solution)/shard_map/ppermute | solution.py:302
  24.4 0.1 shard_map.184.left_ref
  24.5 1.6 %collective-permute-start.14 = (bf16[1536,128]{1,0:T(8,128)(2,1)S(1)}, bf16[1536,128]{1,0:T(8,128)(2,1)S(1)}, u32[]{:S(2)}, u32[]{:S(2)}) collective-permute-start(bf16[1536,128]{1,0:T(8,128)(2,1)S(1)} %shard_map.184.left_ref), channel_id=1, source_target_pairs={{0,16},{4,20},{8,24},{12,28},{16,0},{20,4},{24,8},{28,12},{1,17},{... | collective-permute-start | bytes 1179656 | tf_op jit(solution)/shard_map/ppermute | solution.py:302
  26.1 0.0 collective-permute-done.4.even_ref.refs_4_
  26.1 0.0 collective-permute-done.5.odd_ref.refs_5_
  26.1 0.1 shard_map.183
  26.2 2.6 %collective-permute-start.9 = (bf16[288,512]{1,0:T(8,128)(2,1)S(1)}, bf16[288,512]{1,0:T(8,128)(2,1)S(1)}, u32[]{:S(2)}, u32[]{:S(2)}) collective-permute-start(bf16[288,512]{1,0:T(8,128)(2,1)S(1)} %get-tuple-element.67), channel_id=1, source_target_pairs={{0,1},{1,0},{2,3},{3,2},{4,5},{5,4},{6,7},{7,6},{8,9},{9,8},{10,11... | collective-permute-start | bytes 884744 | tf_op jit(solution)/shard_map/ppermute | solution.py:394
  28.8 0.0 collective-permute-start.10
  28.8 3.1 %collective-permute-done.7.even_ref.refs_6_ = bf16[288,512]{1,0:T(8,128)(2,1)S(1)} collective-permute-done((bf16[288,512]{1,0:T(8,128)(2,1)S(1)}, bf16[288,512]{1,0:T(8,128)(2,1)S(1)}, u32[]{:S(2)}, u32[]{:S(2)}) %collective-permute-start.7) | collective-permute-done | bytes 294944 | tf_op jit(solution)/shard_map/ppermute | solution.py:394
  31.8 0.1 shard_map.185
  31.9 3.2 %collective-permute-start.12 = (bf16[288,512]{1,0:T(8,128)(2,1)S(1)}, bf16[288,512]{1,0:T(8,128)(2,1)S(1)}, u32[]{:S(2)}, u32[]{:S(2)}) collective-permute-start(bf16[288,512]{1,0:T(8,128)(2,1)S(1)} %get-tuple-element.71), channel_id=1, source_target_pairs={{0,1},{1,0},{2,3},{3,2},{4,5},{5,4},{6,7},{7,6},{8,9},{9,8},{10,11... | collective-permute-start | bytes 884744 | tf_op jit(solution)/shard_map/ppermute | solution.py:394
  35.1 0.0 collective-permute-start.13
  35.1 0.2 collective-permute-done.14.right_ref
  35.3 0.1 shard_map.187.own_ref
  35.4 0.4 collective-permute-start.19
  35.7 2.4 %collective-permute-done.9.refs_8_.even_ref = bf16[288,512]{1,0:T(8,128)(2,1)S(1)} collective-permute-done((bf16[288,512]{1,0:T(8,128)(2,1)S(1)}, bf16[288,512]{1,0:T(8,128)(2,1)S(1)}, u32[]{:S(2)}, u32[]{:S(2)}) %collective-permute-start.9) | collective-permute-done | bytes 294944 | tf_op jit(solution)/shard_map/ppermute | solution.py:394
  38.2 0.1 shard_map.189
  38.2 3.2 %collective-permute-start.17 = (bf16[288,512]{1,0:T(8,128)(2,1)S(1)}, bf16[288,512]{1,0:T(8,128)(2,1)S(1)}, u32[]{:S(2)}, u32[]{:S(2)}) collective-permute-start(bf16[288,512]{1,0:T(8,128)(2,1)S(1)} %get-tuple-element.77), channel_id=1, source_target_pairs={{0,1},{1,0},{2,3},{3,2},{4,5},{5,4},{6,7},{7,6},{8,9},{9,8},{10,11... | collective-permute-start | bytes 884744 | tf_op jit(solution)/shard_map/ppermute | solution.py:394
  41.5 3.0 %collective-permute-done.12.refs_10_.even_ref = bf16[288,512]{1,0:T(8,128)(2,1)S(1)} collective-permute-done((bf16[288,512]{1,0:T(8,128)(2,1)S(1)}, bf16[288,512]{1,0:T(8,128)(2,1)S(1)}, u32[]{:S(2)}, u32[]{:S(2)}) %collective-permute-start.12) | collective-permute-done | bytes 294944 | tf_op jit(solution)/shard_map/ppermute | solution.py:394
  44.5 0.1 shard_map.188
  44.5 3.2 %collective-permute-start.15 = (bf16[288,512]{1,0:T(8,128)(2,1)S(1)}, bf16[288,512]{1,0:T(8,128)(2,1)S(1)}, u32[]{:S(2)}, u32[]{:S(2)}) collective-permute-start(bf16[288,512]{1,0:T(8,128)(2,1)S(1)} %get-tuple-element.75), channel_id=1, source_target_pairs={{0,1},{1,0},{2,3},{3,2},{4,5},{5,4},{6,7},{7,6},{8,9},{9,8},{10,11... | collective-permute-start | bytes 884744 | tf_op jit(solution)/shard_map/ppermute | solution.py:394
  47.8 0.0 collective-permute-start.16
  47.8 1.8 %shard_map.186 = bf16[1,256,512]{2,1,0:T(8,128)(2,1)} custom-call(bf16[1,256,2304]{2,1,0:T(8,128)(2,1)S(1)} %get-tuple-element.51.inputs_ref, f32[256,128]{1,0:T(8,128)S(1)} %get-tuple-element.52.rms_ref, bf16[1,576,512]{2,1,0:T(8,128)(2,1)S(1)} %copy-done, f32[576,128]{1,0:T(8,128)S(1)} %get-tuple-element.53.spread_ref, ...), custom_call_target="tpu_custom_call" | custom-call | tf_op jit(solution)/shard_map/pallas_call | solution.py:72
  49.6 0.1 copy-done.4
  49.7 2.8 %shard_map.190 = (f32[2,1536,128]{2,1,0:T(8,128)}, f32[2,1536,128]{2,1,0:T(8,128)}) custom-call(bf16[1536,128]{1,0:T(8,128)(2,1)S(1)} %shard_map.187.own_ref, bf16[1536,128]{1,0:T(8,128)(2,1)S(1)} %collective-permute-done.19.other_ref, f32[2,1536,128]{2,1,0:T(8,128)S(1)} %bitcast.4, f32[2,1536,128]{2,1,0:T(8,128)S(1)} %bitcast.5), custom_call_target="tpu_custom_call" | custom-call | tf_op jit(solution)/shard_map/pallas_call | solution.py:72
  52.5 0.0 copy-start.6
  52.5 0.0 copy-start.7
  52.6 1.5 %shard_map.191 = (f32[288,128]{1,0:T(8,128)S(1)}, bf16[1,576,512]{2,1,0:T(8,128)(2,1)}, f32[1,576,512]{2,1,0:T(8,128)}, f32[1,576,512]{2,1,0:T(8,128)}) custom-call(f32[576,128]{1,0:T(8,128)S(1)} %get-tuple-element.53.spread_ref, bf16[1,576,512]{2,1,0:T(8,128)(2,1)S(1)} %copy-done, f32[1,576,512]{2,1,0:T(8,128)S(1)} %copy-done.1, ...), custom_call_target="tpu_custom_call" | custom-call | tf_op jit(solution)/shard_map/pallas_call | solution.py:72
  54.0 2.9 %collective-permute-done.15.refs_0_ = bf16[288,512]{1,0:T(8,128)(2,1)S(1)} collective-permute-done((bf16[288,512]{1,0:T(8,128)(2,1)S(1)}, bf16[288,512]{1,0:T(8,128)(2,1)S(1)}, u32[]{:S(2)}, u32[]{:S(2)}) %collective-permute-start.15) | collective-permute-done | bytes 294944 | tf_op jit(solution)/shard_map/ppermute | solution.py:394
  56.9 1.7 %shard_map.192 = (bf16[1,576,512]{2,1,0:T(8,128)(2,1)}, f32[1,576,512]{2,1,0:T(8,128)}, f32[1,576,512]{2,1,0:T(8,128)}, f32[1,576]{1,0:T(1,128)}, f32[1,576]{1,0:T(1,128)}, /*index=5*/f32[1,576]{1,0:T(1,128)}) custom-call(f32[576,128]{1,0:T(8,128)S(1)} %get-tuple-element.53.spread_ref, ...), custom_call_target="tpu_custom_call", output_to_operand_aliasing={{0}: (11, {}), {1}: (12, {}), {2}: (13, {})} | custom-call | tf_op jit(solution)/shard_map/pallas_call | solution.py:72
  (23 shorter events, 0.1 us)
Async XLA Ops:
  0.6 10.6 %collective-permute-start.6 = (bf16[1,393216]{1,0:T(2,128)(2,1)}, bf16[1,393216]{1,0:T(2,128)(2,1)S(1)}, u32[]{:S(2)}, u32[]{:S(2)}) collective-permute-start(bf16[1,393216]{1,0:T(2,128)(2,1)} %mine_ref), channel_id=1, source_target_pairs={{0,4},{4,0},{8,12},{12,8},{16,20},{20,16},{24,28},{28,24},{1,5},{5... | collective-permute-start | bytes 2359304 | tf_op jit(solution)/shard_map/ppermute | solution.py:302
  2.4 12.0 %collective-permute-start = (bf16[288,512]{1,0:T(8,128)(2,1)S(1)}, bf16[288,512]{1,0:T(8,128)(2,1)S(1)}, u32[]{:S(2)}, u32[]{:S(2)}) collective-permute-start(bf16[288,512]{1,0:T(8,128)(2,1)S(1)} %get-tuple-element.54), channel_id=1, source_target_pairs={{0,1},{1,0},{2,3},{3,2},{4,5},{5,4},{6,7},{7,6},{8,9},{9,8},{10,11... | collective-permute-start | bytes 884744 | tf_op jit(solution)/shard_map/ppermute | solution.py:394
  5.0 9.4 %collective-permute-start.1 = (bf16[288,512]{1,0:T(8,128)(2,1)S(1)}, bf16[288,512]{1,0:T(8,128)(2,1)S(1)}, u32[]{:S(2)}, u32[]{:S(2)}) collective-permute-start(bf16[288,512]{1,0:T(8,128)(2,1)S(1)} %get-tuple-element.55), channel_id=1, source_target_pairs={{0,4},{1,2},{2,1},{3,7},{4,0},{5,6},{6,5},{7,3},{8,12},{9,10},{10,... | collective-permute-start | bytes 884744 | tf_op jit(solution)/shard_map/ppermute | solution.py:394
  5.2 14.0 %collective-permute-start.2 = (bf16[288,512]{1,0:T(8,128)(2,1)S(1)}, bf16[288,512]{1,0:T(8,128)(2,1)S(1)}, u32[]{:S(2)}, u32[]{:S(2)}) collective-permute-start(bf16[288,512]{1,0:T(8,128)(2,1)S(1)} %get-tuple-element.56), channel_id=1, source_target_pairs={{0,1},{1,0},{2,3},{3,2},{4,5},{5,4},{6,7},{7,6},{8,9},{9,8},{10,11... | collective-permute-start | bytes 884744 | tf_op jit(solution)/shard_map/ppermute | solution.py:394
  8.2 11.0 %collective-permute-start.3 = (bf16[288,512]{1,0:T(8,128)(2,1)S(1)}, bf16[288,512]{1,0:T(8,128)(2,1)S(1)}, u32[]{:S(2)}, u32[]{:S(2)}) collective-permute-start(bf16[288,512]{1,0:T(8,128)(2,1)S(1)} %get-tuple-element.57), channel_id=1, source_target_pairs={{0,4},{1,2},{2,1},{3,7},{4,0},{5,6},{6,5},{7,3},{8,12},{9,10},{10,... | collective-permute-start | bytes 884744 | tf_op jit(solution)/shard_map/ppermute | solution.py:394
  8.2 0.7 %copy-start.5 = (f32[1,576]{1,0:T(1,128)S(1)}, f32[1,576]{1,0:T(1,128)}, u32[]{:S(2)}) copy-start(f32[1,576]{1,0:T(1,128)} %refs_3_.1) | copy-start | bytes 6916
  12.8 11.6 %collective-permute-start.11 = (bf16[1536,128]{1,0:T(8,128)(2,1)S(1)}, bf16[1536,128]{1,0:T(8,128)(2,1)S(1)}, u32[]{:S(2)}, u32[]{:S(2)}) collective-permute-start(bf16[1536,128]{1,0:T(8,128)(2,1)S(1)} %shard_map.181.left_ref), channel_id=1, source_target_pairs={{0,8},{4,12},{8,0},{12,4},{16,24},{20,28},{24,16},{28,20},{1,9},{5... | collective-permute-start | bytes 1179656 | tf_op jit(solution)/shard_map/ppermute | solution.py:302
  14.4 11.6 %collective-permute-start.4 = (bf16[288,512]{1,0:T(8,128)(2,1)S(1)}, bf16[288,512]{1,0:T(8,128)(2,1)S(1)}, u32[]{:S(2)}, u32[]{:S(2)}) collective-permute-start(bf16[288,512]{1,0:T(8,128)(2,1)S(1)} %get-tuple-element.59), channel_id=1, source_target_pairs={{0,1},{1,0},{2,3},{3,2},{4,5},{5,4},{6,7},{7,6},{8,9},{9,8},{10,11... | collective-permute-start | bytes 884744 | tf_op jit(solution)/shard_map/ppermute | solution.py:394
  16.1 10.0 %collective-permute-start.5 = (bf16[288,512]{1,0:T(8,128)(2,1)S(1)}, bf16[288,512]{1,0:T(8,128)(2,1)S(1)}, u32[]{:S(2)}, u32[]{:S(2)}) collective-permute-start(bf16[288,512]{1,0:T(8,128)(2,1)S(1)} %get-tuple-element.60), channel_id=1, source_target_pairs={{0,4},{1,2},{2,1},{3,7},{4,0},{5,6},{6,5},{7,3},{8,12},{9,10},{10,... | collective-permute-start | bytes 884744 | tf_op jit(solution)/shard_map/ppermute | solution.py:394
  19.3 12.6 %collective-permute-start.7 = (bf16[288,512]{1,0:T(8,128)(2,1)S(1)}, bf16[288,512]{1,0:T(8,128)(2,1)S(1)}, u32[]{:S(2)}, u32[]{:S(2)}) collective-permute-start(bf16[288,512]{1,0:T(8,128)(2,1)S(1)} %get-tuple-element.65), channel_id=1, source_target_pairs={{0,1},{1,0},{2,3},{3,2},{4,5},{5,4},{6,7},{7,6},{8,9},{9,8},{10,11... | collective-permute-start | bytes 884744 | tf_op jit(solution)/shard_map/ppermute | solution.py:394
  22.4 9.4 %collective-permute-start.8 = (bf16[288,512]{1,0:T(8,128)(2,1)S(1)}, bf16[288,512]{1,0:T(8,128)(2,1)S(1)}, u32[]{:S(2)}, u32[]{:S(2)}) collective-permute-start(bf16[288,512]{1,0:T(8,128)(2,1)S(1)} %get-tuple-element.66), channel_id=1, source_target_pairs={{0,4},{1,2},{2,1},{3,7},{4,0},{5,6},{6,5},{7,3},{8,12},{9,10},{10,... | collective-permute-start | bytes 884744 | tf_op jit(solution)/shard_map/ppermute | solution.py:394
  24.5 10.8 %collective-permute-start.14 = (bf16[1536,128]{1,0:T(8,128)(2,1)S(1)}, bf16[1536,128]{1,0:T(8,128)(2,1)S(1)}, u32[]{:S(2)}, u32[]{:S(2)}) collective-permute-start(bf16[1536,128]{1,0:T(8,128)(2,1)S(1)} %shard_map.184.left_ref), channel_id=1, source_target_pairs={{0,16},{4,20},{8,24},{12,28},{16,0},{20,4},{24,8},{28,12},{1,17},{... | collective-permute-start | bytes 1179656 | tf_op jit(solution)/shard_map/ppermute | solution.py:302
  26.2 12.0 %collective-permute-start.9 = (bf16[288,512]{1,0:T(8,128)(2,1)S(1)}, bf16[288,512]{1,0:T(8,128)(2,1)S(1)}, u32[]{:S(2)}, u32[]{:S(2)}) collective-permute-start(bf16[288,512]{1,0:T(8,128)(2,1)S(1)} %get-tuple-element.67), channel_id=1, source_target_pairs={{0,1},{1,0},{2,3},{3,2},{4,5},{5,4},{6,7},{7,6},{8,9},{9,8},{10,11... | collective-permute-start | bytes 884744 | tf_op jit(solution)/shard_map/ppermute | solution.py:394
  28.8 9.4 %collective-permute-start.10 = (bf16[288,512]{1,0:T(8,128)(2,1)S(1)}, bf16[288,512]{1,0:T(8,128)(2,1)S(1)}, u32[]{:S(2)}, u32[]{:S(2)}) collective-permute-start(bf16[288,512]{1,0:T(8,128)(2,1)S(1)} %get-tuple-element.68), channel_id=1, source_target_pairs={{0,4},{1,2},{2,1},{3,7},{4,0},{5,6},{6,5},{7,3},{8,12},{9,10},{10,... | collective-permute-start | bytes 884744 | tf_op jit(solution)/shard_map/ppermute | solution.py:394
  31.9 12.6 %collective-permute-start.12 = (bf16[288,512]{1,0:T(8,128)(2,1)S(1)}, bf16[288,512]{1,0:T(8,128)(2,1)S(1)}, u32[]{:S(2)}, u32[]{:S(2)}) collective-permute-start(bf16[288,512]{1,0:T(8,128)(2,1)S(1)} %get-tuple-element.71), channel_id=1, source_target_pairs={{0,1},{1,0},{2,3},{3,2},{4,5},{5,4},{6,7},{7,6},{8,9},{9,8},{10,11... | collective-permute-start | bytes 884744 | tf_op jit(solution)/shard_map/ppermute | solution.py:394
  35.1 9.4 %collective-permute-start.13 = (bf16[288,512]{1,0:T(8,128)(2,1)S(1)}, bf16[288,512]{1,0:T(8,128)(2,1)S(1)}, u32[]{:S(2)}, u32[]{:S(2)}) collective-permute-start(bf16[288,512]{1,0:T(8,128)(2,1)S(1)} %get-tuple-element.72), channel_id=1, source_target_pairs={{0,4},{1,2},{2,1},{3,7},{4,0},{5,6},{6,5},{7,3},{8,12},{9,10},{10,... | collective-permute-start | bytes 884744 | tf_op jit(solution)/shard_map/ppermute | solution.py:394
  35.4 14.2 %collective-permute-start.19 = (bf16[1536,128]{1,0:T(8,128)(2,1)S(1)}, bf16[1536,128]{1,0:T(8,128)(2,1)S(1)}, u32[]{:S(2)}, u32[]{:S(2)}) collective-permute-start(bf16[1536,128]{1,0:T(8,128)(2,1)S(1)} %shard_map.187.own_ref), channel_id=1, source_target_pairs={{0,4},{4,0},{8,12},{12,8},{16,20},{20,16},{24,28},{28,24},{1,5},{5... | collective-permute-start | bytes 1179656 | tf_op jit(solution)/shard_map/ppermute | solution.py:302
  38.2 14.3 %collective-permute-start.17 = (bf16[288,512]{1,0:T(8,128)(2,1)S(1)}, bf16[288,512]{1,0:T(8,128)(2,1)S(1)}, u32[]{:S(2)}, u32[]{:S(2)}) collective-permute-start(bf16[288,512]{1,0:T(8,128)(2,1)S(1)} %get-tuple-element.77), channel_id=1, source_target_pairs={{0,1},{1,0},{2,3},{3,2},{4,5},{5,4},{6,7},{7,6},{8,9},{9,8},{10,11... | collective-permute-start | bytes 884744 | tf_op jit(solution)/shard_map/ppermute | solution.py:394
  41.4 6.3 %copy-start = (bf16[1,576,512]{2,1,0:T(8,128)(2,1)S(1)}, bf16[1,576,512]{2,1,0:T(8,128)(2,1)}, u32[]{:S(2)}) copy-start(bf16[1,576,512]{2,1,0:T(8,128)(2,1)} %weight_ref.7) | copy-start | bytes 1769476
  41.5 11.1 %collective-permute-start.18 = (bf16[288,512]{1,0:T(8,128)(2,1)S(1)}, bf16[288,512]{1,0:T(8,128)(2,1)S(1)}, u32[]{:S(2)}, u32[]{:S(2)}) collective-permute-start(bf16[288,512]{1,0:T(8,128)(2,1)S(1)} %get-tuple-element.78), channel_id=1, source_target_pairs={{0,4},{1,2},{2,1},{3,7},{4,0},{5,6},{6,5},{7,3},{8,12},{9,10},{10,... | collective-permute-start | bytes 884744 | tf_op jit(solution)/shard_map/ppermute | solution.py:394
  44.5 12.4 %collective-permute-start.15 = (bf16[288,512]{1,0:T(8,128)(2,1)S(1)}, bf16[288,512]{1,0:T(8,128)(2,1)S(1)}, u32[]{:S(2)}, u32[]{:S(2)}) collective-permute-start(bf16[288,512]{1,0:T(8,128)(2,1)S(1)} %get-tuple-element.75), channel_id=1, source_target_pairs={{0,1},{1,0},{2,3},{3,2},{4,5},{5,4},{6,7},{7,6},{8,9},{9,8},{10,11... | collective-permute-start | bytes 884744 | tf_op jit(solution)/shard_map/ppermute | solution.py:394
  47.8 9.1 %collective-permute-start.16 = (bf16[288,512]{1,0:T(8,128)(2,1)S(1)}, bf16[288,512]{1,0:T(8,128)(2,1)S(1)}, u32[]{:S(2)}, u32[]{:S(2)}) collective-permute-start(bf16[288,512]{1,0:T(8,128)(2,1)S(1)} %get-tuple-element.76), channel_id=1, source_target_pairs={{0,4},{1,2},{2,1},{3,7},{4,0},{5,6},{6,5},{7,3},{8,12},{9,10},{10,... | collective-permute-start | bytes 884744 | tf_op jit(solution)/shard_map/ppermute | solution.py:394
  47.8 1.8 %copy-start.3 = (f32[393216]{0:T(1024)S(1)}, f32[393216]{0:T(1024)}, u32[]{:S(2)}) copy-start(f32[393216]{0:T(1024)} %param.20) | copy-start | bytes 4718596
  47.8 1.9 %copy-start.4 = (f32[393216]{0:T(1024)S(1)}, f32[393216]{0:T(1024)}, u32[]{:S(2)}) copy-start(f32[393216]{0:T(1024)} %param.21) | copy-start | bytes 4718596
  49.7 2.9 %copy-start.1 = (f32[1,576,512]{2,1,0:T(8,128)S(1)}, f32[1,576,512]{2,1,0:T(8,128)}, u32[]{:S(2)}) copy-start(f32[1,576,512]{2,1,0:T(8,128)} %first_ref.3) | copy-start | bytes 3538948
  49.7 2.9 %copy-start.2 = (f32[1,576,512]{2,1,0:T(8,128)S(1)}, f32[1,576,512]{2,1,0:T(8,128)}, u32[]{:S(2)}) copy-start(f32[1,576,512]{2,1,0:T(8,128)} %second_ref.3) | copy-start | bytes 3538948
  52.5 4.4 %copy-start.6 = (f32[1,576]{1,0:T(1,128)S(1)}, f32[1,576]{1,0:T(1,128)}, u32[]{:S(2)}) copy-start(f32[1,576]{1,0:T(1,128)} %refs_4_.1) | copy-start | bytes 6916
  52.5 4.4 %copy-start.7 = (f32[1,576]{1,0:T(1,128)S(1)}, f32[1,576]{1,0:T(1,128)}, u32[]{:S(2)}) copy-start(f32[1,576]{1,0:T(1,128)} %refs_5_.1) | copy-start | bytes 6916
